TPU v7x, 128 devices: a whole 4x4x4 slice. The times are simulated.
128 devices in a mesh: row: 8 (over y_hi, z), col: 16 (over y_lo, x, core).
Axes of the slice: x: 4, y: 4 (y_hi: 2, y_lo: 2; y = y_hi * 2 + y_lo), z: 4, core: 2. Of those that a mesh axis runs over, the one named last changes fastest.
Arguments:
- vectors: bfloat16 [65536, 256], P(('row', 'col')), may hold values from -6 to 6
- blocks: bfloat16 [8, 16, 256, 128, 128], P('row', 'col'), may hold values from -0.046875 to 0.046875
- block_rows: int32 [8, 16, 256], P('row', 'col'), may hold values from 0 to 63
- block_cols: int32 [8, 16, 256], P('row', 'col'), may hold values from 0 to 31
- block_count: int32 [8, 16], P('row', 'col'), may hold values from 32 to 256, as said below
- lower_edge: float32 [1], replicated, may hold values from -0.6 to -0.3
- upper_edge: float32 [1], replicated, may hold values from 1 to 2
Outputs:
- filtered: float32 [65536, 256], P(('row', 'col'))
Inputs may be any that keep to these rules, and one draw needn't show every extreme that they name: `block_count`: some device has all 256 slots live.
All inputs are finite; a program needn't handle non-finite values.
Results may differ from a plain program's by a relative error of at most 0.008.
Values may be sent and summed in bfloat16 or wider, within the bound.
No kernel may reach another device: no remote copies, remote signals or barrier semaphores. Data moves between devices by JAX's collectives and lax.ppermute only.
A program may use at most 192 MiB of HBM per device.

v0:
```python
import functools
import itertools

import jax
import jax.numpy as jnp
from jax import lax
from jax.experimental import pallas as pl
from jax.experimental.pallas import tpu as pltpu
from jax.sharding import PartitionSpec as P

DEGREE = 2
UNROLL = 16
GROUP = 64
BOTH = ("row", "col")


def linear(y_hi, z, y_lo, x, core):
    return (y_hi * 4 + z) * 16 + y_lo * 8 + x * 2 + core


def pairs(move):
    every = itertools.product(range(2), range(4), range(2), range(4), range(2))
    return [(linear(*d), linear(*move(*d))) for d in every]


def ring_first(core):
    return 3 if core else 1


def ring_second(core):
    return 1 if core else 3


TO_CORE = pairs(lambda h, z, l, x, k: (h, z, l, x, k ^ 1))
ROW_MOVES = (
    pairs(lambda h, z, l, x, k: (h, z, l ^ 1, x, k)),
    pairs(lambda h, z, l, x, k: (h, z, l, x ^ ring_first(k), k)),
    pairs(lambda h, z, l, x, k: (h, z, l, x ^ ring_second(k), k)),
)
COL_MOVES = (
    pairs(lambda h, z, l, x, k: (h ^ 1, z, l, x, k)),
    pairs(lambda h, z, l, x, k: (h, z ^ ring_first(k), l, x, k)),
    pairs(lambda h, z, l, x, k: (h, z ^ ring_second(k), l, x, k)),
)


def move(value, table):
    return lax.ppermute(value, BOTH, table)


def slot_kernel(row_tile_ref, col_tile_ref, count_ref, own_ref, mate_ref, *rest):
    row_parts, col_parts, outs = rest[:4], rest[4:8], rest[8:16]
    blocks, row_side, col_side, row_acc, col_acc, cast, side_sems, block_sems, out_sems = rest[16:]
    slots = own_ref.shape[0]
    groups = slots // GROUP
    tiles = row_side.shape[0]
    quarter = tiles // 4

    def live_of(group):
        count = count_ref[group // groups]
        return jnp.clip(count - (group % groups) * GROUP, 0, GROUP)

    def block_copy(group):
        source = own_ref if group < groups else mate_ref
        return pltpu.make_async_copy(
            source.at[pl.ds((group % groups) * GROUP, GROUP)],
            blocks.at[pl.ds(group * GROUP, GROUP)],
            block_sems.at[group],
        )

    def start_if_live(group):
        @pl.when(live_of(group) > 0)
        def _():
            block_copy(group).start()

    copies = []
    for side, parts in ((col_side, col_parts), (row_side, row_parts)):
        for i, part in enumerate(parts):
            copies.append(
                pltpu.make_async_copy(
                    part, side.at[pl.ds(i * quarter, quarter)], side_sems.at[len(copies)]
                )
            )
    start_if_live(0)
    for c in copies:
        c.start()
    row_acc[...] = jnp.zeros_like(row_acc)
    for group in range(1, 2 * groups):
        start_if_live(group)
    col_acc[...] = jnp.zeros_like(col_acc)
    for c in copies:
        c.wait()

    def one_group(group, carry):
        live = live_of(group)

        @pl.when(live > 0)
        def _():
            pltpu.make_async_copy(
                own_ref.at[pl.ds(0, GROUP)],
                blocks.at[pl.ds(group * GROUP, GROUP)],
                block_sems.at[group],
            ).wait()

        def body(i, inner):
            for u in range(UNROLL):
                k = group * GROUP + i * UNROLL + u
                row = row_tile_ref[k]
                col = col_tile_ref[k]
                block = blocks[k]
                row_acc[row] += jnp.dot(
                    block, col_side[col & (tiles - 1)], preferred_element_type=jnp.float32
                )
                col_acc[col] += lax.dot_general(
                    block, row_side[row & (tiles - 1)], (((0,), (0,)), ((), ())),
                    preferred_element_type=jnp.float32,
                )
            return inner

        return lax.fori_loop(0, (live + UNROLL - 1) // UNROLL, body, carry)

    lax.fori_loop(0, 2 * groups, one_group, 0)

    finals = []

    def hand_out(source, out):
        copy = pltpu.make_async_copy(source, out, out_sems.at[len(finals)])
        copy.start()
        finals.append(copy)

    for acc, base in ((row_acc, 0), (col_acc, 4)):
        for i, at in enumerate((2, 0)):
            hand_out(acc.at[pl.ds(at * quarter, quarter)], outs[base + 2 + i])
    for j, (acc, base) in enumerate(((row_acc, 0), (col_acc, 4))):
        for i, at in enumerate((3, 1)):
            cast[2 * j + i] = acc[at * quarter : (at + 1) * quarter].astype(cast.dtype)
            hand_out(cast.at[2 * j + i], outs[base + i])
    for c in finals:
        c.wait()


def slot_products(row_tiles, col_tiles, counts, own, mate, row_parts, col_parts):
    slots, order, _ = own.shape
    quarter, _, width = row_parts[0].shape
    tiles = 4 * quarter
    anywhere = pl.BlockSpec(memory_space=pl.ANY)
    in_smem = pl.BlockSpec(memory_space=pltpu.SMEM)
    sent = jax.ShapeDtypeStruct((quarter, order, width), jnp.bfloat16)
    kept = jax.ShapeDtypeStruct((quarter, order, width), jnp.float32)
    return pl.pallas_call(
        slot_kernel,
        in_specs=[in_smem] * 3 + [anywhere] * 10,
        out_specs=[anywhere] * 8,
        out_shape=[sent, sent, kept, kept] * 2,
        scratch_shapes=[
            pltpu.VMEM((2 * slots, order, order), jnp.bfloat16),
            pltpu.VMEM((tiles, order, width), jnp.bfloat16),
            pltpu.VMEM((tiles, order, width), jnp.bfloat16),
            pltpu.VMEM((tiles + 1, order, width), jnp.float32),
            pltpu.VMEM((tiles + 1, order, width), jnp.float32),
            pltpu.VMEM((4, quarter, order, width), jnp.bfloat16),
            pltpu.SemaphoreType.DMA((8,)),
            pltpu.SemaphoreType.DMA((2 * slots // GROUP,)),
            pltpu.SemaphoreType.DMA((8,)),
        ],
        compiler_params=pltpu.CompilerParams(vmem_limit_bytes=36 * 1024 * 1024),
        cost_estimate=pl.CostEstimate(
            flops=8 * slots * order * order * width, bytes_accessed=26 * 1024 * 1024, transcendentals=0
        ),
    )(row_tiles, col_tiles, counts, own, mate, *row_parts, *col_parts)


def gather(operand, moves):
    across, first, second = moves
    parts = []
    for value in (operand, move(operand, across)):
        near = jnp.concatenate([value, move(value, first)])
        parts += [near, move(near, second)]
    return parts


def scatter_sum(sent_first, sent_next, kept_first, kept_next, moves):
    across, first, second = moves
    half = kept_first.shape[0] // 2
    sums = []
    for keep, send in ((kept_first, sent_first), (kept_next, sent_next)):
        near = keep + move(send, second).astype(jnp.float32)
        sums.append(
            near[:half] + move(near[half:].astype(jnp.bfloat16), first).astype(jnp.float32)
        )
    return sums[1] + move(sums[0].astype(jnp.bfloat16), across).astype(jnp.float32)


def place_of(near_bit, ring, core):
    high, low = ring >> 1, ring & 1
    mixed = high ^ low
    third = jnp.where(core == 0, high, mixed)
    second = jnp.where(core == 0, mixed, high)
    return near_bit * 4 + third * 2 + second


def per_device(vectors, blocks, block_rows, block_cols, block_count, lower_edge, upper_edge):
    center = (upper_edge[0] + lower_edge[0]) * 0.5
    half_width = (upper_edge[0] - lower_edge[0]) * 0.5
    own = blocks[0, 0]
    slots, order, _ = own.shape
    seg, width = vectors.shape
    half = width // 2
    row_at, col_at = lax.axis_index("row"), lax.axis_index("col")
    core = col_at & 1

    mine = jnp.where(core == 0, vectors[:, :half], vectors[:, half:])
    other = move(jnp.where(core == 0, vectors[:, half:], vectors[:, :half]), TO_CORE)
    table = jnp.concatenate(
        [block_rows[0, 0], block_cols[0, 0], jnp.broadcast_to(block_count[0, 0], (order,))]
    )
    other, table, own = lax.optimization_barrier((other, table, own))
    mate_table = move(table, TO_CORE)
    mate = move(own, TO_CORE)
    operand = jnp.where(
        core == 0, jnp.concatenate([mine, other]), jnp.concatenate([other, mine])
    )

    def tiles_of(table, source_core):
        rows, cols, count = table[:slots], table[slots : 2 * slots], table[2 * slots]
        live = jnp.arange(slots) < count
        place = place_of((rows >> 5) ^ (col_at >> 3), ((rows >> 3) & 3) ^ ((col_at >> 1) & 3), core)
        row_tiles = place * 8 + (rows & 7)
        place = place_of((cols >> 4) ^ (row_at >> 2), ((cols >> 2) & 3) ^ (row_at & 3), core)
        col_tiles = place * 8 + source_core * 4 + (cols & 3)
        return jnp.where(live, row_tiles, 64), jnp.where(live, col_tiles, 64), count

    own_rows, own_cols, own_count = tiles_of(table, core)
    mate_rows, mate_cols, mate_count = tiles_of(mate_table, 1 - core)
    row_tiles = jnp.concatenate([own_rows, mate_rows])
    col_tiles = jnp.concatenate([own_cols, mate_cols])
    counts = jnp.stack([own_count, mate_count])

    current = operand.astype(jnp.float32)
    previous = jnp.zeros_like(current)
    for degree in range(DEGREE):
        tiled = current.astype(jnp.bfloat16).reshape(-1, order, half)
        col_parts = gather(tiled, COL_MOVES)
        row_parts = gather(tiled, ROW_MOVES)
        found = slot_products(row_tiles, col_tiles, counts, own, mate, row_parts, col_parts)
        applied = scatter_sum(*found[:4], ROW_MOVES) + scatter_sum(*found[4:], COL_MOVES)
        shifted = applied.reshape(2 * seg, half) - center * current
        if degree == 0:
            following = shifted / half_width
        else:
            following = 2.0 * shifted / half_width - previous
        previous, current = (current, following)

    mine = jnp.where(core == 0, current[:seg], current[seg:])
    other = move(jnp.where(core == 0, current[seg:], current[:seg]), TO_CORE)
    return jnp.where(
        core == 0, jnp.concatenate([mine, other], 1), jnp.concatenate([other, mine], 1)
    )


def solution(mesh):
    return jax.shard_map(
        per_device,
        mesh=mesh,
        in_specs=(
            P(("row", "col"), None),
            P("row", "col", None, None, None),
            P("row", "col", None),
            P("row", "col", None),
            P("row", "col"),
            P(),
            P(),
        ),
        out_specs=P(("row", "col"), None),
        check_vma=False,
    )
```

profile of v0, /device:TPU:1, one launch (start us, length us, event | category | flops | bytes accessed | tf_op | source)
XLA Modules:
  0.0 180.5 jit_solution(13282527187935693547)
XLA Ops:
  0.0 1.0 broadcast_select_fusion
  1.0 1.5 collective-permute-start
  3.2 0.7 pad_add_fusion
  4.0 3.1 %collective-permute-start.10 = (bf16[8,128,128]{2,1,0:T(8,128)(2,1)S(1)}, bf16[8,128,128]{2,1,0:T(8,128)(2,1)S(1)}, u32[]{:S(2)}, u32[]{:S(2)}) collective-permute-start(bf16[8,128,128]{2,1,0:T(8,128)(2,1)S(1)} %bitcast.17), channel_id=1, source_target_pairs={{0,64},{1,65},{2,66},{3,67},{4,68},{5,69},{6,70},{7,71},{8,72},{9,... | collective-permute-start | bytes 786440 | tf_op jit(solution)/shard_map/ppermute | solution.py:48
  7.1 3.8 %collective-permute-start.8 = (bf16[8,128,128]{2,1,0:T(8,128)(2,1)S(1)}, bf16[8,128,128]{2,1,0:T(8,128)(2,1)S(1)}, u32[]{:S(2)}, u32[]{:S(2)}) collective-permute-start(bf16[8,128,128]{2,1,0:T(8,128)(2,1)S(1)} %bitcast.18), channel_id=1, source_target_pairs={{0,16},{1,49},{2,18},{3,51},{4,20},{5,53},{6,22},{7,55},{8,24},{9,... | collective-permute-start | bytes 786440 | tf_op jit(solution)/shard_map/ppermute | solution.py:48
  10.9 2.5 %collective-permute-start.3 = (bf16[8,128,128]{2,1,0:T(8,128)(2,1)S(1)}, bf16[8,128,128]{2,1,0:T(8,128)(2,1)S(1)}, u32[]{:S(2)}, u32[]{:S(2)}) collective-permute-start(bf16[8,128,128]{2,1,0:T(8,128)(2,1)S(1)} %bitcast.19), channel_id=1, source_target_pairs={{0,2},{1,7},{2,0},{3,5},{4,6},{5,3},{6,4},{7,1},{8,10},{9,15},{10,... | collective-permute-start | bytes 786440 | tf_op jit(solution)/shard_map/ppermute | solution.py:48
  13.4 0.4 collective-permute-start.5
  13.8 0.6 slice.92
  14.6 4.5 %collective-permute-start.11 = (bf16[8,128,128]{2,1,0:T(8,128)(2,1)S(1)}, bf16[8,128,128]{2,1,0:T(8,128)(2,1)S(1)}, u32[]{:S(2)}, u32[]{:S(2)}) collective-permute-start(bf16[8,128,128]{2,1,0:T(8,128)(2,1)S(1)} %collective-permute-done.10), channel_id=1, source_target_pairs={{0,16},{1,49},{2,18},{3,51},{4,20},{5,53},{6,22},{7,55},{8,24},{9,... | collective-permute-start | bytes 786440 | tf_op jit(solution)/shard_map/ppermute | solution.py:48
  19.3 0.8 collective-permute-done.5
  20.1 1.9 %collective-permute-start.6 = (bf16[8,128,128]{2,1,0:T(8,128)(2,1)S(1)}, bf16[8,128,128]{2,1,0:T(8,128)(2,1)S(1)}, u32[]{:S(2)}, u32[]{:S(2)}) collective-permute-start(bf16[8,128,128]{2,1,0:T(8,128)(2,1)S(1)} %collective-permute-done.5), channel_id=1, source_target_pairs={{0,2},{1,7},{2,0},{3,5},{4,6},{5,3},{6,4},{7,1},{8,10},{9,15},{10,... | collective-permute-start | bytes 786440 | tf_op jit(solution)/shard_map/ppermute | solution.py:48
  22.0 3.3 %collective-permute-done.11 = bf16[8,128,128]{2,1,0:T(8,128)(2,1)S(1)} collective-permute-done((bf16[8,128,128]{2,1,0:T(8,128)(2,1)S(1)}, bf16[8,128,128]{2,1,0:T(8,128)(2,1)S(1)}, u32[]{:S(2)}, u32[]{:S(2)}) %collective-permute-start.11) | collective-permute-done | bytes 262176 | tf_op jit(solution)/shard_map/ppermute | solution.py:48
  25.3 0.6 collective-permute-start.4
  25.9 1.7 collective-permute-done.6
  27.8 0.7 add_select_fusion.1
  28.6 0.5 slice.94
  29.1 1.4 pad_add_fusion.3.count_ref
  30.5 0.7 add_select_fusion
  31.2 2.4 %collective-permute-done.4.rest_1_ = bf16[16,128,128]{2,1,0:T(8,128)(2,1)S(1)} collective-permute-done((bf16[16,128,128]{2,1,0:T(8,128)(2,1)S(1)}, bf16[16,128,128]{2,1,0:T(8,128)(2,1)S(1)}, u32[]{:S(2)}, u32[]{:S(2)}) %collective-permute-start.4) | collective-permute-done | bytes 524320 | tf_op jit(solution)/shard_map/ppermute | solution.py:48
  33.6 2.3 %collective-permute-done.12.rest_7_ = bf16[16,128,128]{2,1,0:T(8,128)(2,1)S(1)} collective-permute-done((bf16[16,128,128]{2,1,0:T(8,128)(2,1)S(1)}, bf16[16,128,128]{2,1,0:T(8,128)(2,1)S(1)}, u32[]{:S(2)}, u32[]{:S(2)}) %collective-permute-start.12) | collective-permute-done | bytes 524320 | tf_op jit(solution)/shard_map/ppermute | solution.py:48
  35.9 3.3 %collective-permute-done.7.rest_3_ = bf16[16,128,128]{2,1,0:T(8,128)(2,1)S(1)} collective-permute-done((bf16[16,128,128]{2,1,0:T(8,128)(2,1)S(1)}, bf16[16,128,128]{2,1,0:T(8,128)(2,1)S(1)}, u32[]{:S(2)}, u32[]{:S(2)}) %collective-permute-start.7) | collective-permute-done | bytes 524320 | tf_op jit(solution)/shard_map/ppermute | solution.py:48
  39.2 8.8 %shard_map.73 = (bf16[16,128,128]{2,1,0:T(8,128)(2,1)S(1)}, bf16[16,128,128]{2,1,0:T(8,128)(2,1)S(1)}, f32[16,128,128]{2,1,0:T(8,128)S(1)}, f32[16,128,128]{2,1,...) custom-call(s32[512]{0:T(512)S(1)} %get-tuple-element.57.row_tile_re, ...), custom_call_target="tpu_custom_call" | custom-call | flops 4294967296 | bytes 27262976 | tf_op jit(solution)/shard_map/pallas_call | solution.py:150
  48.2 1.4 collective-permute-start.15
  49.6 1.5 collective-permute-start.20
  51.0 5.4 %collective-permute-done.13 = bf16[16,128,128]{2,1,0:T(8,128)(2,1)S(1)} collective-permute-done((bf16[16,128,128]{2,1,0:T(8,128)(2,1)S(1)}, bf16[16,128,128]{2,1,0:T(8,128)(2,1)S(1)}, u32[]{:S(2)}, u32[]{:S(2)}) %collective-permute-start.13) | collective-permute-done | bytes 524320 | tf_op jit(solution)/shard_map/ppermute | solution.py:48
  56.6 2.7 %collective-permute-start.14 = (bf16[8,128,128]{2,1,0:T(8,128)(2,1)S(1)}, bf16[8,128,128]{2,1,0:T(8,128)(2,1)S(1)}, u32[]{:S(2)}, u32[]{:S(2)}) collective-permute-start(bf16[8,128,128]{2,1,0:T(8,128)(2,1)S(1)} %slice.193), channel_id=1, source_target_pairs={{0,2},{1,7},{2,0},{3,5},{4,6},{5,3},{6,4},{7,1},{8,10},{9,15},{10,... | collective-permute-start | bytes 786440 | tf_op jit(solution)/shard_map/ppermute | solution.py:48
  59.2 2.8 %collective-permute-done.15 = bf16[16,128,128]{2,1,0:T(8,128)(2,1)S(1)} collective-permute-done((bf16[16,128,128]{2,1,0:T(8,128)(2,1)S(1)}, bf16[16,128,128]{2,1,0:T(8,128)(2,1)S(1)}, u32[]{:S(2)}, u32[]{:S(2)}) %collective-permute-start.15) | collective-permute-done | bytes 524320 | tf_op jit(solution)/shard_map/ppermute | solution.py:48
  62.2 2.7 %collective-permute-start.16 = (bf16[8,128,128]{2,1,0:T(8,128)(2,1)S(1)}, bf16[8,128,128]{2,1,0:T(8,128)(2,1)S(1)}, u32[]{:S(2)}, u32[]{:S(2)}) collective-permute-start(bf16[8,128,128]{2,1,0:T(8,128)(2,1)S(1)} %slice.192), channel_id=1, source_target_pairs={{0,2},{1,7},{2,0},{3,5},{4,6},{5,3},{6,4},{7,1},{8,10},{9,15},{10,... | collective-permute-start | bytes 786440 | tf_op jit(solution)/shard_map/ppermute | solution.py:48
  65.0 1.9 %collective-permute-start.21 = (bf16[8,128,128]{2,1,0:T(8,128)(2,1)S(1)}, bf16[8,128,128]{2,1,0:T(8,128)(2,1)S(1)}, u32[]{:S(2)}, u32[]{:S(2)}) collective-permute-start(bf16[8,128,128]{2,1,0:T(8,128)(2,1)S(1)} %slice.190), channel_id=1, source_target_pairs={{0,16},{1,49},{2,18},{3,51},{4,20},{5,53},{6,22},{7,55},{8,24},{9,... | collective-permute-start | bytes 786440 | tf_op jit(solution)/shard_map/ppermute | solution.py:48
  67.1 1.0 collective-permute-start.19
  68.0 3.8 %collective-permute-done.16 = bf16[8,128,128]{2,1,0:T(8,128)(2,1)S(1)} collective-permute-done((bf16[8,128,128]{2,1,0:T(8,128)(2,1)S(1)}, bf16[8,128,128]{2,1,0:T(8,128)(2,1)S(1)}, u32[]{:S(2)}, u32[]{:S(2)}) %collective-permute-start.16) | collective-permute-done | bytes 262176 | tf_op jit(solution)/shard_map/ppermute | solution.py:48
  71.9 1.5 collective-permute-start.17
  73.5 4.3 %collective-permute-start.22 = (bf16[8,128,128]{2,1,0:T(8,128)(2,1)S(1)}, bf16[8,128,128]{2,1,0:T(8,128)(2,1)S(1)}, u32[]{:S(2)}, u32[]{:S(2)}) collective-permute-start(bf16[8,128,128]{2,1,0:T(8,128)(2,1)S(1)} %fusion.11), channel_id=1, source_target_pairs={{0,64},{1,65},{2,66},{3,67},{4,68},{5,69},{6,70},{7,71},{8,72},{9,... | collective-permute-start | bytes 786440 | tf_op jit(solution)/shard_map/ppermute | solution.py:48
  79.1 5.1 %collective-permute-done.22 = bf16[8,128,128]{2,1,0:T(8,128)(2,1)S(1)} collective-permute-done((bf16[8,128,128]{2,1,0:T(8,128)(2,1)S(1)}, bf16[8,128,128]{2,1,0:T(8,128)(2,1)S(1)}, u32[]{:S(2)}, u32[]{:S(2)}) %collective-permute-start.22) | collective-permute-done | bytes 262176 | tf_op jit(solution)/shard_map/ppermute | solution.py:48
  84.4 0.4 collective-permute-start.30
  84.8 0.4 collective-permute-start.28
  85.2 2.9 %collective-permute-start.23 = (bf16[8,128,128]{2,1,0:T(8,128)(2,1)S(1)}, bf16[8,128,128]{2,1,0:T(8,128)(2,1)S(1)}, u32[]{:S(2)}, u32[]{:S(2)}) collective-permute-start(bf16[8,128,128]{2,1,0:T(8,128)(2,1)S(1)} %get-tuple-element.43), channel_id=1, source_target_pairs={{0,2},{1,7},{2,0},{3,5},{4,6},{5,3},{6,4},{7,1},{8,10},{9,15},{10,... | collective-permute-start | bytes 786440 | tf_op jit(solution)/shard_map/ppermute | solution.py:48
  88.1 0.7 collective-permute-start.25
  88.8 5.6 %collective-permute-done.30 = bf16[8,128,128]{2,1,0:T(8,128)(2,1)S(1)} collective-permute-done((bf16[8,128,128]{2,1,0:T(8,128)(2,1)S(1)}, bf16[8,128,128]{2,1,0:T(8,128)(2,1)S(1)}, u32[]{:S(2)}, u32[]{:S(2)}) %collective-permute-start.30) | collective-permute-done | bytes 262176 | tf_op jit(solution)/shard_map/ppermute | solution.py:48
  94.8 2.2 %collective-permute-start.29 = (bf16[16,128,128]{2,1,0:T(8,128)(2,1)S(1)}, bf16[16,128,128]{2,1,0:T(8,128)(2,1)S(1)}, u32[]{:S(2)}, u32[]{:S(2)}) collective-permute-start(bf16[16,128,128]{2,1,0:T(8,128)(2,1)S(1)} %get-tuple-element.47.rest_4_), channel_id=1, source_target_pairs={{0,48},{1,17},{2,50},{3,19},{4,52},{5,21},{6,54},{7,23},{8,56},{9,... | collective-permute-start | bytes 1572872 | tf_op jit(solution)/shard_map/ppermute | solution.py:48
  97.0 2.1 %collective-permute-start.26 = (bf16[8,128,128]{2,1,0:T(8,128)(2,1)S(1)}, bf16[8,128,128]{2,1,0:T(8,128)(2,1)S(1)}, u32[]{:S(2)}, u32[]{:S(2)}) collective-permute-start(bf16[8,128,128]{2,1,0:T(8,128)(2,1)S(1)} %collective-permute-done.25), channel_id=1, source_target_pairs={{0,2},{1,7},{2,0},{3,5},{4,6},{5,3},{6,4},{7,1},{8,10},{9,15},{10,... | collective-permute-start | bytes 786440 | tf_op jit(solution)/shard_map/ppermute | solution.py:48
  99.2 1.6 collective-permute-done.31
  101.0 2.7 %collective-permute-done.26 = bf16[8,128,128]{2,1,0:T(8,128)(2,1)S(1)} collective-permute-done((bf16[8,128,128]{2,1,0:T(8,128)(2,1)S(1)}, bf16[8,128,128]{2,1,0:T(8,128)(2,1)S(1)}, u32[]{:S(2)}, u32[]{:S(2)}) %collective-permute-start.26) | collective-permute-done | bytes 262176 | tf_op jit(solution)/shard_map/ppermute | solution.py:48
  103.8 0.4 collective-permute-start.27
  104.2 2.3 %collective-permute-done.29.rest_5_ = bf16[16,128,128]{2,1,0:T(8,128)(2,1)S(1)} collective-permute-done((bf16[16,128,128]{2,1,0:T(8,128)(2,1)S(1)}, bf16[16,128,128]{2,1,0:T(8,128)(2,1)S(1)}, u32[]{:S(2)}, u32[]{:S(2)}) %collective-permute-start.29) | collective-permute-done | bytes 524320 | tf_op jit(solution)/shard_map/ppermute | solution.py:48
  106.5 1.7 collective-permute-done.24.rest_1_
  108.2 7.0 %collective-permute-done.32.rest_7_ = bf16[16,128,128]{2,1,0:T(8,128)(2,1)S(1)} collective-permute-done((bf16[16,128,128]{2,1,0:T(8,128)(2,1)S(1)}, bf16[16,128,128]{2,1,0:T(8,128)(2,1)S(1)}, u32[]{:S(2)}, u32[]{:S(2)}) %collective-permute-start.32) | collective-permute-done | bytes 524320 | tf_op jit(solution)/shard_map/ppermute | solution.py:48
  115.1 8.8 %shard_map.74 = (bf16[16,128,128]{2,1,0:T(8,128)(2,1)S(1)}, bf16[16,128,128]{2,1,0:T(8,128)(2,1)S(1)}, f32[16,128,128]{2,1,0:T(8,128)S(1)}, f32[16,128,128]{2,1,...) custom-call(s32[512]{0:T(512)S(1)} %get-tuple-element.57.row_tile_re, ...), custom_call_target="tpu_custom_call" | custom-call | flops 4294967296 | bytes 27262976 | tf_op jit(solution)/shard_map/pallas_call | solution.py:150
  124.0 1.5 collective-permute-start.35
  125.5 0.4 collective-permute-start.38
  125.9 1.0 collective-permute-start.40
  126.9 5.4 %collective-permute-done.33 = bf16[16,128,128]{2,1,0:T(8,128)(2,1)S(1)} collective-permute-done((bf16[16,128,128]{2,1,0:T(8,128)(2,1)S(1)}, bf16[16,128,128]{2,1,0:T(8,128)(2,1)S(1)}, u32[]{:S(2)}, u32[]{:S(2)}) %collective-permute-start.33) | collective-permute-done | bytes 524320 | tf_op jit(solution)/shard_map/ppermute | solution.py:48
  132.5 2.6 %collective-permute-start.34 = (bf16[8,128,128]{2,1,0:T(8,128)(2,1)S(1)}, bf16[8,128,128]{2,1,0:T(8,128)(2,1)S(1)}, u32[]{:S(2)}, u32[]{:S(2)}) collective-permute-start(bf16[8,128,128]{2,1,0:T(8,128)(2,1)S(1)} %slice.189), channel_id=1, source_target_pairs={{0,2},{1,7},{2,0},{3,5},{4,6},{5,3},{6,4},{7,1},{8,10},{9,15},{10,... | collective-permute-start | bytes 786440 | tf_op jit(solution)/shard_map/ppermute | solution.py:48
  135.0 2.6 %collective-permute-done.35 = bf16[16,128,128]{2,1,0:T(8,128)(2,1)S(1)} collective-permute-done((bf16[16,128,128]{2,1,0:T(8,128)(2,1)S(1)}, bf16[16,128,128]{2,1,0:T(8,128)(2,1)S(1)}, u32[]{:S(2)}, u32[]{:S(2)}) %collective-permute-start.35) | collective-permute-done | bytes 524320 | tf_op jit(solution)/shard_map/ppermute | solution.py:48
  137.8 2.9 %collective-permute-start.36 = (bf16[8,128,128]{2,1,0:T(8,128)(2,1)S(1)}, bf16[8,128,128]{2,1,0:T(8,128)(2,1)S(1)}, u32[]{:S(2)}, u32[]{:S(2)}) collective-permute-start(bf16[8,128,128]{2,1,0:T(8,128)(2,1)S(1)} %slice.188), channel_id=1, source_target_pairs={{0,2},{1,7},{2,0},{3,5},{4,6},{5,3},{6,4},{7,1},{8,10},{9,15},{10,... | collective-permute-start | bytes 786440 | tf_op jit(solution)/shard_map/ppermute | solution.py:48
  141.1 2.7 %collective-permute-start.39 = (bf16[8,128,128]{2,1,0:T(8,128)(2,1)S(1)}, bf16[8,128,128]{2,1,0:T(8,128)(2,1)S(1)}, u32[]{:S(2)}, u32[]{:S(2)}) collective-permute-start(bf16[8,128,128]{2,1,0:T(8,128)(2,1)S(1)} %slice.187), channel_id=1, source_target_pairs={{0,16},{1,49},{2,18},{3,51},{4,20},{5,53},{6,22},{7,55},{8,24},{9,... | collective-permute-start | bytes 786440 | tf_op jit(solution)/shard_map/ppermute | solution.py:48
  143.8 0.6 collective-permute-done.36
  144.5 1.0 collective-permute-start.37
  145.4 2.2 %collective-permute-done.41 = bf16[8,128,128]{2,1,0:T(8,128)(2,1)S(1)} collective-permute-done((bf16[8,128,128]{2,1,0:T(8,128)(2,1)S(1)}, bf16[8,128,128]{2,1,0:T(8,128)(2,1)S(1)}, u32[]{:S(2)}, u32[]{:S(2)}) %collective-permute-start.41) | collective-permute-done | bytes 262176 | tf_op jit(solution)/shard_map/ppermute | solution.py:48
  147.8 2.9 %collective-permute-done.39 = bf16[8,128,128]{2,1,0:T(8,128)(2,1)S(1)} collective-permute-done((bf16[8,128,128]{2,1,0:T(8,128)(2,1)S(1)}, bf16[8,128,128]{2,1,0:T(8,128)(2,1)S(1)}, u32[]{:S(2)}, u32[]{:S(2)}) %collective-permute-start.39) | collective-permute-done | bytes 262176 | tf_op jit(solution)/shard_map/ppermute | solution.py:48
  150.7 3.8 %collective-permute-done.42 = bf16[8,128,128]{2,1,0:T(8,128)(2,1)S(1)} collective-permute-done((bf16[8,128,128]{2,1,0:T(8,128)(2,1)S(1)}, bf16[8,128,128]{2,1,0:T(8,128)(2,1)S(1)}, u32[]{:S(2)}, u32[]{:S(2)}) %collective-permute-start.42) | collective-permute-done | bytes 262176 | tf_op jit(solution)/shard_map/ppermute | solution.py:48
  154.9 23.6 %collective-permute-start.43 = (f32[512,128]{1,0:T(8,128)S(1)}, f32[512,128]{1,0:T(8,128)S(1)}, u32[]{:S(2)}, u32[]{:S(2)}) collective-permute-start(f32[512,128]{1,0:T(8,128)S(1)} %get-tuple-element.46), channel_id=1, source_target_pairs={{0,1},{1,0},{2,3},{3,2},{4,5},{5,4},{6,7},{7,6},{8,9},{9,8},{10,11... | collective-permute-start | bytes 786440 | tf_op jit(solution)/shard_map/ppermute | solution.py:48
  178.5 1.2 collective-permute-done.43
  179.6 0.8 maximum_select_fusion
  (71 shorter events, 4.2 us)
Async XLA Ops:
  1.0 2.9 %collective-permute-start = (bf16[512,128]{1,0:T(8,128)(2,1)S(1)}, bf16[512,128]{1,0:T(8,128)(2,1)S(1)}, u32[]{:S(2)}, u32[]{:S(2)}) collective-permute-start(bf16[512,128]{1,0:T(8,128)(2,1)S(1)} %get-tuple-element.52), channel_id=1, source_target_pairs={{0,1},{1,0},{2,3},{3,2},{4,5},{5,4},{6,7},{7,6},{8,9},{9,8},{10,11... | collective-permute-start | bytes 393224 | tf_op jit(solution)/shard_map/ppermute | solution.py:48
  3.9 35.4 %collective-permute-start.2 = (bf16[256,128,128]{2,1,0:T(8,128)(2,1)}, bf16[256,128,128]{2,1,0:T(8,128)(2,1)}, u32[]{:S(2)}, u32[]{:S(2)}) collective-permute-start(bf16[256,128,128]{2,1,0:T(8,128)(2,1)} %bitcast.14), channel_id=1, source_target_pairs={{0,1},{1,0},{2,3},{3,2},{4,5},{5,4},{6,7},{7,6},{8,9},{9,8},{10,11... | collective-permute-start | bytes 25165832 | tf_op jit(solution)/shard_map/ppermute | solution.py:48
  4.0 10.3 %collective-permute-start.10 = (bf16[8,128,128]{2,1,0:T(8,128)(2,1)S(1)}, bf16[8,128,128]{2,1,0:T(8,128)(2,1)S(1)}, u32[]{:S(2)}, u32[]{:S(2)}) collective-permute-start(bf16[8,128,128]{2,1,0:T(8,128)(2,1)S(1)} %bitcast.17), channel_id=1, source_target_pairs={{0,64},{1,65},{2,66},{3,67},{4,68},{5,69},{6,70},{7,71},{8,72},{9,... | collective-permute-start | bytes 786440 | tf_op jit(solution)/shard_map/ppermute | solution.py:48
  7.1 7.5 %collective-permute-start.8 = (bf16[8,128,128]{2,1,0:T(8,128)(2,1)S(1)}, bf16[8,128,128]{2,1,0:T(8,128)(2,1)S(1)}, u32[]{:S(2)}, u32[]{:S(2)}) collective-permute-start(bf16[8,128,128]{2,1,0:T(8,128)(2,1)S(1)} %bitcast.18), channel_id=1, source_target_pairs={{0,16},{1,49},{2,18},{3,51},{4,20},{5,53},{6,22},{7,55},{8,24},{9,... | collective-permute-start | bytes 786440 | tf_op jit(solution)/shard_map/ppermute | solution.py:48
  10.9 8.3 %collective-permute-start.3 = (bf16[8,128,128]{2,1,0:T(8,128)(2,1)S(1)}, bf16[8,128,128]{2,1,0:T(8,128)(2,1)S(1)}, u32[]{:S(2)}, u32[]{:S(2)}) collective-permute-start(bf16[8,128,128]{2,1,0:T(8,128)(2,1)S(1)} %bitcast.19), channel_id=1, source_target_pairs={{0,2},{1,7},{2,0},{3,5},{4,6},{5,3},{6,4},{7,1},{8,10},{9,15},{10,... | collective-permute-start | bytes 786440 | tf_op jit(solution)/shard_map/ppermute | solution.py:48
  13.4 6.7 %collective-permute-start.5 = (bf16[8,128,128]{2,1,0:T(8,128)(2,1)S(1)}, bf16[8,128,128]{2,1,0:T(8,128)(2,1)S(1)}, u32[]{:S(2)}, u32[]{:S(2)}) collective-permute-start(bf16[8,128,128]{2,1,0:T(8,128)(2,1)S(1)} %bitcast.20), channel_id=1, source_target_pairs={{0,8},{1,9},{2,10},{3,11},{4,12},{5,13},{6,14},{7,15},{8,0},{9,1},... | collective-permute-start | bytes 786440 | tf_op jit(solution)/shard_map/ppermute | solution.py:48
  14.4 13.4 %collective-permute-start.1 = (s32[640]{0:T(1024)S(1)}, s32[640]{0:T(1024)S(1)}, u32[]{:S(2)}, u32[]{:S(2)}) collective-permute-start(s32[640]{0:T(1024)S(1)} %pad_add_fusion), channel_id=1, source_target_pairs={{0,1},{1,0},{2,3},{3,2},{4,5},{5,4},{6,7},{7,6},{8,9},{9,8},{10,11... | collective-permute-start | bytes 7688 | tf_op jit(solution)/shard_map/ppermute | solution.py:48
  14.6 10.6 %collective-permute-start.11 = (bf16[8,128,128]{2,1,0:T(8,128)(2,1)S(1)}, bf16[8,128,128]{2,1,0:T(8,128)(2,1)S(1)}, u32[]{:S(2)}, u32[]{:S(2)}) collective-permute-start(bf16[8,128,128]{2,1,0:T(8,128)(2,1)S(1)} %collective-permute-done.10), channel_id=1, source_target_pairs={{0,16},{1,49},{2,18},{3,51},{4,20},{5,53},{6,22},{7,55},{8,24},{9,... | collective-permute-start | bytes 786440 | tf_op jit(solution)/shard_map/ppermute | solution.py:48
  19.2 11.9 %collective-permute-start.9 = (bf16[16,128,128]{2,1,0:T(8,128)(2,1)S(1)}, bf16[16,128,128]{2,1,0:T(8,128)(2,1)S(1)}, u32[]{:S(2)}, u32[]{:S(2)}) collective-permute-start(bf16[16,128,128]{2,1,0:T(8,128)(2,1)S(1)} %get-tuple-element.49.rest_4_), channel_id=1, source_target_pairs={{0,48},{1,17},{2,50},{3,19},{4,52},{5,21},{6,54},{7,23},{8,56},{9,... | collective-permute-start | bytes 1572872 | tf_op jit(solution)/shard_map/ppermute | solution.py:48
  20.1 7.5 %collective-permute-start.6 = (bf16[8,128,128]{2,1,0:T(8,128)(2,1)S(1)}, bf16[8,128,128]{2,1,0:T(8,128)(2,1)S(1)}, u32[]{:S(2)}, u32[]{:S(2)}) collective-permute-start(bf16[8,128,128]{2,1,0:T(8,128)(2,1)S(1)} %collective-permute-done.5), channel_id=1, source_target_pairs={{0,2},{1,7},{2,0},{3,5},{4,6},{5,3},{6,4},{7,1},{8,10},{9,15},{10,... | collective-permute-start | bytes 786440 | tf_op jit(solution)/shard_map/ppermute | solution.py:48
  25.3 8.3 %collective-permute-start.4 = (bf16[16,128,128]{2,1,0:T(8,128)(2,1)S(1)}, bf16[16,128,128]{2,1,0:T(8,128)(2,1)S(1)}, u32[]{:S(2)}, u32[]{:S(2)}) collective-permute-start(bf16[16,128,128]{2,1,0:T(8,128)(2,1)S(1)} %get-tuple-element.50.rest_0_), channel_id=1, source_target_pairs={{0,6},{1,3},{2,4},{3,1},{4,2},{5,7},{6,0},{7,5},{8,14},{9,11},{10,... | collective-permute-start | bytes 1572872 | tf_op jit(solution)/shard_map/ppermute | solution.py:48
  27.6 8.3 %collective-permute-start.12 = (bf16[16,128,128]{2,1,0:T(8,128)(2,1)S(1)}, bf16[16,128,128]{2,1,0:T(8,128)(2,1)S(1)}, u32[]{:S(2)}, u32[]{:S(2)}) collective-permute-start(bf16[16,128,128]{2,1,0:T(8,128)(2,1)S(1)} %constant_dynamic-update-slice_fusion.2.rest_6_), channel_id=1, source_target_pairs={{0,48},{1,17},{2,50},{3,19},{4,52},{5,21},{6,54},{7,23},{8,56},{9,... | collective-permute-start | bytes 1572872 | tf_op jit(solution)/shard_map/ppermute | solution.py:48
  27.8 11.5 %collective-permute-start.7 = (bf16[16,128,128]{2,1,0:T(8,128)(2,1)S(1)}, bf16[16,128,128]{2,1,0:T(8,128)(2,1)S(1)}, u32[]{:S(2)}, u32[]{:S(2)}) collective-permute-start(bf16[16,128,128]{2,1,0:T(8,128)(2,1)S(1)} %constant_dynamic-update-slice_fusion.rest_2_), channel_id=1, source_target_pairs={{0,6},{1,3},{2,4},{3,1},{4,2},{5,7},{6,0},{7,5},{8,14},{9,11},{10,... | collective-permute-start | bytes 1572872 | tf_op jit(solution)/shard_map/ppermute | solution.py:48
  48.0 8.4 %collective-permute-start.13 = (bf16[16,128,128]{2,1,0:T(8,128)(2,1)S(1)}, bf16[16,128,128]{2,1,0:T(8,128)(2,1)S(1)}, u32[]{:S(2)}, u32[]{:S(2)}) collective-permute-start(bf16[16,128,128]{2,1,0:T(8,128)(2,1)S(1)} %get-tuple-element.28), channel_id=1, source_target_pairs={{0,6},{1,3},{2,4},{3,1},{4,2},{5,7},{6,0},{7,5},{8,14},{9,11},{10,... | collective-permute-start | bytes 1572872 | tf_op jit(solution)/shard_map/ppermute | solution.py:48
  48.2 13.8 %collective-permute-start.15 = (bf16[16,128,128]{2,1,0:T(8,128)(2,1)S(1)}, bf16[16,128,128]{2,1,0:T(8,128)(2,1)S(1)}, u32[]{:S(2)}, u32[]{:S(2)}) collective-permute-start(bf16[16,128,128]{2,1,0:T(8,128)(2,1)S(1)} %get-tuple-element.30), channel_id=1, source_target_pairs={{0,6},{1,3},{2,4},{3,1},{4,2},{5,7},{6,0},{7,5},{8,14},{9,11},{10,... | collective-permute-start | bytes 1572872 | tf_op jit(solution)/shard_map/ppermute | solution.py:48
  49.5 17.4 %collective-permute-start.18 = (bf16[16,128,128]{2,1,0:T(8,128)(2,1)S(1)}, bf16[16,128,128]{2,1,0:T(8,128)(2,1)S(1)}, u32[]{:S(2)}, u32[]{:S(2)}) collective-permute-start(bf16[16,128,128]{2,1,0:T(8,128)(2,1)S(1)} %get-tuple-element.32), channel_id=1, source_target_pairs={{0,48},{1,17},{2,50},{3,19},{4,52},{5,21},{6,54},{7,23},{8,56},{9,... | collective-permute-start | bytes 1572872 | tf_op jit(solution)/shard_map/ppermute | solution.py:48
  49.6 15.3 %collective-permute-start.20 = (bf16[16,128,128]{2,1,0:T(8,128)(2,1)S(1)}, bf16[16,128,128]{2,1,0:T(8,128)(2,1)S(1)}, u32[]{:S(2)}, u32[]{:S(2)}) collective-permute-start(bf16[16,128,128]{2,1,0:T(8,128)(2,1)S(1)} %get-tuple-element.34), channel_id=1, source_target_pairs={{0,48},{1,17},{2,50},{3,19},{4,52},{5,21},{6,54},{7,23},{8,56},{9,... | collective-permute-start | bytes 1572872 | tf_op jit(solution)/shard_map/ppermute | solution.py:48
  56.6 22.5 %collective-permute-start.14 = (bf16[8,128,128]{2,1,0:T(8,128)(2,1)S(1)}, bf16[8,128,128]{2,1,0:T(8,128)(2,1)S(1)}, u32[]{:S(2)}, u32[]{:S(2)}) collective-permute-start(bf16[8,128,128]{2,1,0:T(8,128)(2,1)S(1)} %slice.193), channel_id=1, source_target_pairs={{0,2},{1,7},{2,0},{3,5},{4,6},{5,3},{6,4},{7,1},{8,10},{9,15},{10,... | collective-permute-start | bytes 786440 | tf_op jit(solution)/shard_map/ppermute | solution.py:48
  62.2 9.7 %collective-permute-start.16 = (bf16[8,128,128]{2,1,0:T(8,128)(2,1)S(1)}, bf16[8,128,128]{2,1,0:T(8,128)(2,1)S(1)}, u32[]{:S(2)}, u32[]{:S(2)}) collective-permute-start(bf16[8,128,128]{2,1,0:T(8,128)(2,1)S(1)} %slice.192), channel_id=1, source_target_pairs={{0,2},{1,7},{2,0},{3,5},{4,6},{5,3},{6,4},{7,1},{8,10},{9,15},{10,... | collective-permute-start | bytes 786440 | tf_op jit(solution)/shard_map/ppermute | solution.py:48
  65.0 8.4 %collective-permute-start.21 = (bf16[8,128,128]{2,1,0:T(8,128)(2,1)S(1)}, bf16[8,128,128]{2,1,0:T(8,128)(2,1)S(1)}, u32[]{:S(2)}, u32[]{:S(2)}) collective-permute-start(bf16[8,128,128]{2,1,0:T(8,128)(2,1)S(1)} %slice.190), channel_id=1, source_target_pairs={{0,16},{1,49},{2,18},{3,51},{4,20},{5,53},{6,22},{7,55},{8,24},{9,... | collective-permute-start | bytes 786440 | tf_op jit(solution)/shard_map/ppermute | solution.py:48
  67.1 12.0 %collective-permute-start.19 = (bf16[8,128,128]{2,1,0:T(8,128)(2,1)S(1)}, bf16[8,128,128]{2,1,0:T(8,128)(2,1)S(1)}, u32[]{:S(2)}, u32[]{:S(2)}) collective-permute-start(bf16[8,128,128]{2,1,0:T(8,128)(2,1)S(1)} %slice.191), channel_id=1, source_target_pairs={{0,16},{1,49},{2,18},{3,51},{4,20},{5,53},{6,22},{7,55},{8,24},{9,... | collective-permute-start | bytes 786440 | tf_op jit(solution)/shard_map/ppermute | solution.py:48
  71.9 7.1 %collective-permute-start.17 = (bf16[8,128,128]{2,1,0:T(8,128)(2,1)S(1)}, bf16[8,128,128]{2,1,0:T(8,128)(2,1)S(1)}, u32[]{:S(2)}, u32[]{:S(2)}) collective-permute-start(bf16[8,128,128]{2,1,0:T(8,128)(2,1)S(1)} %fusion.14), channel_id=1, source_target_pairs={{0,8},{1,9},{2,10},{3,11},{4,12},{5,13},{6,14},{7,15},{8,0},{9,1},... | collective-permute-start | bytes 786440 | tf_op jit(solution)/shard_map/ppermute | solution.py:48
  73.5 10.7 %collective-permute-start.22 = (bf16[8,128,128]{2,1,0:T(8,128)(2,1)S(1)}, bf16[8,128,128]{2,1,0:T(8,128)(2,1)S(1)}, u32[]{:S(2)}, u32[]{:S(2)}) collective-permute-start(bf16[8,128,128]{2,1,0:T(8,128)(2,1)S(1)} %fusion.11), channel_id=1, source_target_pairs={{0,64},{1,65},{2,66},{3,67},{4,68},{5,69},{6,70},{7,71},{8,72},{9,... | collective-permute-start | bytes 786440 | tf_op jit(solution)/shard_map/ppermute | solution.py:48
  84.4 10.0 %collective-permute-start.30 = (bf16[8,128,128]{2,1,0:T(8,128)(2,1)S(1)}, bf16[8,128,128]{2,1,0:T(8,128)(2,1)S(1)}, u32[]{:S(2)}, u32[]{:S(2)}) collective-permute-start(bf16[8,128,128]{2,1,0:T(8,128)(2,1)S(1)} %get-tuple-element.43), channel_id=1, source_target_pairs={{0,64},{1,65},{2,66},{3,67},{4,68},{5,69},{6,70},{7,71},{8,72},{9,... | collective-permute-start | bytes 786440 | tf_op jit(solution)/shard_map/ppermute | solution.py:48
  84.8 9.9 %collective-permute-start.28 = (bf16[8,128,128]{2,1,0:T(8,128)(2,1)S(1)}, bf16[8,128,128]{2,1,0:T(8,128)(2,1)S(1)}, u32[]{:S(2)}, u32[]{:S(2)}) collective-permute-start(bf16[8,128,128]{2,1,0:T(8,128)(2,1)S(1)} %get-tuple-element.43), channel_id=1, source_target_pairs={{0,16},{1,49},{2,18},{3,51},{4,20},{5,53},{6,22},{7,55},{8,24},{9,... | collective-permute-start | bytes 786440 | tf_op jit(solution)/shard_map/ppermute | solution.py:48
  85.2 9.5 %collective-permute-start.23 = (bf16[8,128,128]{2,1,0:T(8,128)(2,1)S(1)}, bf16[8,128,128]{2,1,0:T(8,128)(2,1)S(1)}, u32[]{:S(2)}, u32[]{:S(2)}) collective-permute-start(bf16[8,128,128]{2,1,0:T(8,128)(2,1)S(1)} %get-tuple-element.43), channel_id=1, source_target_pairs={{0,2},{1,7},{2,0},{3,5},{4,6},{5,3},{6,4},{7,1},{8,10},{9,15},{10,... | collective-permute-start | bytes 786440 | tf_op jit(solution)/shard_map/ppermute | solution.py:48
  88.1 9.0 %collective-permute-start.25 = (bf16[8,128,128]{2,1,0:T(8,128)(2,1)S(1)}, bf16[8,128,128]{2,1,0:T(8,128)(2,1)S(1)}, u32[]{:S(2)}, u32[]{:S(2)}) collective-permute-start(bf16[8,128,128]{2,1,0:T(8,128)(2,1)S(1)} %get-tuple-element.43), channel_id=1, source_target_pairs={{0,8},{1,9},{2,10},{3,11},{4,12},{5,13},{6,14},{7,15},{8,0},{9,1},... | collective-permute-start | bytes 786440 | tf_op jit(solution)/shard_map/ppermute | solution.py:48
  94.4 6.4 %collective-permute-start.31 = (bf16[8,128,128]{2,1,0:T(8,128)(2,1)S(1)}, bf16[8,128,128]{2,1,0:T(8,128)(2,1)S(1)}, u32[]{:S(2)}, u32[]{:S(2)}) collective-permute-start(bf16[8,128,128]{2,1,0:T(8,128)(2,1)S(1)} %collective-permute-done.30), channel_id=1, source_target_pairs={{0,16},{1,49},{2,18},{3,51},{4,20},{5,53},{6,22},{7,55},{8,24},{9,... | collective-permute-start | bytes 786440 | tf_op jit(solution)/shard_map/ppermute | solution.py:48
  94.8 11.6 %collective-permute-start.29 = (bf16[16,128,128]{2,1,0:T(8,128)(2,1)S(1)}, bf16[16,128,128]{2,1,0:T(8,128)(2,1)S(1)}, u32[]{:S(2)}, u32[]{:S(2)}) collective-permute-start(bf16[16,128,128]{2,1,0:T(8,128)(2,1)S(1)} %get-tuple-element.47.rest_4_), channel_id=1, source_target_pairs={{0,48},{1,17},{2,50},{3,19},{4,52},{5,21},{6,54},{7,23},{8,56},{9,... | collective-permute-start | bytes 1572872 | tf_op jit(solution)/shard_map/ppermute | solution.py:48
  97.0 11.1 %collective-permute-start.24 = (bf16[16,128,128]{2,1,0:T(8,128)(2,1)S(1)}, bf16[16,128,128]{2,1,0:T(8,128)(2,1)S(1)}, u32[]{:S(2)}, u32[]{:S(2)}) collective-permute-start(bf16[16,128,128]{2,1,0:T(8,128)(2,1)S(1)} %get-tuple-element.48.rest_0_), channel_id=1, source_target_pairs={{0,6},{1,3},{2,4},{3,1},{4,2},{5,7},{6,0},{7,5},{8,14},{9,11},{10,... | collective-permute-start | bytes 1572872 | tf_op jit(solution)/shard_map/ppermute | solution.py:48
  97.0 6.7 %collective-permute-start.26 = (bf16[8,128,128]{2,1,0:T(8,128)(2,1)S(1)}, bf16[8,128,128]{2,1,0:T(8,128)(2,1)S(1)}, u32[]{:S(2)}, u32[]{:S(2)}) collective-permute-start(bf16[8,128,128]{2,1,0:T(8,128)(2,1)S(1)} %collective-permute-done.25), channel_id=1, source_target_pairs={{0,2},{1,7},{2,0},{3,5},{4,6},{5,3},{6,4},{7,1},{8,10},{9,15},{10,... | collective-permute-start | bytes 786440 | tf_op jit(solution)/shard_map/ppermute | solution.py:48
  100.9 14.3 %collective-permute-start.32 = (bf16[16,128,128]{2,1,0:T(8,128)(2,1)S(1)}, bf16[16,128,128]{2,1,0:T(8,128)(2,1)S(1)}, u32[]{:S(2)}, u32[]{:S(2)}) collective-permute-start(bf16[16,128,128]{2,1,0:T(8,128)(2,1)S(1)} %constant_dynamic-update-slice_fusion.6.rest_6_), channel_id=1, source_target_pairs={{0,48},{1,17},{2,50},{3,19},{4,52},{5,21},{6,54},{7,23},{8,56},{9,... | collective-permute-start | bytes 1572872 | tf_op jit(solution)/shard_map/ppermute | solution.py:48
  103.8 11.3 %collective-permute-start.27 = (bf16[16,128,128]{2,1,0:T(8,128)(2,1)S(1)}, bf16[16,128,128]{2,1,0:T(8,128)(2,1)S(1)}, u32[]{:S(2)}, u32[]{:S(2)}) collective-permute-start(bf16[16,128,128]{2,1,0:T(8,128)(2,1)S(1)} %constant_dynamic-update-slice_fusion.4.rest_2_), channel_id=1, source_target_pairs={{0,6},{1,3},{2,4},{3,1},{4,2},{5,7},{6,0},{7,5},{8,14},{9,11},{10,... | collective-permute-start | bytes 1572872 | tf_op jit(solution)/shard_map/ppermute | solution.py:48
  123.9 8.4 %collective-permute-start.33 = (bf16[16,128,128]{2,1,0:T(8,128)(2,1)S(1)}, bf16[16,128,128]{2,1,0:T(8,128)(2,1)S(1)}, u32[]{:S(2)}, u32[]{:S(2)}) collective-permute-start(bf16[16,128,128]{2,1,0:T(8,128)(2,1)S(1)} %get-tuple-element.36), channel_id=1, source_target_pairs={{0,6},{1,3},{2,4},{3,1},{4,2},{5,7},{6,0},{7,5},{8,14},{9,11},{10,... | collective-permute-start | bytes 1572872 | tf_op jit(solution)/shard_map/ppermute | solution.py:48
  124.0 13.6 %collective-permute-start.35 = (bf16[16,128,128]{2,1,0:T(8,128)(2,1)S(1)}, bf16[16,128,128]{2,1,0:T(8,128)(2,1)S(1)}, u32[]{:S(2)}, u32[]{:S(2)}) collective-permute-start(bf16[16,128,128]{2,1,0:T(8,128)(2,1)S(1)} %get-tuple-element.38), channel_id=1, source_target_pairs={{0,6},{1,3},{2,4},{3,1},{4,2},{5,7},{6,0},{7,5},{8,14},{9,11},{10,... | collective-permute-start | bytes 1572872 | tf_op jit(solution)/shard_map/ppermute | solution.py:48
  125.5 15.5 %collective-permute-start.38 = (bf16[16,128,128]{2,1,0:T(8,128)(2,1)S(1)}, bf16[16,128,128]{2,1,0:T(8,128)(2,1)S(1)}, u32[]{:S(2)}, u32[]{:S(2)}) collective-permute-start(bf16[16,128,128]{2,1,0:T(8,128)(2,1)S(1)} %get-tuple-element.40), channel_id=1, source_target_pairs={{0,48},{1,17},{2,50},{3,19},{4,52},{5,21},{6,54},{7,23},{8,56},{9,... | collective-permute-start | bytes 1572872 | tf_op jit(solution)/shard_map/ppermute | solution.py:48
  125.9 14.8 %collective-permute-start.40 = (bf16[16,128,128]{2,1,0:T(8,128)(2,1)S(1)}, bf16[16,128,128]{2,1,0:T(8,128)(2,1)S(1)}, u32[]{:S(2)}, u32[]{:S(2)}) collective-permute-start(bf16[16,128,128]{2,1,0:T(8,128)(2,1)S(1)} %get-tuple-element.42), channel_id=1, source_target_pairs={{0,48},{1,17},{2,50},{3,19},{4,52},{5,21},{6,54},{7,23},{8,56},{9,... | collective-permute-start | bytes 1572872 | tf_op jit(solution)/shard_map/ppermute | solution.py:48
  132.5 15.3 %collective-permute-start.34 = (bf16[8,128,128]{2,1,0:T(8,128)(2,1)S(1)}, bf16[8,128,128]{2,1,0:T(8,128)(2,1)S(1)}, u32[]{:S(2)}, u32[]{:S(2)}) collective-permute-start(bf16[8,128,128]{2,1,0:T(8,128)(2,1)S(1)} %slice.189), channel_id=1, source_target_pairs={{0,2},{1,7},{2,0},{3,5},{4,6},{5,3},{6,4},{7,1},{8,10},{9,15},{10,... | collective-permute-start | bytes 786440 | tf_op jit(solution)/shard_map/ppermute | solution.py:48
  137.8 6.6 %collective-permute-start.36 = (bf16[8,128,128]{2,1,0:T(8,128)(2,1)S(1)}, bf16[8,128,128]{2,1,0:T(8,128)(2,1)S(1)}, u32[]{:S(2)}, u32[]{:S(2)}) collective-permute-start(bf16[8,128,128]{2,1,0:T(8,128)(2,1)S(1)} %slice.188), channel_id=1, source_target_pairs={{0,2},{1,7},{2,0},{3,5},{4,6},{5,3},{6,4},{7,1},{8,10},{9,15},{10,... | collective-permute-start | bytes 786440 | tf_op jit(solution)/shard_map/ppermute | solution.py:48
  140.8 6.8 %collective-permute-start.41 = (bf16[8,128,128]{2,1,0:T(8,128)(2,1)S(1)}, bf16[8,128,128]{2,1,0:T(8,128)(2,1)S(1)}, u32[]{:S(2)}, u32[]{:S(2)}) collective-permute-start(bf16[8,128,128]{2,1,0:T(8,128)(2,1)S(1)} %slice.186), channel_id=1, source_target_pairs={{0,16},{1,49},{2,18},{3,51},{4,20},{5,53},{6,22},{7,55},{8,24},{9,... | collective-permute-start | bytes 786440 | tf_op jit(solution)/shard_map/ppermute | solution.py:48
  141.1 9.6 %collective-permute-start.39 = (bf16[8,128,128]{2,1,0:T(8,128)(2,1)S(1)}, bf16[8,128,128]{2,1,0:T(8,128)(2,1)S(1)}, u32[]{:S(2)}, u32[]{:S(2)}) collective-permute-start(bf16[8,128,128]{2,1,0:T(8,128)(2,1)S(1)} %slice.187), channel_id=1, source_target_pairs={{0,16},{1,49},{2,18},{3,51},{4,20},{5,53},{6,22},{7,55},{8,24},{9,... | collective-permute-start | bytes 786440 | tf_op jit(solution)/shard_map/ppermute | solution.py:48
  144.5 6.2 %collective-permute-start.37 = (bf16[8,128,128]{2,1,0:T(8,128)(2,1)S(1)}, bf16[8,128,128]{2,1,0:T(8,128)(2,1)S(1)}, u32[]{:S(2)}, u32[]{:S(2)}) collective-permute-start(bf16[8,128,128]{2,1,0:T(8,128)(2,1)S(1)} %fusion.9), channel_id=1, source_target_pairs={{0,8},{1,9},{2,10},{3,11},{4,12},{5,13},{6,14},{7,15},{8,0},{9,1},... | collective-permute-start | bytes 786440 | tf_op jit(solution)/shard_map/ppermute | solution.py:48
  147.7 6.8 %collective-permute-start.42 = (bf16[8,128,128]{2,1,0:T(8,128)(2,1)S(1)}, bf16[8,128,128]{2,1,0:T(8,128)(2,1)S(1)}, u32[]{:S(2)}, u32[]{:S(2)}) collective-permute-start(bf16[8,128,128]{2,1,0:T(8,128)(2,1)S(1)} %fusion.6), channel_id=1, source_target_pairs={{0,64},{1,65},{2,66},{3,67},{4,68},{5,69},{6,70},{7,71},{8,72},{9,... | collective-permute-start | bytes 786440 | tf_op jit(solution)/shard_map/ppermute | solution.py:48
  154.9 24.7 %collective-permute-start.43 = (f32[512,128]{1,0:T(8,128)S(1)}, f32[512,128]{1,0:T(8,128)S(1)}, u32[]{:S(2)}, u32[]{:S(2)}) collective-permute-start(f32[512,128]{1,0:T(8,128)S(1)} %get-tuple-element.46), channel_id=1, source_target_pairs={{0,1},{1,0},{2,3},{3,2},{4,5},{5,4},{6,7},{7,6},{8,9},{9,8},{10,11... | collective-permute-start | bytes 786440 | tf_op jit(solution)/shard_map/ppermute | solution.py:48
where the time goes:
time: 179 us; the launch traced here: 180 us
  starting transfers between devices  80.9 us (45%)
  waiting for transfers between devices  70.8 us (40%)
  Pallas kernels  17.5 us (10%)
  other arithmetic  7.25 us (4%)
  between operations  2.36 us (1%)
    ppermute x44, starting transfers between devices, move(): return lax.ppermute(value, BOTH, table)  80.9 us
    ppermute x44, waiting for transfers between devices, move(): return lax.ppermute(value, BOTH, table)  70.8 us
    pallas_call x2, Pallas kernels, slot_products(): pl.pallas_call(slot_kernel, in_specs=[in_smem] * 3 + [anywhere] * 10, out...  17.5 us
  transfers between devices with their start and end apart: 44, of which 24 were waited for; matrix products, arithmetic and copies ran while one was open for 4% of the time, Pallas kernels for 0%

commit v1 on v0

--- a/solution.py
+++ b/solution.py
@@ -12,6 +12,8 @@
 UNROLL = 16
 GROUP = 64
 BOTH = ("row", "col")
+ROW_FLIPS = (0, 1)
+COL_FLIPS = (0, 1)
 
 
 def linear(y_hi, z, y_lo, x, core):
@@ -32,16 +34,22 @@
 
 
 TO_CORE = pairs(lambda h, z, l, x, k: (h, z, l, x, k ^ 1))
-ROW_MOVES = (
-    pairs(lambda h, z, l, x, k: (h, z, l ^ 1, x, k)),
-    pairs(lambda h, z, l, x, k: (h, z, l, x ^ ring_first(k), k)),
-    pairs(lambda h, z, l, x, k: (h, z, l, x ^ ring_second(k), k)),
-)
-COL_MOVES = (
-    pairs(lambda h, z, l, x, k: (h ^ 1, z, l, x, k)),
-    pairs(lambda h, z, l, x, k: (h, z ^ ring_first(k), l, x, k)),
-    pairs(lambda h, z, l, x, k: (h, z ^ ring_second(k), l, x, k)),
-)
+
+
+def row_moves(flip):
+    return (
+        pairs(lambda h, z, l, x, k: (h, z, l ^ 1, x, k)),
+        pairs(lambda h, z, l, x, k: (h, z, l, x ^ ring_first(k ^ flip), k)),
+        pairs(lambda h, z, l, x, k: (h, z, l, x ^ ring_second(k ^ flip), k)),
+    )
+
+
+def col_moves(flip):
+    return (
+        pairs(lambda h, z, l, x, k: (h ^ 1, z, l, x, k)),
+        pairs(lambda h, z, l, x, k: (h, z ^ ring_first(k ^ flip), l, x, k)),
+        pairs(lambda h, z, l, x, k: (h, z ^ ring_second(k ^ flip), l, x, k)),
+    )
 
 
 def move(value, table):
@@ -182,13 +190,14 @@
 def scatter_sum(sent_first, sent_next, kept_first, kept_next, moves):
     across, first, second = moves
     half = kept_first.shape[0] // 2
-    sums = []
-    for keep, send in ((kept_first, sent_first), (kept_next, sent_next)):
-        near = keep + move(send, second).astype(jnp.float32)
-        sums.append(
-            near[:half] + move(near[half:].astype(jnp.bfloat16), first).astype(jnp.float32)
-        )
-    return sums[1] + move(sums[0].astype(jnp.bfloat16), across).astype(jnp.float32)
+    got = move(sent_first, second)
+    got, sent_next = lax.optimization_barrier((got, sent_next))
+    near = kept_first + got.astype(jnp.float32)
+    sum_first = near[:half] + move(near[half:].astype(jnp.bfloat16), first).astype(jnp.float32)
+    got = move(sent_next, second)
+    near = kept_next + got.astype(jnp.float32)
+    sum_next = near[:half] + move(near[half:].astype(jnp.bfloat16), first).astype(jnp.float32)
+    return sum_next + move(sum_first.astype(jnp.bfloat16), across).astype(jnp.float32)
 
 
 def place_of(near_bit, ring, core):
@@ -221,29 +230,32 @@
         core == 0, jnp.concatenate([mine, other]), jnp.concatenate([other, mine])
     )
 
-    def tiles_of(table, source_core):
+    def tiles_of(table, source_core, row_core, col_core):
         rows, cols, count = table[:slots], table[slots : 2 * slots], table[2 * slots]
         live = jnp.arange(slots) < count
-        place = place_of((rows >> 5) ^ (col_at >> 3), ((rows >> 3) & 3) ^ ((col_at >> 1) & 3), core)
+        place = place_of(
+            (rows >> 5) ^ (col_at >> 3), ((rows >> 3) & 3) ^ ((col_at >> 1) & 3), row_core
+        )
         row_tiles = place * 8 + (rows & 7)
-        place = place_of((cols >> 4) ^ (row_at >> 2), ((cols >> 2) & 3) ^ (row_at & 3), core)
+        place = place_of((cols >> 4) ^ (row_at >> 2), ((cols >> 2) & 3) ^ (row_at & 3), col_core)
         col_tiles = place * 8 + source_core * 4 + (cols & 3)
-        return jnp.where(live, row_tiles, 64), jnp.where(live, col_tiles, 64), count
-
-    own_rows, own_cols, own_count = tiles_of(table, core)
-    mate_rows, mate_cols, mate_count = tiles_of(mate_table, 1 - core)
-    row_tiles = jnp.concatenate([own_rows, mate_rows])
-    col_tiles = jnp.concatenate([own_cols, mate_cols])
-    counts = jnp.stack([own_count, mate_count])
+        return jnp.where(live, row_tiles, 64), jnp.where(live, col_tiles, 64)
+
+    counts = jnp.stack([table[2 * slots], mate_table[2 * slots]])
 
     current = operand.astype(jnp.float32)
     previous = jnp.zeros_like(current)
     for degree in range(DEGREE):
         tiled = current.astype(jnp.bfloat16).reshape(-1, order, half)
-        col_parts = gather(tiled, COL_MOVES)
-        row_parts = gather(tiled, ROW_MOVES)
+        row_flip, col_flip = ROW_FLIPS[degree % 2], COL_FLIPS[degree % 2]
+        row_plan, col_plan = row_moves(row_flip), col_moves(col_flip)
+        own_tiles = tiles_of(table, core, core ^ row_flip, core ^ col_flip)
+        mate_tiles = tiles_of(mate_table, 1 - core, core ^ row_flip, core ^ col_flip)
+        row_tiles, col_tiles = (jnp.concatenate(pair) for pair in zip(own_tiles, mate_tiles))
+        col_parts = gather(tiled, col_plan)
+        row_parts = gather(tiled, row_plan)
         found = slot_products(row_tiles, col_tiles, counts, own, mate, row_parts, col_parts)
-        applied = scatter_sum(*found[:4], ROW_MOVES) + scatter_sum(*found[4:], COL_MOVES)
+        applied = scatter_sum(*found[:4], row_plan) + scatter_sum(*found[4:], col_plan)
         shifted = applied.reshape(2 * seg, half) - center * current
         if degree == 0:
             following = shifted / half_width

time: 179 us -> 167 us (0.933); the launches traced: 180 us -> 166 us
  waiting for transfers between devices: 70.8 us -> 58.9 us
  Pallas kernels: 17.5 us -> 13 us
  starting transfers between devices: 80.9 us -> 83.3 us
    ppermute x44, waiting for transfers between devices: 70.8 us -> 58.9 us  [move(): return lax.ppermute(value, BOTH, table)]
    pallas_call x2, Pallas kernels: 17.5 us -> 13 us  [slot_products(): pl.pallas_call(slot_kernel, in_specs=[in_smem] * 3 + [anywhere] * 10, out...]
    ppermute x44, starting transfers between devices: 80.9 us -> 83.3 us  [move(): return lax.ppermute(value, BOTH, table)]
  transfers between devices with their start and end apart: 44 -> 44, of which waited for: 24 -> 23; matrix products, arithmetic and copies ran while one was open for 4% -> 4% of each run, Pallas kernels for 0% -> 0%
where the time goes in v1:
time: 167 us; the launch traced here: 166 us
  starting transfers between devices  83.3 us (50%)
  waiting for transfers between devices  58.9 us (35%)
  Pallas kernels  13 us (8%)
  other arithmetic  7.12 us (4%)
  between operations  2.34 us (1%)
    ppermute x44, starting transfers between devices, move(): return lax.ppermute(value, BOTH, table)  83.3 us
    ppermute x44, waiting for transfers between devices, move(): return lax.ppermute(value, BOTH, table)  58.9 us
    pallas_call x2, Pallas kernels, slot_products(): pl.pallas_call(slot_kernel, in_specs=[in_smem] * 3 + [anywhere] * 10, out...  13 us
  transfers between devices with their start and end apart: 44, of which 23 were waited for; matrix products, arithmetic and copies ran while one was open for 4% of the time, Pallas kernels for 0%

profile of v1, /device:TPU:1, one launch (start us, length us, event | category | flops | bytes accessed | tf_op | source)
XLA Modules:
  0.0 166.2 jit_solution(2532279159273813815)
XLA Ops:
  0.0 1.0 broadcast_select_fusion
  1.0 1.5 collective-permute-start
  3.2 0.7 pad_add_fusion
  4.0 3.1 %collective-permute-start.10 = (bf16[8,128,128]{2,1,0:T(8,128)(2,1)S(1)}, bf16[8,128,128]{2,1,0:T(8,128)(2,1)S(1)}, u32[]{:S(2)}, u32[]{:S(2)}) collective-permute-start(bf16[8,128,128]{2,1,0:T(8,128)(2,1)S(1)} %bitcast.17), channel_id=1, source_target_pairs={{0,64},{1,65},{2,66},{3,67},{4,68},{5,69},{6,70},{7,71},{8,72},{9,... | collective-permute-start | bytes 786440 | tf_op jit(solution)/shard_map/ppermute | solution.py:56
  7.1 3.8 %collective-permute-start.8 = (bf16[8,128,128]{2,1,0:T(8,128)(2,1)S(1)}, bf16[8,128,128]{2,1,0:T(8,128)(2,1)S(1)}, u32[]{:S(2)}, u32[]{:S(2)}) collective-permute-start(bf16[8,128,128]{2,1,0:T(8,128)(2,1)S(1)} %bitcast.18), channel_id=1, source_target_pairs={{0,16},{1,49},{2,18},{3,51},{4,20},{5,53},{6,22},{7,55},{8,24},{9,... | collective-permute-start | bytes 786440 | tf_op jit(solution)/shard_map/ppermute | solution.py:56
  10.9 2.5 %collective-permute-start.3 = (bf16[8,128,128]{2,1,0:T(8,128)(2,1)S(1)}, bf16[8,128,128]{2,1,0:T(8,128)(2,1)S(1)}, u32[]{:S(2)}, u32[]{:S(2)}) collective-permute-start(bf16[8,128,128]{2,1,0:T(8,128)(2,1)S(1)} %bitcast.19), channel_id=1, source_target_pairs={{0,2},{1,7},{2,0},{3,5},{4,6},{5,3},{6,4},{7,1},{8,10},{9,15},{10,... | collective-permute-start | bytes 786440 | tf_op jit(solution)/shard_map/ppermute | solution.py:56
  13.4 0.4 collective-permute-start.5
  13.8 0.5 slice.100
  14.6 4.5 %collective-permute-start.11 = (bf16[8,128,128]{2,1,0:T(8,128)(2,1)S(1)}, bf16[8,128,128]{2,1,0:T(8,128)(2,1)S(1)}, u32[]{:S(2)}, u32[]{:S(2)}) collective-permute-start(bf16[8,128,128]{2,1,0:T(8,128)(2,1)S(1)} %collective-permute-done.10), channel_id=1, source_target_pairs={{0,16},{1,49},{2,18},{3,51},{4,20},{5,53},{6,22},{7,55},{8,24},{9,... | collective-permute-start | bytes 786440 | tf_op jit(solution)/shard_map/ppermute | solution.py:56
  19.3 0.8 collective-permute-done.5
  20.1 1.9 %collective-permute-start.6 = (bf16[8,128,128]{2,1,0:T(8,128)(2,1)S(1)}, bf16[8,128,128]{2,1,0:T(8,128)(2,1)S(1)}, u32[]{:S(2)}, u32[]{:S(2)}) collective-permute-start(bf16[8,128,128]{2,1,0:T(8,128)(2,1)S(1)} %collective-permute-done.5), channel_id=1, source_target_pairs={{0,2},{1,7},{2,0},{3,5},{4,6},{5,3},{6,4},{7,1},{8,10},{9,15},{10,... | collective-permute-start | bytes 786440 | tf_op jit(solution)/shard_map/ppermute | solution.py:56
  22.0 3.3 %collective-permute-done.11 = bf16[8,128,128]{2,1,0:T(8,128)(2,1)S(1)} collective-permute-done((bf16[8,128,128]{2,1,0:T(8,128)(2,1)S(1)}, bf16[8,128,128]{2,1,0:T(8,128)(2,1)S(1)}, u32[]{:S(2)}, u32[]{:S(2)}) %collective-permute-start.11) | collective-permute-done | bytes 262176 | tf_op jit(solution)/shard_map/ppermute | solution.py:56
  25.3 0.6 collective-permute-start.4
  25.9 1.7 %collective-permute-done.6 = bf16[8,128,128]{2,1,0:T(8,128)(2,1)S(1)} collective-permute-done((bf16[8,128,128]{2,1,0:T(8,128)(2,1)S(1)}, bf16[8,128,128]{2,1,0:T(8,128)(2,1)S(1)}, u32[]{:S(2)}, u32[]{:S(2)}) %collective-permute-start.6) | collective-permute-done | bytes 262176 | tf_op jit(solution)/shard_map/ppermute | solution.py:56
  27.8 0.6 add_select_fusion.5
  28.5 0.5 slice.102
  29.0 1.3 pad_add_fusion.5.count_ref
  30.3 0.7 add_select_fusion.4
  31.0 2.6 %collective-permute-done.4.rest_1_ = bf16[16,128,128]{2,1,0:T(8,128)(2,1)S(1)} collective-permute-done((bf16[16,128,128]{2,1,0:T(8,128)(2,1)S(1)}, bf16[16,128,128]{2,1,0:T(8,128)(2,1)S(1)}, u32[]{:S(2)}, u32[]{:S(2)}) %collective-permute-start.4) | collective-permute-done | bytes 524320 | tf_op jit(solution)/shard_map/ppermute | solution.py:56
  33.6 2.3 %collective-permute-done.12.rest_7_ = bf16[16,128,128]{2,1,0:T(8,128)(2,1)S(1)} collective-permute-done((bf16[16,128,128]{2,1,0:T(8,128)(2,1)S(1)}, bf16[16,128,128]{2,1,0:T(8,128)(2,1)S(1)}, u32[]{:S(2)}, u32[]{:S(2)}) %collective-permute-start.12) | collective-permute-done | bytes 524320 | tf_op jit(solution)/shard_map/ppermute | solution.py:56
  35.9 3.3 %collective-permute-done.7.rest_3_ = bf16[16,128,128]{2,1,0:T(8,128)(2,1)S(1)} collective-permute-done((bf16[16,128,128]{2,1,0:T(8,128)(2,1)S(1)}, bf16[16,128,128]{2,1,0:T(8,128)(2,1)S(1)}, u32[]{:S(2)}, u32[]{:S(2)}) %collective-permute-start.7) | collective-permute-done | bytes 524320 | tf_op jit(solution)/shard_map/ppermute | solution.py:56
  39.2 6.5 %shard_map.73 = (bf16[16,128,128]{2,1,0:T(8,128)(2,1)S(1)}, bf16[16,128,128]{2,1,0:T(8,128)(2,1)S(1)}, f32[16,128,128]{2,1,0:T(8,128)S(1)}, f32[16,128,128]{2,1,...) custom-call(s32[512]{0:T(512)S(1)} %get-tuple-element.79.row_tile_re, ...), custom_call_target="tpu_custom_call" | custom-call | flops 4294967296 | bytes 27262976 | tf_op jit(solution)/shard_map/pallas_call | solution.py:158
  45.7 2.9 %collective-permute-start.13 = (bf16[16,128,128]{2,1,0:T(8,128)(2,1)S(1)}, bf16[16,128,128]{2,1,0:T(8,128)(2,1)S(1)}, u32[]{:S(2)}, u32[]{:S(2)}) collective-permute-start(bf16[16,128,128]{2,1,0:T(8,128)(2,1)S(1)} %get-tuple-element.36), channel_id=1, source_target_pairs={{0,6},{1,3},{2,4},{3,1},{4,2},{5,7},{6,0},{7,5},{8,14},{9,11},{10,... | collective-permute-start | bytes 1572872 | tf_op jit(solution)/shard_map/ppermute | solution.py:56
  48.7 6.9 %collective-permute-done.13 = bf16[16,128,128]{2,1,0:T(8,128)(2,1)S(1)} collective-permute-done((bf16[16,128,128]{2,1,0:T(8,128)(2,1)S(1)}, bf16[16,128,128]{2,1,0:T(8,128)(2,1)S(1)}, u32[]{:S(2)}, u32[]{:S(2)}) %collective-permute-start.13) | collective-permute-done | bytes 524320 | tf_op jit(solution)/shard_map/ppermute | solution.py:56
  55.7 1.3 collective-permute-start.16
  57.0 0.9 collective-permute-start.14
  58.0 2.4 %collective-permute-start.21 = (bf16[8,128,128]{2,1,0:T(8,128)(2,1)S(1)}, bf16[8,128,128]{2,1,0:T(8,128)(2,1)S(1)}, u32[]{:S(2)}, u32[]{:S(2)}) collective-permute-start(bf16[8,128,128]{2,1,0:T(8,128)(2,1)S(1)} %slice.222), channel_id=1, source_target_pairs={{0,16},{1,49},{2,18},{3,51},{4,20},{5,53},{6,22},{7,55},{8,24},{9,... | collective-permute-start | bytes 786440 | tf_op jit(solution)/shard_map/ppermute | solution.py:56
  60.4 1.5 collective-permute-start.19
  62.2 3.5 %collective-permute-start.17 = (bf16[8,128,128]{2,1,0:T(8,128)(2,1)S(1)}, bf16[8,128,128]{2,1,0:T(8,128)(2,1)S(1)}, u32[]{:S(2)}, u32[]{:S(2)}) collective-permute-start(bf16[8,128,128]{2,1,0:T(8,128)(2,1)S(1)} %fusion.14), channel_id=1, source_target_pairs={{0,8},{1,9},{2,10},{3,11},{4,12},{5,13},{6,14},{7,15},{8,0},{9,1},... | collective-permute-start | bytes 786440 | tf_op jit(solution)/shard_map/ppermute | solution.py:56
  65.8 3.2 %collective-permute-start.22 = (bf16[8,128,128]{2,1,0:T(8,128)(2,1)S(1)}, bf16[8,128,128]{2,1,0:T(8,128)(2,1)S(1)}, u32[]{:S(2)}, u32[]{:S(2)}) collective-permute-start(bf16[8,128,128]{2,1,0:T(8,128)(2,1)S(1)} %fusion.11), channel_id=1, source_target_pairs={{0,64},{1,65},{2,66},{3,67},{4,68},{5,69},{6,70},{7,71},{8,72},{9,... | collective-permute-start | bytes 786440 | tf_op jit(solution)/shard_map/ppermute | solution.py:56
  69.1 2.0 %collective-permute-start.15 = (bf16[8,128,128]{2,1,0:T(8,128)(2,1)S(1)}, bf16[8,128,128]{2,1,0:T(8,128)(2,1)S(1)}, u32[]{:S(2)}, u32[]{:S(2)}) collective-permute-start(bf16[8,128,128]{2,1,0:T(8,128)(2,1)S(1)} %slice.225), channel_id=1, source_target_pairs={{0,2},{1,7},{2,0},{3,5},{4,6},{5,3},{6,4},{7,1},{8,10},{9,15},{10,... | collective-permute-start | bytes 786440 | tf_op jit(solution)/shard_map/ppermute | solution.py:56
  71.2 2.8 %collective-permute-start.20 = (bf16[8,128,128]{2,1,0:T(8,128)(2,1)S(1)}, bf16[8,128,128]{2,1,0:T(8,128)(2,1)S(1)}, u32[]{:S(2)}, u32[]{:S(2)}) collective-permute-start(bf16[8,128,128]{2,1,0:T(8,128)(2,1)S(1)} %slice.223), channel_id=1, source_target_pairs={{0,16},{1,49},{2,18},{3,51},{4,20},{5,53},{6,22},{7,55},{8,24},{9,... | collective-permute-start | bytes 786440 | tf_op jit(solution)/shard_map/ppermute | solution.py:56
  75.3 0.6 collective-permute-done.22
  75.9 4.3 %collective-permute-done.20 = bf16[8,128,128]{2,1,0:T(8,128)(2,1)S(1)} collective-permute-done((bf16[8,128,128]{2,1,0:T(8,128)(2,1)S(1)}, bf16[8,128,128]{2,1,0:T(8,128)(2,1)S(1)}, u32[]{:S(2)}, u32[]{:S(2)}) %collective-permute-start.20) | collective-permute-done | bytes 262176 | tf_op jit(solution)/shard_map/ppermute | solution.py:56
  80.5 2.8 %collective-permute-start.30 = (bf16[8,128,128]{2,1,0:T(8,128)(2,1)S(1)}, bf16[8,128,128]{2,1,0:T(8,128)(2,1)S(1)}, u32[]{:S(2)}, u32[]{:S(2)}) collective-permute-start(bf16[8,128,128]{2,1,0:T(8,128)(2,1)S(1)} %get-tuple-element.59), channel_id=1, source_target_pairs={{0,64},{1,65},{2,66},{3,67},{4,68},{5,69},{6,70},{7,71},{8,72},{9,... | collective-permute-start | bytes 786440 | tf_op jit(solution)/shard_map/ppermute | solution.py:56
  83.3 2.8 %collective-permute-start.25 = (bf16[8,128,128]{2,1,0:T(8,128)(2,1)S(1)}, bf16[8,128,128]{2,1,0:T(8,128)(2,1)S(1)}, u32[]{:S(2)}, u32[]{:S(2)}) collective-permute-start(bf16[8,128,128]{2,1,0:T(8,128)(2,1)S(1)} %get-tuple-element.59), channel_id=1, source_target_pairs={{0,8},{1,9},{2,10},{3,11},{4,12},{5,13},{6,14},{7,15},{8,0},{9,1},... | collective-permute-start | bytes 786440 | tf_op jit(solution)/shard_map/ppermute | solution.py:56
  86.1 1.2 collective-permute-done.30
  87.3 0.3 collective-permute-start.31
  87.6 1.1 collective-permute-done.28
  88.7 1.4 collective-permute-start.29
  90.1 0.9 collective-permute-start.24
  91.0 3.7 %collective-permute-done.25 = bf16[8,128,128]{2,1,0:T(8,128)(2,1)S(1)} collective-permute-done((bf16[8,128,128]{2,1,0:T(8,128)(2,1)S(1)}, bf16[8,128,128]{2,1,0:T(8,128)(2,1)S(1)}, u32[]{:S(2)}, u32[]{:S(2)}) %collective-permute-start.25) | collective-permute-done | bytes 262176 | tf_op jit(solution)/shard_map/ppermute | solution.py:56
  94.9 2.5 %collective-permute-start.32 = (bf16[16,128,128]{2,1,0:T(8,128)(2,1)S(1)}, bf16[16,128,128]{2,1,0:T(8,128)(2,1)S(1)}, u32[]{:S(2)}, u32[]{:S(2)}) collective-permute-start(bf16[16,128,128]{2,1,0:T(8,128)(2,1)S(1)} %constant_dynamic-update-slice_fusion.6.rest_6_), channel_id=1, source_target_pairs={{0,16},{1,49},{2,18},{3,51},{4,20},{5,53},{6,22},{7,55},{8,24},{9,... | collective-permute-start | bytes 1572872 | tf_op jit(solution)/shard_map/ppermute | solution.py:56
  97.4 2.9 %collective-permute-done.26 = bf16[8,128,128]{2,1,0:T(8,128)(2,1)S(1)} collective-permute-done((bf16[8,128,128]{2,1,0:T(8,128)(2,1)S(1)}, bf16[8,128,128]{2,1,0:T(8,128)(2,1)S(1)}, u32[]{:S(2)}, u32[]{:S(2)}) %collective-permute-start.26) | collective-permute-done | bytes 262176 | tf_op jit(solution)/shard_map/ppermute | solution.py:56
  100.3 3.1 %collective-permute-start.27 = (bf16[16,128,128]{2,1,0:T(8,128)(2,1)S(1)}, bf16[16,128,128]{2,1,0:T(8,128)(2,1)S(1)}, u32[]{:S(2)}, u32[]{:S(2)}) collective-permute-start(bf16[16,128,128]{2,1,0:T(8,128)(2,1)S(1)} %constant_dynamic-update-slice_fusion.4.rest_2_), channel_id=1, source_target_pairs={{0,2},{1,7},{2,0},{3,5},{4,6},{5,3},{6,4},{7,1},{8,10},{9,15},{10,... | collective-permute-start | bytes 1572872 | tf_op jit(solution)/shard_map/ppermute | solution.py:56
  103.4 6.2 %collective-permute-done.32.rest_7_ = bf16[16,128,128]{2,1,0:T(8,128)(2,1)S(1)} collective-permute-done((bf16[16,128,128]{2,1,0:T(8,128)(2,1)S(1)}, bf16[16,128,128]{2,1,0:T(8,128)(2,1)S(1)}, u32[]{:S(2)}, u32[]{:S(2)}) %collective-permute-start.32) | collective-permute-done | bytes 524320 | tf_op jit(solution)/shard_map/ppermute | solution.py:56
  109.6 3.0 %collective-permute-done.27.rest_3_ = bf16[16,128,128]{2,1,0:T(8,128)(2,1)S(1)} collective-permute-done((bf16[16,128,128]{2,1,0:T(8,128)(2,1)S(1)}, bf16[16,128,128]{2,1,0:T(8,128)(2,1)S(1)}, u32[]{:S(2)}, u32[]{:S(2)}) %collective-permute-start.27) | collective-permute-done | bytes 524320 | tf_op jit(solution)/shard_map/ppermute | solution.py:56
  112.6 6.5 %shard_map.74 = (bf16[16,128,128]{2,1,0:T(8,128)(2,1)S(1)}, bf16[16,128,128]{2,1,0:T(8,128)(2,1)S(1)}, f32[16,128,128]{2,1,0:T(8,128)S(1)}, f32[16,128,128]{2,1,...) custom-call(s32[512]{0:T(512)S(1)} %get-tuple-element.77.row_tile_re, ...), custom_call_target="tpu_custom_call" | custom-call | flops 4294967296 | bytes 27262976 | tf_op jit(solution)/shard_map/pallas_call | solution.py:158
  119.1 2.9 %collective-permute-start.33 = (bf16[16,128,128]{2,1,0:T(8,128)(2,1)S(1)}, bf16[16,128,128]{2,1,0:T(8,128)(2,1)S(1)}, u32[]{:S(2)}, u32[]{:S(2)}) collective-permute-start(bf16[16,128,128]{2,1,0:T(8,128)(2,1)S(1)} %get-tuple-element.48), channel_id=1, source_target_pairs={{0,2},{1,7},{2,0},{3,5},{4,6},{5,3},{6,4},{7,1},{8,10},{9,15},{10,... | collective-permute-start | bytes 1572872 | tf_op jit(solution)/shard_map/ppermute | solution.py:56
  122.0 2.7 %collective-permute-start.38 = (bf16[16,128,128]{2,1,0:T(8,128)(2,1)S(1)}, bf16[16,128,128]{2,1,0:T(8,128)(2,1)S(1)}, u32[]{:S(2)}, u32[]{:S(2)}) collective-permute-start(bf16[16,128,128]{2,1,0:T(8,128)(2,1)S(1)} %get-tuple-element.54), channel_id=1, source_target_pairs={{0,16},{1,49},{2,18},{3,51},{4,20},{5,53},{6,22},{7,55},{8,24},{9,... | collective-permute-start | bytes 1572872 | tf_op jit(solution)/shard_map/ppermute | solution.py:56
  124.7 3.9 %collective-permute-done.33 = bf16[16,128,128]{2,1,0:T(8,128)(2,1)S(1)} collective-permute-done((bf16[16,128,128]{2,1,0:T(8,128)(2,1)S(1)}, bf16[16,128,128]{2,1,0:T(8,128)(2,1)S(1)}, u32[]{:S(2)}, u32[]{:S(2)}) %collective-permute-start.33) | collective-permute-done | bytes 524320 | tf_op jit(solution)/shard_map/ppermute | solution.py:56
  128.8 0.8 collective-permute-start.36
  129.6 2.1 %collective-permute-start.34 = (bf16[16,128,128]{2,1,0:T(8,128)(2,1)S(1)}, bf16[16,128,128]{2,1,0:T(8,128)(2,1)S(1)}, u32[]{:S(2)}, u32[]{:S(2)}) collective-permute-start(bf16[16,128,128]{2,1,0:T(8,128)(2,1)S(1)} %get-tuple-element.50), channel_id=1, source_target_pairs={{0,2},{1,7},{2,0},{3,5},{4,6},{5,3},{6,4},{7,1},{8,10},{9,15},{10,... | collective-permute-start | bytes 1572872 | tf_op jit(solution)/shard_map/ppermute | solution.py:56
  131.8 0.4 collective-permute-start.41
  132.2 2.4 %collective-permute-start.39 = (bf16[16,128,128]{2,1,0:T(8,128)(2,1)S(1)}, bf16[16,128,128]{2,1,0:T(8,128)(2,1)S(1)}, u32[]{:S(2)}, u32[]{:S(2)}) collective-permute-start(bf16[16,128,128]{2,1,0:T(8,128)(2,1)S(1)} %get-tuple-element.56), channel_id=1, source_target_pairs={{0,16},{1,49},{2,18},{3,51},{4,20},{5,53},{6,22},{7,55},{8,24},{9,... | collective-permute-start | bytes 1572872 | tf_op jit(solution)/shard_map/ppermute | solution.py:56
  134.6 1.0 collective-permute-done.36
  135.7 3.8 %collective-permute-start.37 = (bf16[8,128,128]{2,1,0:T(8,128)(2,1)S(1)}, bf16[8,128,128]{2,1,0:T(8,128)(2,1)S(1)}, u32[]{:S(2)}, u32[]{:S(2)}) collective-permute-start(bf16[8,128,128]{2,1,0:T(8,128)(2,1)S(1)} %fusion.9), channel_id=1, source_target_pairs={{0,8},{1,9},{2,10},{3,11},{4,12},{5,13},{6,14},{7,15},{8,0},{9,1},... | collective-permute-start | bytes 786440 | tf_op jit(solution)/shard_map/ppermute | solution.py:56
  139.4 0.4 collective-permute-done.41
  139.9 3.9 %collective-permute-start.42 = (bf16[8,128,128]{2,1,0:T(8,128)(2,1)S(1)}, bf16[8,128,128]{2,1,0:T(8,128)(2,1)S(1)}, u32[]{:S(2)}, u32[]{:S(2)}) collective-permute-start(bf16[8,128,128]{2,1,0:T(8,128)(2,1)S(1)} %fusion.6), channel_id=1, source_target_pairs={{0,64},{1,65},{2,66},{3,67},{4,68},{5,69},{6,70},{7,71},{8,72},{9,... | collective-permute-start | bytes 786440 | tf_op jit(solution)/shard_map/ppermute | solution.py:56
  144.3 5.9 %collective-permute-done.42 = bf16[8,128,128]{2,1,0:T(8,128)(2,1)S(1)} collective-permute-done((bf16[8,128,128]{2,1,0:T(8,128)(2,1)S(1)}, bf16[8,128,128]{2,1,0:T(8,128)(2,1)S(1)}, u32[]{:S(2)}, u32[]{:S(2)}) %collective-permute-start.42) | collective-permute-done | bytes 262176 | tf_op jit(solution)/shard_map/ppermute | solution.py:56
  150.2 2.1 %collective-permute-done.35 = bf16[8,128,128]{2,1,0:T(8,128)(2,1)S(1)} collective-permute-done((bf16[8,128,128]{2,1,0:T(8,128)(2,1)S(1)}, bf16[8,128,128]{2,1,0:T(8,128)(2,1)S(1)}, u32[]{:S(2)}, u32[]{:S(2)}) %collective-permute-start.35) | collective-permute-done | bytes 262176 | tf_op jit(solution)/shard_map/ppermute | solution.py:56
  152.8 11.4 %collective-permute-start.43 = (f32[512,128]{1,0:T(8,128)S(1)}, f32[512,128]{1,0:T(8,128)S(1)}, u32[]{:S(2)}, u32[]{:S(2)}) collective-permute-start(f32[512,128]{1,0:T(8,128)S(1)} %get-tuple-element.62), channel_id=1, source_target_pairs={{0,1},{1,0},{2,3},{3,2},{4,5},{5,4},{6,7},{7,6},{8,9},{9,8},{10,11... | collective-permute-start | bytes 786440 | tf_op jit(solution)/shard_map/ppermute | solution.py:56
  164.2 1.2 collective-permute-done.43
  165.3 0.8 maximum_select_fusion
  (72 shorter events, 3.9 us)
Async XLA Ops:
  1.0 2.9 %collective-permute-start = (bf16[512,128]{1,0:T(8,128)(2,1)S(1)}, bf16[512,128]{1,0:T(8,128)(2,1)S(1)}, u32[]{:S(2)}, u32[]{:S(2)}) collective-permute-start(bf16[512,128]{1,0:T(8,128)(2,1)S(1)} %get-tuple-element.68), channel_id=1, source_target_pairs={{0,1},{1,0},{2,3},{3,2},{4,5},{5,4},{6,7},{7,6},{8,9},{9,8},{10,11... | collective-permute-start | bytes 393224 | tf_op jit(solution)/shard_map/ppermute | solution.py:56
  3.9 35.4 %collective-permute-start.2 = (bf16[256,128,128]{2,1,0:T(8,128)(2,1)}, bf16[256,128,128]{2,1,0:T(8,128)(2,1)}, u32[]{:S(2)}, u32[]{:S(2)}) collective-permute-start(bf16[256,128,128]{2,1,0:T(8,128)(2,1)} %bitcast.14), channel_id=1, source_target_pairs={{0,1},{1,0},{2,3},{3,2},{4,5},{5,4},{6,7},{7,6},{8,9},{9,8},{10,11... | collective-permute-start | bytes 25165832 | tf_op jit(solution)/shard_map/ppermute | solution.py:56
  4.0 10.3 %collective-permute-start.10 = (bf16[8,128,128]{2,1,0:T(8,128)(2,1)S(1)}, bf16[8,128,128]{2,1,0:T(8,128)(2,1)S(1)}, u32[]{:S(2)}, u32[]{:S(2)}) collective-permute-start(bf16[8,128,128]{2,1,0:T(8,128)(2,1)S(1)} %bitcast.17), channel_id=1, source_target_pairs={{0,64},{1,65},{2,66},{3,67},{4,68},{5,69},{6,70},{7,71},{8,72},{9,... | collective-permute-start | bytes 786440 | tf_op jit(solution)/shard_map/ppermute | solution.py:56
  7.1 7.5 %collective-permute-start.8 = (bf16[8,128,128]{2,1,0:T(8,128)(2,1)S(1)}, bf16[8,128,128]{2,1,0:T(8,128)(2,1)S(1)}, u32[]{:S(2)}, u32[]{:S(2)}) collective-permute-start(bf16[8,128,128]{2,1,0:T(8,128)(2,1)S(1)} %bitcast.18), channel_id=1, source_target_pairs={{0,16},{1,49},{2,18},{3,51},{4,20},{5,53},{6,22},{7,55},{8,24},{9,... | collective-permute-start | bytes 786440 | tf_op jit(solution)/shard_map/ppermute | solution.py:56
  10.9 8.3 %collective-permute-start.3 = (bf16[8,128,128]{2,1,0:T(8,128)(2,1)S(1)}, bf16[8,128,128]{2,1,0:T(8,128)(2,1)S(1)}, u32[]{:S(2)}, u32[]{:S(2)}) collective-permute-start(bf16[8,128,128]{2,1,0:T(8,128)(2,1)S(1)} %bitcast.19), channel_id=1, source_target_pairs={{0,2},{1,7},{2,0},{3,5},{4,6},{5,3},{6,4},{7,1},{8,10},{9,15},{10,... | collective-permute-start | bytes 786440 | tf_op jit(solution)/shard_map/ppermute | solution.py:56
  13.4 6.7 %collective-permute-start.5 = (bf16[8,128,128]{2,1,0:T(8,128)(2,1)S(1)}, bf16[8,128,128]{2,1,0:T(8,128)(2,1)S(1)}, u32[]{:S(2)}, u32[]{:S(2)}) collective-permute-start(bf16[8,128,128]{2,1,0:T(8,128)(2,1)S(1)} %bitcast.20), channel_id=1, source_target_pairs={{0,8},{1,9},{2,10},{3,11},{4,12},{5,13},{6,14},{7,15},{8,0},{9,1},... | collective-permute-start | bytes 786440 | tf_op jit(solution)/shard_map/ppermute | solution.py:56
  14.3 13.4 %collective-permute-start.1 = (s32[640]{0:T(1024)S(1)}, s32[640]{0:T(1024)S(1)}, u32[]{:S(2)}, u32[]{:S(2)}) collective-permute-start(s32[640]{0:T(1024)S(1)} %pad_add_fusion), channel_id=1, source_target_pairs={{0,1},{1,0},{2,3},{3,2},{4,5},{5,4},{6,7},{7,6},{8,9},{9,8},{10,11... | collective-permute-start | bytes 7688 | tf_op jit(solution)/shard_map/ppermute | solution.py:56
  14.6 10.6 %collective-permute-start.11 = (bf16[8,128,128]{2,1,0:T(8,128)(2,1)S(1)}, bf16[8,128,128]{2,1,0:T(8,128)(2,1)S(1)}, u32[]{:S(2)}, u32[]{:S(2)}) collective-permute-start(bf16[8,128,128]{2,1,0:T(8,128)(2,1)S(1)} %collective-permute-done.10), channel_id=1, source_target_pairs={{0,16},{1,49},{2,18},{3,51},{4,20},{5,53},{6,22},{7,55},{8,24},{9,... | collective-permute-start | bytes 786440 | tf_op jit(solution)/shard_map/ppermute | solution.py:56
  19.2 11.8 %collective-permute-start.9 = (bf16[16,128,128]{2,1,0:T(8,128)(2,1)S(1)}, bf16[16,128,128]{2,1,0:T(8,128)(2,1)S(1)}, u32[]{:S(2)}, u32[]{:S(2)}) collective-permute-start(bf16[16,128,128]{2,1,0:T(8,128)(2,1)S(1)} %get-tuple-element.65.rest_4_), channel_id=1, source_target_pairs={{0,48},{1,17},{2,50},{3,19},{4,52},{5,21},{6,54},{7,23},{8,56},{9,... | collective-permute-start | bytes 1572872 | tf_op jit(solution)/shard_map/ppermute | solution.py:56
  20.1 7.5 %collective-permute-start.6 = (bf16[8,128,128]{2,1,0:T(8,128)(2,1)S(1)}, bf16[8,128,128]{2,1,0:T(8,128)(2,1)S(1)}, u32[]{:S(2)}, u32[]{:S(2)}) collective-permute-start(bf16[8,128,128]{2,1,0:T(8,128)(2,1)S(1)} %collective-permute-done.5), channel_id=1, source_target_pairs={{0,2},{1,7},{2,0},{3,5},{4,6},{5,3},{6,4},{7,1},{8,10},{9,15},{10,... | collective-permute-start | bytes 786440 | tf_op jit(solution)/shard_map/ppermute | solution.py:56
  25.3 8.3 %collective-permute-start.4 = (bf16[16,128,128]{2,1,0:T(8,128)(2,1)S(1)}, bf16[16,128,128]{2,1,0:T(8,128)(2,1)S(1)}, u32[]{:S(2)}, u32[]{:S(2)}) collective-permute-start(bf16[16,128,128]{2,1,0:T(8,128)(2,1)S(1)} %get-tuple-element.66.rest_0_), channel_id=1, source_target_pairs={{0,6},{1,3},{2,4},{3,1},{4,2},{5,7},{6,0},{7,5},{8,14},{9,11},{10,... | collective-permute-start | bytes 1572872 | tf_op jit(solution)/shard_map/ppermute | solution.py:56
  27.6 8.3 %collective-permute-start.12 = (bf16[16,128,128]{2,1,0:T(8,128)(2,1)S(1)}, bf16[16,128,128]{2,1,0:T(8,128)(2,1)S(1)}, u32[]{:S(2)}, u32[]{:S(2)}) collective-permute-start(bf16[16,128,128]{2,1,0:T(8,128)(2,1)S(1)} %constant_dynamic-update-slice_fusion.2.rest_6_), channel_id=1, source_target_pairs={{0,48},{1,17},{2,50},{3,19},{4,52},{5,21},{6,54},{7,23},{8,56},{9,... | collective-permute-start | bytes 1572872 | tf_op jit(solution)/shard_map/ppermute | solution.py:56
  27.8 11.5 %collective-permute-start.7 = (bf16[16,128,128]{2,1,0:T(8,128)(2,1)S(1)}, bf16[16,128,128]{2,1,0:T(8,128)(2,1)S(1)}, u32[]{:S(2)}, u32[]{:S(2)}) collective-permute-start(bf16[16,128,128]{2,1,0:T(8,128)(2,1)S(1)} %constant_dynamic-update-slice_fusion.rest_2_), channel_id=1, source_target_pairs={{0,6},{1,3},{2,4},{3,1},{4,2},{5,7},{6,0},{7,5},{8,14},{9,11},{10,... | collective-permute-start | bytes 1572872 | tf_op jit(solution)/shard_map/ppermute | solution.py:56
  45.7 9.8 %collective-permute-start.13 = (bf16[16,128,128]{2,1,0:T(8,128)(2,1)S(1)}, bf16[16,128,128]{2,1,0:T(8,128)(2,1)S(1)}, u32[]{:S(2)}, u32[]{:S(2)}) collective-permute-start(bf16[16,128,128]{2,1,0:T(8,128)(2,1)S(1)} %get-tuple-element.36), channel_id=1, source_target_pairs={{0,6},{1,3},{2,4},{3,1},{4,2},{5,7},{6,0},{7,5},{8,14},{9,11},{10,... | collective-permute-start | bytes 1572872 | tf_op jit(solution)/shard_map/ppermute | solution.py:56
  48.6 9.2 %collective-permute-start.18 = (bf16[16,128,128]{2,1,0:T(8,128)(2,1)S(1)}, bf16[16,128,128]{2,1,0:T(8,128)(2,1)S(1)}, u32[]{:S(2)}, u32[]{:S(2)}) collective-permute-start(bf16[16,128,128]{2,1,0:T(8,128)(2,1)S(1)} %get-tuple-element.42), channel_id=1, source_target_pairs={{0,48},{1,17},{2,50},{3,19},{4,52},{5,21},{6,54},{7,23},{8,56},{9,... | collective-permute-start | bytes 1572872 | tf_op jit(solution)/shard_map/ppermute | solution.py:56
  55.7 6.5 %collective-permute-start.16 = (bf16[8,128,128]{2,1,0:T(8,128)(2,1)S(1)}, bf16[8,128,128]{2,1,0:T(8,128)(2,1)S(1)}, u32[]{:S(2)}, u32[]{:S(2)}) collective-permute-start(bf16[8,128,128]{2,1,0:T(8,128)(2,1)S(1)} %slice.224), channel_id=1, source_target_pairs={{0,2},{1,7},{2,0},{3,5},{4,6},{5,3},{6,4},{7,1},{8,10},{9,15},{10,... | collective-permute-start | bytes 786440 | tf_op jit(solution)/shard_map/ppermute | solution.py:56
  57.0 12.0 %collective-permute-start.14 = (bf16[16,128,128]{2,1,0:T(8,128)(2,1)S(1)}, bf16[16,128,128]{2,1,0:T(8,128)(2,1)S(1)}, u32[]{:S(2)}, u32[]{:S(2)}) collective-permute-start(bf16[16,128,128]{2,1,0:T(8,128)(2,1)S(1)} %get-tuple-element.38), channel_id=1, source_target_pairs={{0,6},{1,3},{2,4},{3,1},{4,2},{5,7},{6,0},{7,5},{8,14},{9,11},{10,... | collective-permute-start | bytes 1572872 | tf_op jit(solution)/shard_map/ppermute | solution.py:56
  58.0 7.8 %collective-permute-start.21 = (bf16[8,128,128]{2,1,0:T(8,128)(2,1)S(1)}, bf16[8,128,128]{2,1,0:T(8,128)(2,1)S(1)}, u32[]{:S(2)}, u32[]{:S(2)}) collective-permute-start(bf16[8,128,128]{2,1,0:T(8,128)(2,1)S(1)} %slice.222), channel_id=1, source_target_pairs={{0,16},{1,49},{2,18},{3,51},{4,20},{5,53},{6,22},{7,55},{8,24},{9,... | collective-permute-start | bytes 786440 | tf_op jit(solution)/shard_map/ppermute | solution.py:56
  60.4 10.7 %collective-permute-start.19 = (bf16[16,128,128]{2,1,0:T(8,128)(2,1)S(1)}, bf16[16,128,128]{2,1,0:T(8,128)(2,1)S(1)}, u32[]{:S(2)}, u32[]{:S(2)}) collective-permute-start(bf16[16,128,128]{2,1,0:T(8,128)(2,1)S(1)} %get-tuple-element.44), channel_id=1, source_target_pairs={{0,48},{1,17},{2,50},{3,19},{4,52},{5,21},{6,54},{7,23},{8,56},{9,... | collective-permute-start | bytes 1572872 | tf_op jit(solution)/shard_map/ppermute | solution.py:56
  62.2 13.1 %collective-permute-start.17 = (bf16[8,128,128]{2,1,0:T(8,128)(2,1)S(1)}, bf16[8,128,128]{2,1,0:T(8,128)(2,1)S(1)}, u32[]{:S(2)}, u32[]{:S(2)}) collective-permute-start(bf16[8,128,128]{2,1,0:T(8,128)(2,1)S(1)} %fusion.14), channel_id=1, source_target_pairs={{0,8},{1,9},{2,10},{3,11},{4,12},{5,13},{6,14},{7,15},{8,0},{9,1},... | collective-permute-start | bytes 786440 | tf_op jit(solution)/shard_map/ppermute | solution.py:56
  65.8 10.1 %collective-permute-start.22 = (bf16[8,128,128]{2,1,0:T(8,128)(2,1)S(1)}, bf16[8,128,128]{2,1,0:T(8,128)(2,1)S(1)}, u32[]{:S(2)}, u32[]{:S(2)}) collective-permute-start(bf16[8,128,128]{2,1,0:T(8,128)(2,1)S(1)} %fusion.11), channel_id=1, source_target_pairs={{0,64},{1,65},{2,66},{3,67},{4,68},{5,69},{6,70},{7,71},{8,72},{9,... | collective-permute-start | bytes 786440 | tf_op jit(solution)/shard_map/ppermute | solution.py:56
  69.1 6.8 %collective-permute-start.15 = (bf16[8,128,128]{2,1,0:T(8,128)(2,1)S(1)}, bf16[8,128,128]{2,1,0:T(8,128)(2,1)S(1)}, u32[]{:S(2)}, u32[]{:S(2)}) collective-permute-start(bf16[8,128,128]{2,1,0:T(8,128)(2,1)S(1)} %slice.225), channel_id=1, source_target_pairs={{0,2},{1,7},{2,0},{3,5},{4,6},{5,3},{6,4},{7,1},{8,10},{9,15},{10,... | collective-permute-start | bytes 786440 | tf_op jit(solution)/shard_map/ppermute | solution.py:56
  71.2 9.0 %collective-permute-start.20 = (bf16[8,128,128]{2,1,0:T(8,128)(2,1)S(1)}, bf16[8,128,128]{2,1,0:T(8,128)(2,1)S(1)}, u32[]{:S(2)}, u32[]{:S(2)}) collective-permute-start(bf16[8,128,128]{2,1,0:T(8,128)(2,1)S(1)} %slice.223), channel_id=1, source_target_pairs={{0,16},{1,49},{2,18},{3,51},{4,20},{5,53},{6,22},{7,55},{8,24},{9,... | collective-permute-start | bytes 786440 | tf_op jit(solution)/shard_map/ppermute | solution.py:56
  80.5 6.8 %collective-permute-start.30 = (bf16[8,128,128]{2,1,0:T(8,128)(2,1)S(1)}, bf16[8,128,128]{2,1,0:T(8,128)(2,1)S(1)}, u32[]{:S(2)}, u32[]{:S(2)}) collective-permute-start(bf16[8,128,128]{2,1,0:T(8,128)(2,1)S(1)} %get-tuple-element.59), channel_id=1, source_target_pairs={{0,64},{1,65},{2,66},{3,67},{4,68},{5,69},{6,70},{7,71},{8,72},{9,... | collective-permute-start | bytes 786440 | tf_op jit(solution)/shard_map/ppermute | solution.py:56
  83.3 5.3 %collective-permute-start.28 = (bf16[8,128,128]{2,1,0:T(8,128)(2,1)S(1)}, bf16[8,128,128]{2,1,0:T(8,128)(2,1)S(1)}, u32[]{:S(2)}, u32[]{:S(2)}) collective-permute-start(bf16[8,128,128]{2,1,0:T(8,128)(2,1)S(1)} %get-tuple-element.59), channel_id=1, source_target_pairs={{0,48},{1,17},{2,50},{3,19},{4,52},{5,21},{6,54},{7,23},{8,56},{9,... | collective-permute-start | bytes 786440 | tf_op jit(solution)/shard_map/ppermute | solution.py:56
  83.3 5.3 %collective-permute-start.23 = (bf16[8,128,128]{2,1,0:T(8,128)(2,1)S(1)}, bf16[8,128,128]{2,1,0:T(8,128)(2,1)S(1)}, u32[]{:S(2)}, u32[]{:S(2)}) collective-permute-start(bf16[8,128,128]{2,1,0:T(8,128)(2,1)S(1)} %get-tuple-element.59), channel_id=1, source_target_pairs={{0,6},{1,3},{2,4},{3,1},{4,2},{5,7},{6,0},{7,5},{8,14},{9,11},{10,... | collective-permute-start | bytes 786440 | tf_op jit(solution)/shard_map/ppermute | solution.py:56
  83.3 11.4 %collective-permute-start.25 = (bf16[8,128,128]{2,1,0:T(8,128)(2,1)S(1)}, bf16[8,128,128]{2,1,0:T(8,128)(2,1)S(1)}, u32[]{:S(2)}, u32[]{:S(2)}) collective-permute-start(bf16[8,128,128]{2,1,0:T(8,128)(2,1)S(1)} %get-tuple-element.59), channel_id=1, source_target_pairs={{0,8},{1,9},{2,10},{3,11},{4,12},{5,13},{6,14},{7,15},{8,0},{9,1},... | collective-permute-start | bytes 786440 | tf_op jit(solution)/shard_map/ppermute | solution.py:56
  87.3 7.5 %collective-permute-start.31 = (bf16[8,128,128]{2,1,0:T(8,128)(2,1)S(1)}, bf16[8,128,128]{2,1,0:T(8,128)(2,1)S(1)}, u32[]{:S(2)}, u32[]{:S(2)}) collective-permute-start(bf16[8,128,128]{2,1,0:T(8,128)(2,1)S(1)} %collective-permute-done.30), channel_id=1, source_target_pairs={{0,48},{1,17},{2,50},{3,19},{4,52},{5,21},{6,54},{7,23},{8,56},{9,... | collective-permute-start | bytes 786440 | tf_op jit(solution)/shard_map/ppermute | solution.py:56
  88.7 14.7 %collective-permute-start.29 = (bf16[16,128,128]{2,1,0:T(8,128)(2,1)S(1)}, bf16[16,128,128]{2,1,0:T(8,128)(2,1)S(1)}, u32[]{:S(2)}, u32[]{:S(2)}) collective-permute-start(bf16[16,128,128]{2,1,0:T(8,128)(2,1)S(1)} %get-tuple-element.63.rest_4_), channel_id=1, source_target_pairs={{0,16},{1,49},{2,18},{3,51},{4,20},{5,53},{6,22},{7,55},{8,24},{9,... | collective-permute-start | bytes 1572872 | tf_op jit(solution)/shard_map/ppermute | solution.py:56
  90.1 13.3 %collective-permute-start.24 = (bf16[16,128,128]{2,1,0:T(8,128)(2,1)S(1)}, bf16[16,128,128]{2,1,0:T(8,128)(2,1)S(1)}, u32[]{:S(2)}, u32[]{:S(2)}) collective-permute-start(bf16[16,128,128]{2,1,0:T(8,128)(2,1)S(1)} %get-tuple-element.64.rest_0_), channel_id=1, source_target_pairs={{0,2},{1,7},{2,0},{3,5},{4,6},{5,3},{6,4},{7,1},{8,10},{9,15},{10,... | collective-permute-start | bytes 1572872 | tf_op jit(solution)/shard_map/ppermute | solution.py:56
  94.8 5.5 %collective-permute-start.26 = (bf16[8,128,128]{2,1,0:T(8,128)(2,1)S(1)}, bf16[8,128,128]{2,1,0:T(8,128)(2,1)S(1)}, u32[]{:S(2)}, u32[]{:S(2)}) collective-permute-start(bf16[8,128,128]{2,1,0:T(8,128)(2,1)S(1)} %collective-permute-done.25), channel_id=1, source_target_pairs={{0,6},{1,3},{2,4},{3,1},{4,2},{5,7},{6,0},{7,5},{8,14},{9,11},{10,... | collective-permute-start | bytes 786440 | tf_op jit(solution)/shard_map/ppermute | solution.py:56
  94.9 14.7 %collective-permute-start.32 = (bf16[16,128,128]{2,1,0:T(8,128)(2,1)S(1)}, bf16[16,128,128]{2,1,0:T(8,128)(2,1)S(1)}, u32[]{:S(2)}, u32[]{:S(2)}) collective-permute-start(bf16[16,128,128]{2,1,0:T(8,128)(2,1)S(1)} %constant_dynamic-update-slice_fusion.6.rest_6_), channel_id=1, source_target_pairs={{0,16},{1,49},{2,18},{3,51},{4,20},{5,53},{6,22},{7,55},{8,24},{9,... | collective-permute-start | bytes 1572872 | tf_op jit(solution)/shard_map/ppermute | solution.py:56
  100.3 12.3 %collective-permute-start.27 = (bf16[16,128,128]{2,1,0:T(8,128)(2,1)S(1)}, bf16[16,128,128]{2,1,0:T(8,128)(2,1)S(1)}, u32[]{:S(2)}, u32[]{:S(2)}) collective-permute-start(bf16[16,128,128]{2,1,0:T(8,128)(2,1)S(1)} %constant_dynamic-update-slice_fusion.4.rest_2_), channel_id=1, source_target_pairs={{0,2},{1,7},{2,0},{3,5},{4,6},{5,3},{6,4},{7,1},{8,10},{9,15},{10,... | collective-permute-start | bytes 1572872 | tf_op jit(solution)/shard_map/ppermute | solution.py:56
  119.1 9.5 %collective-permute-start.33 = (bf16[16,128,128]{2,1,0:T(8,128)(2,1)S(1)}, bf16[16,128,128]{2,1,0:T(8,128)(2,1)S(1)}, u32[]{:S(2)}, u32[]{:S(2)}) collective-permute-start(bf16[16,128,128]{2,1,0:T(8,128)(2,1)S(1)} %get-tuple-element.48), channel_id=1, source_target_pairs={{0,2},{1,7},{2,0},{3,5},{4,6},{5,3},{6,4},{7,1},{8,10},{9,15},{10,... | collective-permute-start | bytes 1572872 | tf_op jit(solution)/shard_map/ppermute | solution.py:56
  122.0 9.6 %collective-permute-start.38 = (bf16[16,128,128]{2,1,0:T(8,128)(2,1)S(1)}, bf16[16,128,128]{2,1,0:T(8,128)(2,1)S(1)}, u32[]{:S(2)}, u32[]{:S(2)}) collective-permute-start(bf16[16,128,128]{2,1,0:T(8,128)(2,1)S(1)} %get-tuple-element.54), channel_id=1, source_target_pairs={{0,16},{1,49},{2,18},{3,51},{4,20},{5,53},{6,22},{7,55},{8,24},{9,... | collective-permute-start | bytes 1572872 | tf_op jit(solution)/shard_map/ppermute | solution.py:56
  128.8 6.8 %collective-permute-start.36 = (bf16[8,128,128]{2,1,0:T(8,128)(2,1)S(1)}, bf16[8,128,128]{2,1,0:T(8,128)(2,1)S(1)}, u32[]{:S(2)}, u32[]{:S(2)}) collective-permute-start(bf16[8,128,128]{2,1,0:T(8,128)(2,1)S(1)} %slice.220), channel_id=1, source_target_pairs={{0,6},{1,3},{2,4},{3,1},{4,2},{5,7},{6,0},{7,5},{8,14},{9,11},{10,... | collective-permute-start | bytes 786440 | tf_op jit(solution)/shard_map/ppermute | solution.py:56
  129.6 14.2 %collective-permute-start.34 = (bf16[16,128,128]{2,1,0:T(8,128)(2,1)S(1)}, bf16[16,128,128]{2,1,0:T(8,128)(2,1)S(1)}, u32[]{:S(2)}, u32[]{:S(2)}) collective-permute-start(bf16[16,128,128]{2,1,0:T(8,128)(2,1)S(1)} %get-tuple-element.50), channel_id=1, source_target_pairs={{0,2},{1,7},{2,0},{3,5},{4,6},{5,3},{6,4},{7,1},{8,10},{9,15},{10,... | collective-permute-start | bytes 1572872 | tf_op jit(solution)/shard_map/ppermute | solution.py:56
  131.8 8.0 %collective-permute-start.41 = (bf16[8,128,128]{2,1,0:T(8,128)(2,1)S(1)}, bf16[8,128,128]{2,1,0:T(8,128)(2,1)S(1)}, u32[]{:S(2)}, u32[]{:S(2)}) collective-permute-start(bf16[8,128,128]{2,1,0:T(8,128)(2,1)S(1)} %slice.218), channel_id=1, source_target_pairs={{0,48},{1,17},{2,50},{3,19},{4,52},{5,21},{6,54},{7,23},{8,56},{9,... | collective-permute-start | bytes 786440 | tf_op jit(solution)/shard_map/ppermute | solution.py:56
  132.2 11.9 %collective-permute-start.39 = (bf16[16,128,128]{2,1,0:T(8,128)(2,1)S(1)}, bf16[16,128,128]{2,1,0:T(8,128)(2,1)S(1)}, u32[]{:S(2)}, u32[]{:S(2)}) collective-permute-start(bf16[16,128,128]{2,1,0:T(8,128)(2,1)S(1)} %get-tuple-element.56), channel_id=1, source_target_pairs={{0,16},{1,49},{2,18},{3,51},{4,20},{5,53},{6,22},{7,55},{8,24},{9,... | collective-permute-start | bytes 1572872 | tf_op jit(solution)/shard_map/ppermute | solution.py:56
  135.7 8.7 %collective-permute-start.37 = (bf16[8,128,128]{2,1,0:T(8,128)(2,1)S(1)}, bf16[8,128,128]{2,1,0:T(8,128)(2,1)S(1)}, u32[]{:S(2)}, u32[]{:S(2)}) collective-permute-start(bf16[8,128,128]{2,1,0:T(8,128)(2,1)S(1)} %fusion.9), channel_id=1, source_target_pairs={{0,8},{1,9},{2,10},{3,11},{4,12},{5,13},{6,14},{7,15},{8,0},{9,1},... | collective-permute-start | bytes 786440 | tf_op jit(solution)/shard_map/ppermute | solution.py:56
  139.9 10.3 %collective-permute-start.42 = (bf16[8,128,128]{2,1,0:T(8,128)(2,1)S(1)}, bf16[8,128,128]{2,1,0:T(8,128)(2,1)S(1)}, u32[]{:S(2)}, u32[]{:S(2)}) collective-permute-start(bf16[8,128,128]{2,1,0:T(8,128)(2,1)S(1)} %fusion.6), channel_id=1, source_target_pairs={{0,64},{1,65},{2,66},{3,67},{4,68},{5,69},{6,70},{7,71},{8,72},{9,... | collective-permute-start | bytes 786440 | tf_op jit(solution)/shard_map/ppermute | solution.py:56
  144.0 8.4 %collective-permute-start.35 = (bf16[8,128,128]{2,1,0:T(8,128)(2,1)S(1)}, bf16[8,128,128]{2,1,0:T(8,128)(2,1)S(1)}, u32[]{:S(2)}, u32[]{:S(2)}) collective-permute-start(bf16[8,128,128]{2,1,0:T(8,128)(2,1)S(1)} %slice.221), channel_id=1, source_target_pairs={{0,6},{1,3},{2,4},{3,1},{4,2},{5,7},{6,0},{7,5},{8,14},{9,11},{10,... | collective-permute-start | bytes 786440 | tf_op jit(solution)/shard_map/ppermute | solution.py:56
  144.2 8.1 %collective-permute-start.40 = (bf16[8,128,128]{2,1,0:T(8,128)(2,1)S(1)}, bf16[8,128,128]{2,1,0:T(8,128)(2,1)S(1)}, u32[]{:S(2)}, u32[]{:S(2)}) collective-permute-start(bf16[8,128,128]{2,1,0:T(8,128)(2,1)S(1)} %slice.219), channel_id=1, source_target_pairs={{0,48},{1,17},{2,50},{3,19},{4,52},{5,21},{6,54},{7,23},{8,56},{9,... | collective-permute-start | bytes 786440 | tf_op jit(solution)/shard_map/ppermute | solution.py:56
  152.8 12.5 %collective-permute-start.43 = (f32[512,128]{1,0:T(8,128)S(1)}, f32[512,128]{1,0:T(8,128)S(1)}, u32[]{:S(2)}, u32[]{:S(2)}) collective-permute-start(f32[512,128]{1,0:T(8,128)S(1)} %get-tuple-element.62), channel_id=1, source_target_pairs={{0,1},{1,0},{2,3},{3,2},{4,5},{5,4},{6,7},{7,6},{8,9},{9,8},{10,11... | collective-permute-start | bytes 786440 | tf_op jit(solution)/shard_map/ppermute | solution.py:56

commit v2 on v1

--- a/solution.py
+++ b/solution.py
@@ -9,11 +9,11 @@
 from jax.sharding import PartitionSpec as P
 
 DEGREE = 2
-UNROLL = 16
+UNROLL = 32
 GROUP = 64
 BOTH = ("row", "col")
-ROW_FLIPS = (0, 1)
-COL_FLIPS = (0, 1)
+ROW_FLIPS = (1, 0)
+COL_FLIPS = (1, 0)
 
 
 def linear(y_hi, z, y_lo, x, core):

time: 167 us -> 164 us (0.982)
  starting transfers between devices: 83.3 us -> 72.4 us
  waiting for transfers between devices: 58.9 us -> 65 us
    ppermute x44, starting transfers between devices: 83.3 us -> 72.4 us  [move(): return lax.ppermute(value, BOTH, table)]
    ppermute x44, waiting for transfers between devices: 58.9 us -> 65 us  [move(): return lax.ppermute(value, BOTH, table)]
  transfers between devices with their start and end apart: 44 -> 44, of which waited for: 23 -> 24; matrix products, arithmetic and copies ran while one was open for 4% -> 4% of each run, Pallas kernels for 0% -> 0%
where the time goes in v2:
time: 164 us; the launch traced here: 162 us
  starting transfers between devices  72.4 us (44%)
  waiting for transfers between devices  65 us (40%)
  Pallas kernels  13.9 us (8%)
  other arithmetic  7.12 us (4%)
  between operations  2.34 us (1%)
    ppermute x44, starting transfers between devices, move(): return lax.ppermute(value, BOTH, table)  72.4 us
    ppermute x44, waiting for transfers between devices, move(): return lax.ppermute(value, BOTH, table)  65 us
    pallas_call x2, Pallas kernels, slot_products(): pl.pallas_call(slot_kernel, in_specs=[in_smem] * 3 + [anywhere] * 10, out...  13.9 us
  transfers between devices with their start and end apart: 44, of which 24 were waited for; matrix products, arithmetic and copies ran while one was open for 4% of the time, Pallas kernels for 0%

profile of v2, /device:TPU:1, one launch (start us, length us, event | category | flops | bytes accessed | tf_op | source)
XLA Modules:
  0.0 162.4 jit_solution(2839753346872615841)
XLA Ops:
  0.0 1.0 broadcast_select_fusion
  1.0 1.5 collective-permute-start
  3.2 0.7 pad_add_fusion
  4.0 3.1 %collective-permute-start.10 = (bf16[8,128,128]{2,1,0:T(8,128)(2,1)S(1)}, bf16[8,128,128]{2,1,0:T(8,128)(2,1)S(1)}, u32[]{:S(2)}, u32[]{:S(2)}) collective-permute-start(bf16[8,128,128]{2,1,0:T(8,128)(2,1)S(1)} %bitcast.17), channel_id=1, source_target_pairs={{0,64},{1,65},{2,66},{3,67},{4,68},{5,69},{6,70},{7,71},{8,72},{9,... | collective-permute-start | bytes 786440 | tf_op jit(solution)/shard_map/ppermute | solution.py:56
  7.1 1.6 %collective-permute-start.8 = (bf16[8,128,128]{2,1,0:T(8,128)(2,1)S(1)}, bf16[8,128,128]{2,1,0:T(8,128)(2,1)S(1)}, u32[]{:S(2)}, u32[]{:S(2)}) collective-permute-start(bf16[8,128,128]{2,1,0:T(8,128)(2,1)S(1)} %bitcast.18), channel_id=1, source_target_pairs={{0,48},{1,17},{2,50},{3,19},{4,52},{5,21},{6,54},{7,23},{8,56},{9,... | collective-permute-start | bytes 786440 | tf_op jit(solution)/shard_map/ppermute | solution.py:56
  8.8 1.2 collective-permute-start.3
  10.0 0.4 collective-permute-start.5
  10.4 0.5 slice.100
  10.9 2.2 %collective-permute-done.10 = bf16[8,128,128]{2,1,0:T(8,128)(2,1)S(1)} collective-permute-done((bf16[8,128,128]{2,1,0:T(8,128)(2,1)S(1)}, bf16[8,128,128]{2,1,0:T(8,128)(2,1)S(1)}, u32[]{:S(2)}, u32[]{:S(2)}) %collective-permute-start.10) | collective-permute-done | bytes 262176 | tf_op jit(solution)/shard_map/ppermute | solution.py:56
  13.1 2.8 %collective-permute-start.1 = (s32[640]{0:T(1024)S(1)}, s32[640]{0:T(1024)S(1)}, u32[]{:S(2)}, u32[]{:S(2)}) collective-permute-start(s32[640]{0:T(1024)S(1)} %pad_add_fusion), channel_id=1, source_target_pairs={{0,1},{1,0},{2,3},{3,2},{4,5},{5,4},{6,7},{7,6},{8,9},{9,8},{10,11... | collective-permute-start | bytes 7688 | tf_op jit(solution)/shard_map/ppermute | solution.py:56
  15.9 1.1 collective-permute-start.11
  17.1 2.3 %collective-permute-start.9 = (bf16[16,128,128]{2,1,0:T(8,128)(2,1)S(1)}, bf16[16,128,128]{2,1,0:T(8,128)(2,1)S(1)}, u32[]{:S(2)}, u32[]{:S(2)}) collective-permute-start(bf16[16,128,128]{2,1,0:T(8,128)(2,1)S(1)} %get-tuple-element.65.rest_4_), channel_id=1, source_target_pairs={{0,16},{1,49},{2,18},{3,51},{4,20},{5,53},{6,22},{7,55},{8,24},{9,... | collective-permute-start | bytes 1572872 | tf_op jit(solution)/shard_map/ppermute | solution.py:56
  19.4 1.2 collective-permute-start.6
  20.7 0.8 collective-permute-done.11
  21.4 2.1 %collective-permute-start.4 = (bf16[16,128,128]{2,1,0:T(8,128)(2,1)S(1)}, bf16[16,128,128]{2,1,0:T(8,128)(2,1)S(1)}, u32[]{:S(2)}, u32[]{:S(2)}) collective-permute-start(bf16[16,128,128]{2,1,0:T(8,128)(2,1)S(1)} %get-tuple-element.66.rest_0_), channel_id=1, source_target_pairs={{0,2},{1,7},{2,0},{3,5},{4,6},{5,3},{6,4},{7,1},{8,10},{9,15},{10,... | collective-permute-start | bytes 1572872 | tf_op jit(solution)/shard_map/ppermute | solution.py:56
  23.6 1.4 collective-permute-done.6
  24.9 4.4 %collective-permute-start.12 = (bf16[16,128,128]{2,1,0:T(8,128)(2,1)S(1)}, bf16[16,128,128]{2,1,0:T(8,128)(2,1)S(1)}, u32[]{:S(2)}, u32[]{:S(2)}) collective-permute-start(bf16[16,128,128]{2,1,0:T(8,128)(2,1)S(1)} %constant_dynamic-update-slice_fusion.2.rest_6_), channel_id=1, source_target_pairs={{0,16},{1,49},{2,18},{3,51},{4,20},{5,53},{6,22},{7,55},{8,24},{9,... | collective-permute-start | bytes 1572872 | tf_op jit(solution)/shard_map/ppermute | solution.py:56
  29.4 1.5 collective-permute-start.7
  30.9 0.6 add_select_fusion.5
  31.6 0.5 slice.102
  32.1 1.3 pad_add_fusion.5.count_ref
  33.4 0.7 add_select_fusion.4
  34.1 1.8 %collective-permute-done.12.rest_7_ = bf16[16,128,128]{2,1,0:T(8,128)(2,1)S(1)} collective-permute-done((bf16[16,128,128]{2,1,0:T(8,128)(2,1)S(1)}, bf16[16,128,128]{2,1,0:T(8,128)(2,1)S(1)}, u32[]{:S(2)}, u32[]{:S(2)}) %collective-permute-start.12) | collective-permute-done | bytes 524320 | tf_op jit(solution)/shard_map/ppermute | solution.py:56
  36.0 3.2 %collective-permute-done.7.rest_3_ = bf16[16,128,128]{2,1,0:T(8,128)(2,1)S(1)} collective-permute-done((bf16[16,128,128]{2,1,0:T(8,128)(2,1)S(1)}, bf16[16,128,128]{2,1,0:T(8,128)(2,1)S(1)}, u32[]{:S(2)}, u32[]{:S(2)}) %collective-permute-start.7) | collective-permute-done | bytes 524320 | tf_op jit(solution)/shard_map/ppermute | solution.py:56
  39.1 7.0 %shard_map.73 = (bf16[16,128,128]{2,1,0:T(8,128)(2,1)S(1)}, bf16[16,128,128]{2,1,0:T(8,128)(2,1)S(1)}, f32[16,128,128]{2,1,0:T(8,128)S(1)}, f32[16,128,128]{2,1,...) custom-call(s32[512]{0:T(512)S(1)} %get-tuple-element.79.row_tile_re, ...), custom_call_target="tpu_custom_call" | custom-call | flops 4294967296 | bytes 27262976 | tf_op jit(solution)/shard_map/pallas_call | solution.py:158
  46.1 2.7 %collective-permute-start.13 = (bf16[16,128,128]{2,1,0:T(8,128)(2,1)S(1)}, bf16[16,128,128]{2,1,0:T(8,128)(2,1)S(1)}, u32[]{:S(2)}, u32[]{:S(2)}) collective-permute-start(bf16[16,128,128]{2,1,0:T(8,128)(2,1)S(1)} %get-tuple-element.36), channel_id=1, source_target_pairs={{0,2},{1,7},{2,0},{3,5},{4,6},{5,3},{6,4},{7,1},{8,10},{9,15},{10,... | collective-permute-start | bytes 1572872 | tf_op jit(solution)/shard_map/ppermute | solution.py:56
  48.8 4.5 %collective-permute-start.18 = (bf16[16,128,128]{2,1,0:T(8,128)(2,1)S(1)}, bf16[16,128,128]{2,1,0:T(8,128)(2,1)S(1)}, u32[]{:S(2)}, u32[]{:S(2)}) collective-permute-start(bf16[16,128,128]{2,1,0:T(8,128)(2,1)S(1)} %get-tuple-element.42), channel_id=1, source_target_pairs={{0,16},{1,49},{2,18},{3,51},{4,20},{5,53},{6,22},{7,55},{8,24},{9,... | collective-permute-start | bytes 1572872 | tf_op jit(solution)/shard_map/ppermute | solution.py:56
  53.3 2.1 %collective-permute-done.13 = bf16[16,128,128]{2,1,0:T(8,128)(2,1)S(1)} collective-permute-done((bf16[16,128,128]{2,1,0:T(8,128)(2,1)S(1)}, bf16[16,128,128]{2,1,0:T(8,128)(2,1)S(1)}, u32[]{:S(2)}, u32[]{:S(2)}) %collective-permute-start.13) | collective-permute-done | bytes 524320 | tf_op jit(solution)/shard_map/ppermute | solution.py:56
  55.9 2.5 %collective-permute-start.14 = (bf16[16,128,128]{2,1,0:T(8,128)(2,1)S(1)}, bf16[16,128,128]{2,1,0:T(8,128)(2,1)S(1)}, u32[]{:S(2)}, u32[]{:S(2)}) collective-permute-start(bf16[16,128,128]{2,1,0:T(8,128)(2,1)S(1)} %get-tuple-element.38), channel_id=1, source_target_pairs={{0,2},{1,7},{2,0},{3,5},{4,6},{5,3},{6,4},{7,1},{8,10},{9,15},{10,... | collective-permute-start | bytes 1572872 | tf_op jit(solution)/shard_map/ppermute | solution.py:56
  58.4 1.5 collective-permute-done.18
  60.1 3.9 %collective-permute-start.19 = (bf16[16,128,128]{2,1,0:T(8,128)(2,1)S(1)}, bf16[16,128,128]{2,1,0:T(8,128)(2,1)S(1)}, u32[]{:S(2)}, u32[]{:S(2)}) collective-permute-start(bf16[16,128,128]{2,1,0:T(8,128)(2,1)S(1)} %get-tuple-element.44), channel_id=1, source_target_pairs={{0,16},{1,49},{2,18},{3,51},{4,20},{5,53},{6,22},{7,55},{8,24},{9,... | collective-permute-start | bytes 1572872 | tf_op jit(solution)/shard_map/ppermute | solution.py:56
  64.2 1.4 collective-permute-done.21
  65.7 2.5 %collective-permute-start.22 = (bf16[8,128,128]{2,1,0:T(8,128)(2,1)S(1)}, bf16[8,128,128]{2,1,0:T(8,128)(2,1)S(1)}, u32[]{:S(2)}, u32[]{:S(2)}) collective-permute-start(bf16[8,128,128]{2,1,0:T(8,128)(2,1)S(1)} %fusion.11), channel_id=1, source_target_pairs={{0,64},{1,65},{2,66},{3,67},{4,68},{5,69},{6,70},{7,71},{8,72},{9,... | collective-permute-start | bytes 786440 | tf_op jit(solution)/shard_map/ppermute | solution.py:56
  68.3 0.8 collective-permute-start.15
  69.1 2.8 %collective-permute-done.19 = bf16[16,128,128]{2,1,0:T(8,128)(2,1)S(1)} collective-permute-done((bf16[16,128,128]{2,1,0:T(8,128)(2,1)S(1)}, bf16[16,128,128]{2,1,0:T(8,128)(2,1)S(1)}, u32[]{:S(2)}, u32[]{:S(2)}) %collective-permute-start.19) | collective-permute-done | bytes 524320 | tf_op jit(solution)/shard_map/ppermute | solution.py:56
  72.1 1.8 %collective-permute-start.20 = (bf16[8,128,128]{2,1,0:T(8,128)(2,1)S(1)}, bf16[8,128,128]{2,1,0:T(8,128)(2,1)S(1)}, u32[]{:S(2)}, u32[]{:S(2)}) collective-permute-start(bf16[8,128,128]{2,1,0:T(8,128)(2,1)S(1)} %slice.223), channel_id=1, source_target_pairs={{0,48},{1,17},{2,50},{3,19},{4,52},{5,21},{6,54},{7,23},{8,56},{9,... | collective-permute-start | bytes 786440 | tf_op jit(solution)/shard_map/ppermute | solution.py:56
  75.2 5.0 %collective-permute-done.20 = bf16[8,128,128]{2,1,0:T(8,128)(2,1)S(1)} collective-permute-done((bf16[8,128,128]{2,1,0:T(8,128)(2,1)S(1)}, bf16[8,128,128]{2,1,0:T(8,128)(2,1)S(1)}, u32[]{:S(2)}, u32[]{:S(2)}) %collective-permute-start.20) | collective-permute-done | bytes 262176 | tf_op jit(solution)/shard_map/ppermute | solution.py:56
  80.4 1.6 %collective-permute-start.30 = (bf16[8,128,128]{2,1,0:T(8,128)(2,1)S(1)}, bf16[8,128,128]{2,1,0:T(8,128)(2,1)S(1)}, u32[]{:S(2)}, u32[]{:S(2)}) collective-permute-start(bf16[8,128,128]{2,1,0:T(8,128)(2,1)S(1)} %get-tuple-element.59), channel_id=1, source_target_pairs={{0,64},{1,65},{2,66},{3,67},{4,68},{5,69},{6,70},{7,71},{8,72},{9,... | collective-permute-start | bytes 786440 | tf_op jit(solution)/shard_map/ppermute | solution.py:56
  82.1 0.7 collective-permute-start.28
  82.8 1.2 collective-permute-start.23
  84.1 3.2 %collective-permute-done.30 = bf16[8,128,128]{2,1,0:T(8,128)(2,1)S(1)} collective-permute-done((bf16[8,128,128]{2,1,0:T(8,128)(2,1)S(1)}, bf16[8,128,128]{2,1,0:T(8,128)(2,1)S(1)}, u32[]{:S(2)}, u32[]{:S(2)}) %collective-permute-start.30) | collective-permute-done | bytes 262176 | tf_op jit(solution)/shard_map/ppermute | solution.py:56
  87.2 2.6 %collective-permute-done.28 = bf16[8,128,128]{2,1,0:T(8,128)(2,1)S(1)} collective-permute-done((bf16[8,128,128]{2,1,0:T(8,128)(2,1)S(1)}, bf16[8,128,128]{2,1,0:T(8,128)(2,1)S(1)}, u32[]{:S(2)}, u32[]{:S(2)}) %collective-permute-start.28) | collective-permute-done | bytes 262176 | tf_op jit(solution)/shard_map/ppermute | solution.py:56
  90.1 0.9 collective-permute-start.26
  91.1 2.6 %collective-permute-done.31 = bf16[8,128,128]{2,1,0:T(8,128)(2,1)S(1)} collective-permute-done((bf16[8,128,128]{2,1,0:T(8,128)(2,1)S(1)}, bf16[8,128,128]{2,1,0:T(8,128)(2,1)S(1)}, u32[]{:S(2)}, u32[]{:S(2)}) %collective-permute-start.31) | collective-permute-done | bytes 262176 | tf_op jit(solution)/shard_map/ppermute | solution.py:56
  93.7 0.8 collective-permute-start.32
  94.5 2.3 %collective-permute-done.26 = bf16[8,128,128]{2,1,0:T(8,128)(2,1)S(1)} collective-permute-done((bf16[8,128,128]{2,1,0:T(8,128)(2,1)S(1)}, bf16[8,128,128]{2,1,0:T(8,128)(2,1)S(1)}, u32[]{:S(2)}, u32[]{:S(2)}) %collective-permute-start.26) | collective-permute-done | bytes 262176 | tf_op jit(solution)/shard_map/ppermute | solution.py:56
  97.3 4.4 %collective-permute-done.29.rest_5_ = bf16[16,128,128]{2,1,0:T(8,128)(2,1)S(1)} collective-permute-done((bf16[16,128,128]{2,1,0:T(8,128)(2,1)S(1)}, bf16[16,128,128]{2,1,0:T(8,128)(2,1)S(1)}, u32[]{:S(2)}, u32[]{:S(2)}) %collective-permute-start.29) | collective-permute-done | bytes 524320 | tf_op jit(solution)/shard_map/ppermute | solution.py:56
  101.6 7.8 %collective-permute-done.32.rest_7_ = bf16[16,128,128]{2,1,0:T(8,128)(2,1)S(1)} collective-permute-done((bf16[16,128,128]{2,1,0:T(8,128)(2,1)S(1)}, bf16[16,128,128]{2,1,0:T(8,128)(2,1)S(1)}, u32[]{:S(2)}, u32[]{:S(2)}) %collective-permute-start.32) | collective-permute-done | bytes 524320 | tf_op jit(solution)/shard_map/ppermute | solution.py:56
  109.5 7.0 %shard_map.74 = (bf16[16,128,128]{2,1,0:T(8,128)(2,1)S(1)}, bf16[16,128,128]{2,1,0:T(8,128)(2,1)S(1)}, f32[16,128,128]{2,1,0:T(8,128)S(1)}, f32[16,128,128]{2,1,...) custom-call(s32[512]{0:T(512)S(1)} %get-tuple-element.77.row_tile_re, ...), custom_call_target="tpu_custom_call" | custom-call | flops 4294967296 | bytes 27262976 | tf_op jit(solution)/shard_map/pallas_call | solution.py:158
  116.5 0.9 collective-permute-start.38
  117.5 7.1 %collective-permute-done.33 = bf16[16,128,128]{2,1,0:T(8,128)(2,1)S(1)} collective-permute-done((bf16[16,128,128]{2,1,0:T(8,128)(2,1)S(1)}, bf16[16,128,128]{2,1,0:T(8,128)(2,1)S(1)}, u32[]{:S(2)}, u32[]{:S(2)}) %collective-permute-start.33) | collective-permute-done | bytes 524320 | tf_op jit(solution)/shard_map/ppermute | solution.py:56
  124.7 1.5 collective-permute-start.36
  126.4 3.4 %collective-permute-start.41 = (bf16[8,128,128]{2,1,0:T(8,128)(2,1)S(1)}, bf16[8,128,128]{2,1,0:T(8,128)(2,1)S(1)}, u32[]{:S(2)}, u32[]{:S(2)}) collective-permute-start(bf16[8,128,128]{2,1,0:T(8,128)(2,1)S(1)} %slice.218), channel_id=1, source_target_pairs={{0,16},{1,49},{2,18},{3,51},{4,20},{5,53},{6,22},{7,55},{8,24},{9,... | collective-permute-start | bytes 786440 | tf_op jit(solution)/shard_map/ppermute | solution.py:56
  129.9 1.4 collective-permute-done.36
  131.5 2.6 %collective-permute-done.41 = bf16[8,128,128]{2,1,0:T(8,128)(2,1)S(1)} collective-permute-done((bf16[8,128,128]{2,1,0:T(8,128)(2,1)S(1)}, bf16[8,128,128]{2,1,0:T(8,128)(2,1)S(1)}, u32[]{:S(2)}, u32[]{:S(2)}) %collective-permute-start.41) | collective-permute-done | bytes 262176 | tf_op jit(solution)/shard_map/ppermute | solution.py:56
  134.2 2.1 %collective-permute-start.42 = (bf16[8,128,128]{2,1,0:T(8,128)(2,1)S(1)}, bf16[8,128,128]{2,1,0:T(8,128)(2,1)S(1)}, u32[]{:S(2)}, u32[]{:S(2)}) collective-permute-start(bf16[8,128,128]{2,1,0:T(8,128)(2,1)S(1)} %fusion.6), channel_id=1, source_target_pairs={{0,64},{1,65},{2,66},{3,67},{4,68},{5,69},{6,70},{7,71},{8,72},{9,... | collective-permute-start | bytes 786440 | tf_op jit(solution)/shard_map/ppermute | solution.py:56
  136.5 1.7 %collective-permute-done.39 = bf16[16,128,128]{2,1,0:T(8,128)(2,1)S(1)} collective-permute-done((bf16[16,128,128]{2,1,0:T(8,128)(2,1)S(1)}, bf16[16,128,128]{2,1,0:T(8,128)(2,1)S(1)}, u32[]{:S(2)}, u32[]{:S(2)}) %collective-permute-start.39) | collective-permute-done | bytes 524320 | tf_op jit(solution)/shard_map/ppermute | solution.py:56
  138.3 0.8 collective-permute-start.40
  139.2 1.8 %collective-permute-done.42 = bf16[8,128,128]{2,1,0:T(8,128)(2,1)S(1)} collective-permute-done((bf16[8,128,128]{2,1,0:T(8,128)(2,1)S(1)}, bf16[8,128,128]{2,1,0:T(8,128)(2,1)S(1)}, u32[]{:S(2)}, u32[]{:S(2)}) %collective-permute-start.42) | collective-permute-done | bytes 262176 | tf_op jit(solution)/shard_map/ppermute | solution.py:56
  141.0 2.7 %collective-permute-done.35 = bf16[8,128,128]{2,1,0:T(8,128)(2,1)S(1)} collective-permute-done((bf16[8,128,128]{2,1,0:T(8,128)(2,1)S(1)}, bf16[8,128,128]{2,1,0:T(8,128)(2,1)S(1)}, u32[]{:S(2)}, u32[]{:S(2)}) %collective-permute-start.35) | collective-permute-done | bytes 262176 | tf_op jit(solution)/shard_map/ppermute | solution.py:56
  143.8 1.4 collective-permute-done.40
  145.6 14.8 %collective-permute-start.43 = (f32[512,128]{1,0:T(8,128)S(1)}, f32[512,128]{1,0:T(8,128)S(1)}, u32[]{:S(2)}, u32[]{:S(2)}) collective-permute-start(f32[512,128]{1,0:T(8,128)S(1)} %get-tuple-element.62), channel_id=1, source_target_pairs={{0,1},{1,0},{2,3},{3,2},{4,5},{5,4},{6,7},{7,6},{8,9},{9,8},{10,11... | collective-permute-start | bytes 786440 | tf_op jit(solution)/shard_map/ppermute | solution.py:56
  160.4 1.2 collective-permute-done.43
  161.5 0.8 maximum_select_fusion
  (72 shorter events, 4.1 us)
Async XLA Ops:
  1.0 2.9 %collective-permute-start = (bf16[512,128]{1,0:T(8,128)(2,1)S(1)}, bf16[512,128]{1,0:T(8,128)(2,1)S(1)}, u32[]{:S(2)}, u32[]{:S(2)}) collective-permute-start(bf16[512,128]{1,0:T(8,128)(2,1)S(1)} %get-tuple-element.68), channel_id=1, source_target_pairs={{0,1},{1,0},{2,3},{3,2},{4,5},{5,4},{6,7},{7,6},{8,9},{9,8},{10,11... | collective-permute-start | bytes 393224 | tf_op jit(solution)/shard_map/ppermute | solution.py:56
  3.9 35.2 %collective-permute-start.2 = (bf16[256,128,128]{2,1,0:T(8,128)(2,1)}, bf16[256,128,128]{2,1,0:T(8,128)(2,1)}, u32[]{:S(2)}, u32[]{:S(2)}) collective-permute-start(bf16[256,128,128]{2,1,0:T(8,128)(2,1)} %bitcast.14), channel_id=1, source_target_pairs={{0,1},{1,0},{2,3},{3,2},{4,5},{5,4},{6,7},{7,6},{8,9},{9,8},{10,11... | collective-permute-start | bytes 25165832 | tf_op jit(solution)/shard_map/ppermute | solution.py:56
  4.0 9.0 %collective-permute-start.10 = (bf16[8,128,128]{2,1,0:T(8,128)(2,1)S(1)}, bf16[8,128,128]{2,1,0:T(8,128)(2,1)S(1)}, u32[]{:S(2)}, u32[]{:S(2)}) collective-permute-start(bf16[8,128,128]{2,1,0:T(8,128)(2,1)S(1)} %bitcast.17), channel_id=1, source_target_pairs={{0,64},{1,65},{2,66},{3,67},{4,68},{5,69},{6,70},{7,71},{8,72},{9,... | collective-permute-start | bytes 786440 | tf_op jit(solution)/shard_map/ppermute | solution.py:56
  7.1 8.8 %collective-permute-start.8 = (bf16[8,128,128]{2,1,0:T(8,128)(2,1)S(1)}, bf16[8,128,128]{2,1,0:T(8,128)(2,1)S(1)}, u32[]{:S(2)}, u32[]{:S(2)}) collective-permute-start(bf16[8,128,128]{2,1,0:T(8,128)(2,1)S(1)} %bitcast.18), channel_id=1, source_target_pairs={{0,48},{1,17},{2,50},{3,19},{4,52},{5,21},{6,54},{7,23},{8,56},{9,... | collective-permute-start | bytes 786440 | tf_op jit(solution)/shard_map/ppermute | solution.py:56
  8.8 8.3 %collective-permute-start.3 = (bf16[8,128,128]{2,1,0:T(8,128)(2,1)S(1)}, bf16[8,128,128]{2,1,0:T(8,128)(2,1)S(1)}, u32[]{:S(2)}, u32[]{:S(2)}) collective-permute-start(bf16[8,128,128]{2,1,0:T(8,128)(2,1)S(1)} %bitcast.19), channel_id=1, source_target_pairs={{0,6},{1,3},{2,4},{3,1},{4,2},{5,7},{6,0},{7,5},{8,14},{9,11},{10,... | collective-permute-start | bytes 786440 | tf_op jit(solution)/shard_map/ppermute | solution.py:56
  10.0 9.5 %collective-permute-start.5 = (bf16[8,128,128]{2,1,0:T(8,128)(2,1)S(1)}, bf16[8,128,128]{2,1,0:T(8,128)(2,1)S(1)}, u32[]{:S(2)}, u32[]{:S(2)}) collective-permute-start(bf16[8,128,128]{2,1,0:T(8,128)(2,1)S(1)} %bitcast.20), channel_id=1, source_target_pairs={{0,8},{1,9},{2,10},{3,11},{4,12},{5,13},{6,14},{7,15},{8,0},{9,1},... | collective-permute-start | bytes 786440 | tf_op jit(solution)/shard_map/ppermute | solution.py:56
  13.1 16.3 %collective-permute-start.1 = (s32[640]{0:T(1024)S(1)}, s32[640]{0:T(1024)S(1)}, u32[]{:S(2)}, u32[]{:S(2)}) collective-permute-start(s32[640]{0:T(1024)S(1)} %pad_add_fusion), channel_id=1, source_target_pairs={{0,1},{1,0},{2,3},{3,2},{4,5},{5,4},{6,7},{7,6},{8,9},{9,8},{10,11... | collective-permute-start | bytes 7688 | tf_op jit(solution)/shard_map/ppermute | solution.py:56
  15.9 5.5 %collective-permute-start.11 = (bf16[8,128,128]{2,1,0:T(8,128)(2,1)S(1)}, bf16[8,128,128]{2,1,0:T(8,128)(2,1)S(1)}, u32[]{:S(2)}, u32[]{:S(2)}) collective-permute-start(bf16[8,128,128]{2,1,0:T(8,128)(2,1)S(1)} %collective-permute-done.10), channel_id=1, source_target_pairs={{0,48},{1,17},{2,50},{3,19},{4,52},{5,21},{6,54},{7,23},{8,56},{9,... | collective-permute-start | bytes 786440 | tf_op jit(solution)/shard_map/ppermute | solution.py:56
  17.1 17.0 %collective-permute-start.9 = (bf16[16,128,128]{2,1,0:T(8,128)(2,1)S(1)}, bf16[16,128,128]{2,1,0:T(8,128)(2,1)S(1)}, u32[]{:S(2)}, u32[]{:S(2)}) collective-permute-start(bf16[16,128,128]{2,1,0:T(8,128)(2,1)S(1)} %get-tuple-element.65.rest_4_), channel_id=1, source_target_pairs={{0,16},{1,49},{2,18},{3,51},{4,20},{5,53},{6,22},{7,55},{8,24},{9,... | collective-permute-start | bytes 1572872 | tf_op jit(solution)/shard_map/ppermute | solution.py:56
  19.4 5.5 %collective-permute-start.6 = (bf16[8,128,128]{2,1,0:T(8,128)(2,1)S(1)}, bf16[8,128,128]{2,1,0:T(8,128)(2,1)S(1)}, u32[]{:S(2)}, u32[]{:S(2)}) collective-permute-start(bf16[8,128,128]{2,1,0:T(8,128)(2,1)S(1)} %collective-permute-done.5), channel_id=1, source_target_pairs={{0,6},{1,3},{2,4},{3,1},{4,2},{5,7},{6,0},{7,5},{8,14},{9,11},{10,... | collective-permute-start | bytes 786440 | tf_op jit(solution)/shard_map/ppermute | solution.py:56
  21.4 12.7 %collective-permute-start.4 = (bf16[16,128,128]{2,1,0:T(8,128)(2,1)S(1)}, bf16[16,128,128]{2,1,0:T(8,128)(2,1)S(1)}, u32[]{:S(2)}, u32[]{:S(2)}) collective-permute-start(bf16[16,128,128]{2,1,0:T(8,128)(2,1)S(1)} %get-tuple-element.66.rest_0_), channel_id=1, source_target_pairs={{0,2},{1,7},{2,0},{3,5},{4,6},{5,3},{6,4},{7,1},{8,10},{9,15},{10,... | collective-permute-start | bytes 1572872 | tf_op jit(solution)/shard_map/ppermute | solution.py:56
  24.9 11.0 %collective-permute-start.12 = (bf16[16,128,128]{2,1,0:T(8,128)(2,1)S(1)}, bf16[16,128,128]{2,1,0:T(8,128)(2,1)S(1)}, u32[]{:S(2)}, u32[]{:S(2)}) collective-permute-start(bf16[16,128,128]{2,1,0:T(8,128)(2,1)S(1)} %constant_dynamic-update-slice_fusion.2.rest_6_), channel_id=1, source_target_pairs={{0,16},{1,49},{2,18},{3,51},{4,20},{5,53},{6,22},{7,55},{8,24},{9,... | collective-permute-start | bytes 1572872 | tf_op jit(solution)/shard_map/ppermute | solution.py:56
  29.4 9.7 %collective-permute-start.7 = (bf16[16,128,128]{2,1,0:T(8,128)(2,1)S(1)}, bf16[16,128,128]{2,1,0:T(8,128)(2,1)S(1)}, u32[]{:S(2)}, u32[]{:S(2)}) collective-permute-start(bf16[16,128,128]{2,1,0:T(8,128)(2,1)S(1)} %constant_dynamic-update-slice_fusion.rest_2_), channel_id=1, source_target_pairs={{0,2},{1,7},{2,0},{3,5},{4,6},{5,3},{6,4},{7,1},{8,10},{9,15},{10,... | collective-permute-start | bytes 1572872 | tf_op jit(solution)/shard_map/ppermute | solution.py:56
  46.1 9.3 %collective-permute-start.13 = (bf16[16,128,128]{2,1,0:T(8,128)(2,1)S(1)}, bf16[16,128,128]{2,1,0:T(8,128)(2,1)S(1)}, u32[]{:S(2)}, u32[]{:S(2)}) collective-permute-start(bf16[16,128,128]{2,1,0:T(8,128)(2,1)S(1)} %get-tuple-element.36), channel_id=1, source_target_pairs={{0,2},{1,7},{2,0},{3,5},{4,6},{5,3},{6,4},{7,1},{8,10},{9,15},{10,... | collective-permute-start | bytes 1572872 | tf_op jit(solution)/shard_map/ppermute | solution.py:56
  48.8 11.1 %collective-permute-start.18 = (bf16[16,128,128]{2,1,0:T(8,128)(2,1)S(1)}, bf16[16,128,128]{2,1,0:T(8,128)(2,1)S(1)}, u32[]{:S(2)}, u32[]{:S(2)}) collective-permute-start(bf16[16,128,128]{2,1,0:T(8,128)(2,1)S(1)} %get-tuple-element.42), channel_id=1, source_target_pairs={{0,16},{1,49},{2,18},{3,51},{4,20},{5,53},{6,22},{7,55},{8,24},{9,... | collective-permute-start | bytes 1572872 | tf_op jit(solution)/shard_map/ppermute | solution.py:56
  55.6 8.4 %collective-permute-start.16 = (bf16[8,128,128]{2,1,0:T(8,128)(2,1)S(1)}, bf16[8,128,128]{2,1,0:T(8,128)(2,1)S(1)}, u32[]{:S(2)}, u32[]{:S(2)}) collective-permute-start(bf16[8,128,128]{2,1,0:T(8,128)(2,1)S(1)} %slice.224), channel_id=1, source_target_pairs={{0,6},{1,3},{2,4},{3,1},{4,2},{5,7},{6,0},{7,5},{8,14},{9,11},{10,... | collective-permute-start | bytes 786440 | tf_op jit(solution)/shard_map/ppermute | solution.py:56
  55.9 12.2 %collective-permute-start.14 = (bf16[16,128,128]{2,1,0:T(8,128)(2,1)S(1)}, bf16[16,128,128]{2,1,0:T(8,128)(2,1)S(1)}, u32[]{:S(2)}, u32[]{:S(2)}) collective-permute-start(bf16[16,128,128]{2,1,0:T(8,128)(2,1)S(1)} %get-tuple-element.38), channel_id=1, source_target_pairs={{0,2},{1,7},{2,0},{3,5},{4,6},{5,3},{6,4},{7,1},{8,10},{9,15},{10,... | collective-permute-start | bytes 1572872 | tf_op jit(solution)/shard_map/ppermute | solution.py:56
  60.0 5.6 %collective-permute-start.21 = (bf16[8,128,128]{2,1,0:T(8,128)(2,1)S(1)}, bf16[8,128,128]{2,1,0:T(8,128)(2,1)S(1)}, u32[]{:S(2)}, u32[]{:S(2)}) collective-permute-start(bf16[8,128,128]{2,1,0:T(8,128)(2,1)S(1)} %slice.222), channel_id=1, source_target_pairs={{0,48},{1,17},{2,50},{3,19},{4,52},{5,21},{6,54},{7,23},{8,56},{9,... | collective-permute-start | bytes 786440 | tf_op jit(solution)/shard_map/ppermute | solution.py:56
  60.1 11.8 %collective-permute-start.19 = (bf16[16,128,128]{2,1,0:T(8,128)(2,1)S(1)}, bf16[16,128,128]{2,1,0:T(8,128)(2,1)S(1)}, u32[]{:S(2)}, u32[]{:S(2)}) collective-permute-start(bf16[16,128,128]{2,1,0:T(8,128)(2,1)S(1)} %get-tuple-element.44), channel_id=1, source_target_pairs={{0,16},{1,49},{2,18},{3,51},{4,20},{5,53},{6,22},{7,55},{8,24},{9,... | collective-permute-start | bytes 1572872 | tf_op jit(solution)/shard_map/ppermute | solution.py:56
  64.1 11.1 %collective-permute-start.17 = (bf16[8,128,128]{2,1,0:T(8,128)(2,1)S(1)}, bf16[8,128,128]{2,1,0:T(8,128)(2,1)S(1)}, u32[]{:S(2)}, u32[]{:S(2)}) collective-permute-start(bf16[8,128,128]{2,1,0:T(8,128)(2,1)S(1)} %fusion.14), channel_id=1, source_target_pairs={{0,8},{1,9},{2,10},{3,11},{4,12},{5,13},{6,14},{7,15},{8,0},{9,1},... | collective-permute-start | bytes 786440 | tf_op jit(solution)/shard_map/ppermute | solution.py:56
  65.7 9.5 %collective-permute-start.22 = (bf16[8,128,128]{2,1,0:T(8,128)(2,1)S(1)}, bf16[8,128,128]{2,1,0:T(8,128)(2,1)S(1)}, u32[]{:S(2)}, u32[]{:S(2)}) collective-permute-start(bf16[8,128,128]{2,1,0:T(8,128)(2,1)S(1)} %fusion.11), channel_id=1, source_target_pairs={{0,64},{1,65},{2,66},{3,67},{4,68},{5,69},{6,70},{7,71},{8,72},{9,... | collective-permute-start | bytes 786440 | tf_op jit(solution)/shard_map/ppermute | solution.py:56
  68.3 6.9 %collective-permute-start.15 = (bf16[8,128,128]{2,1,0:T(8,128)(2,1)S(1)}, bf16[8,128,128]{2,1,0:T(8,128)(2,1)S(1)}, u32[]{:S(2)}, u32[]{:S(2)}) collective-permute-start(bf16[8,128,128]{2,1,0:T(8,128)(2,1)S(1)} %slice.225), channel_id=1, source_target_pairs={{0,6},{1,3},{2,4},{3,1},{4,2},{5,7},{6,0},{7,5},{8,14},{9,11},{10,... | collective-permute-start | bytes 786440 | tf_op jit(solution)/shard_map/ppermute | solution.py:56
  72.1 8.1 %collective-permute-start.20 = (bf16[8,128,128]{2,1,0:T(8,128)(2,1)S(1)}, bf16[8,128,128]{2,1,0:T(8,128)(2,1)S(1)}, u32[]{:S(2)}, u32[]{:S(2)}) collective-permute-start(bf16[8,128,128]{2,1,0:T(8,128)(2,1)S(1)} %slice.223), channel_id=1, source_target_pairs={{0,48},{1,17},{2,50},{3,19},{4,52},{5,21},{6,54},{7,23},{8,56},{9,... | collective-permute-start | bytes 786440 | tf_op jit(solution)/shard_map/ppermute | solution.py:56
  80.4 6.8 %collective-permute-start.30 = (bf16[8,128,128]{2,1,0:T(8,128)(2,1)S(1)}, bf16[8,128,128]{2,1,0:T(8,128)(2,1)S(1)}, u32[]{:S(2)}, u32[]{:S(2)}) collective-permute-start(bf16[8,128,128]{2,1,0:T(8,128)(2,1)S(1)} %get-tuple-element.59), channel_id=1, source_target_pairs={{0,64},{1,65},{2,66},{3,67},{4,68},{5,69},{6,70},{7,71},{8,72},{9,... | collective-permute-start | bytes 786440 | tf_op jit(solution)/shard_map/ppermute | solution.py:56
  82.1 7.8 %collective-permute-start.28 = (bf16[8,128,128]{2,1,0:T(8,128)(2,1)S(1)}, bf16[8,128,128]{2,1,0:T(8,128)(2,1)S(1)}, u32[]{:S(2)}, u32[]{:S(2)}) collective-permute-start(bf16[8,128,128]{2,1,0:T(8,128)(2,1)S(1)} %get-tuple-element.59), channel_id=1, source_target_pairs={{0,16},{1,49},{2,18},{3,51},{4,20},{5,53},{6,22},{7,55},{8,24},{9,... | collective-permute-start | bytes 786440 | tf_op jit(solution)/shard_map/ppermute | solution.py:56
  82.8 7.0 %collective-permute-start.23 = (bf16[8,128,128]{2,1,0:T(8,128)(2,1)S(1)}, bf16[8,128,128]{2,1,0:T(8,128)(2,1)S(1)}, u32[]{:S(2)}, u32[]{:S(2)}) collective-permute-start(bf16[8,128,128]{2,1,0:T(8,128)(2,1)S(1)} %get-tuple-element.59), channel_id=1, source_target_pairs={{0,2},{1,7},{2,0},{3,5},{4,6},{5,3},{6,4},{7,1},{8,10},{9,15},{10,... | collective-permute-start | bytes 786440 | tf_op jit(solution)/shard_map/ppermute | solution.py:56
  84.1 6.1 %collective-permute-start.25 = (bf16[8,128,128]{2,1,0:T(8,128)(2,1)S(1)}, bf16[8,128,128]{2,1,0:T(8,128)(2,1)S(1)}, u32[]{:S(2)}, u32[]{:S(2)}) collective-permute-start(bf16[8,128,128]{2,1,0:T(8,128)(2,1)S(1)} %get-tuple-element.59), channel_id=1, source_target_pairs={{0,8},{1,9},{2,10},{3,11},{4,12},{5,13},{6,14},{7,15},{8,0},{9,1},... | collective-permute-start | bytes 786440 | tf_op jit(solution)/shard_map/ppermute | solution.py:56
  87.2 6.4 %collective-permute-start.31 = (bf16[8,128,128]{2,1,0:T(8,128)(2,1)S(1)}, bf16[8,128,128]{2,1,0:T(8,128)(2,1)S(1)}, u32[]{:S(2)}, u32[]{:S(2)}) collective-permute-start(bf16[8,128,128]{2,1,0:T(8,128)(2,1)S(1)} %collective-permute-done.30), channel_id=1, source_target_pairs={{0,16},{1,49},{2,18},{3,51},{4,20},{5,53},{6,22},{7,55},{8,24},{9,... | collective-permute-start | bytes 786440 | tf_op jit(solution)/shard_map/ppermute | solution.py:56
  89.9 11.7 %collective-permute-start.29 = (bf16[16,128,128]{2,1,0:T(8,128)(2,1)S(1)}, bf16[16,128,128]{2,1,0:T(8,128)(2,1)S(1)}, u32[]{:S(2)}, u32[]{:S(2)}) collective-permute-start(bf16[16,128,128]{2,1,0:T(8,128)(2,1)S(1)} %get-tuple-element.63.rest_4_), channel_id=1, source_target_pairs={{0,48},{1,17},{2,50},{3,19},{4,52},{5,21},{6,54},{7,23},{8,56},{9,... | collective-permute-start | bytes 1572872 | tf_op jit(solution)/shard_map/ppermute | solution.py:56
  90.1 11.5 %collective-permute-start.24 = (bf16[16,128,128]{2,1,0:T(8,128)(2,1)S(1)}, bf16[16,128,128]{2,1,0:T(8,128)(2,1)S(1)}, u32[]{:S(2)}, u32[]{:S(2)}) collective-permute-start(bf16[16,128,128]{2,1,0:T(8,128)(2,1)S(1)} %get-tuple-element.64.rest_0_), channel_id=1, source_target_pairs={{0,6},{1,3},{2,4},{3,1},{4,2},{5,7},{6,0},{7,5},{8,14},{9,11},{10,... | collective-permute-start | bytes 1572872 | tf_op jit(solution)/shard_map/ppermute | solution.py:56
  90.1 6.7 %collective-permute-start.26 = (bf16[8,128,128]{2,1,0:T(8,128)(2,1)S(1)}, bf16[8,128,128]{2,1,0:T(8,128)(2,1)S(1)}, u32[]{:S(2)}, u32[]{:S(2)}) collective-permute-start(bf16[8,128,128]{2,1,0:T(8,128)(2,1)S(1)} %collective-permute-done.25), channel_id=1, source_target_pairs={{0,2},{1,7},{2,0},{3,5},{4,6},{5,3},{6,4},{7,1},{8,10},{9,15},{10,... | collective-permute-start | bytes 786440 | tf_op jit(solution)/shard_map/ppermute | solution.py:56
  93.7 15.8 %collective-permute-start.32 = (bf16[16,128,128]{2,1,0:T(8,128)(2,1)S(1)}, bf16[16,128,128]{2,1,0:T(8,128)(2,1)S(1)}, u32[]{:S(2)}, u32[]{:S(2)}) collective-permute-start(bf16[16,128,128]{2,1,0:T(8,128)(2,1)S(1)} %constant_dynamic-update-slice_fusion.6.rest_6_), channel_id=1, source_target_pairs={{0,48},{1,17},{2,50},{3,19},{4,52},{5,21},{6,54},{7,23},{8,56},{9,... | collective-permute-start | bytes 1572872 | tf_op jit(solution)/shard_map/ppermute | solution.py:56
  96.9 12.6 %collective-permute-start.27 = (bf16[16,128,128]{2,1,0:T(8,128)(2,1)S(1)}, bf16[16,128,128]{2,1,0:T(8,128)(2,1)S(1)}, u32[]{:S(2)}, u32[]{:S(2)}) collective-permute-start(bf16[16,128,128]{2,1,0:T(8,128)(2,1)S(1)} %constant_dynamic-update-slice_fusion.4.rest_2_), channel_id=1, source_target_pairs={{0,6},{1,3},{2,4},{3,1},{4,2},{5,7},{6,0},{7,5},{8,14},{9,11},{10,... | collective-permute-start | bytes 1572872 | tf_op jit(solution)/shard_map/ppermute | solution.py:56
  116.4 8.1 %collective-permute-start.33 = (bf16[16,128,128]{2,1,0:T(8,128)(2,1)S(1)}, bf16[16,128,128]{2,1,0:T(8,128)(2,1)S(1)}, u32[]{:S(2)}, u32[]{:S(2)}) collective-permute-start(bf16[16,128,128]{2,1,0:T(8,128)(2,1)S(1)} %get-tuple-element.48), channel_id=1, source_target_pairs={{0,6},{1,3},{2,4},{3,1},{4,2},{5,7},{6,0},{7,5},{8,14},{9,11},{10,... | collective-permute-start | bytes 1572872 | tf_op jit(solution)/shard_map/ppermute | solution.py:56
  116.5 9.7 %collective-permute-start.38 = (bf16[16,128,128]{2,1,0:T(8,128)(2,1)S(1)}, bf16[16,128,128]{2,1,0:T(8,128)(2,1)S(1)}, u32[]{:S(2)}, u32[]{:S(2)}) collective-permute-start(bf16[16,128,128]{2,1,0:T(8,128)(2,1)S(1)} %get-tuple-element.54), channel_id=1, source_target_pairs={{0,48},{1,17},{2,50},{3,19},{4,52},{5,21},{6,54},{7,23},{8,56},{9,... | collective-permute-start | bytes 1572872 | tf_op jit(solution)/shard_map/ppermute | solution.py:56
  124.7 6.5 %collective-permute-start.36 = (bf16[8,128,128]{2,1,0:T(8,128)(2,1)S(1)}, bf16[8,128,128]{2,1,0:T(8,128)(2,1)S(1)}, u32[]{:S(2)}, u32[]{:S(2)}) collective-permute-start(bf16[8,128,128]{2,1,0:T(8,128)(2,1)S(1)} %slice.220), channel_id=1, source_target_pairs={{0,2},{1,7},{2,0},{3,5},{4,6},{5,3},{6,4},{7,1},{8,10},{9,15},{10,... | collective-permute-start | bytes 786440 | tf_op jit(solution)/shard_map/ppermute | solution.py:56
  126.3 10.0 %collective-permute-start.34 = (bf16[16,128,128]{2,1,0:T(8,128)(2,1)S(1)}, bf16[16,128,128]{2,1,0:T(8,128)(2,1)S(1)}, u32[]{:S(2)}, u32[]{:S(2)}) collective-permute-start(bf16[16,128,128]{2,1,0:T(8,128)(2,1)S(1)} %get-tuple-element.50), channel_id=1, source_target_pairs={{0,6},{1,3},{2,4},{3,1},{4,2},{5,7},{6,0},{7,5},{8,14},{9,11},{10,... | collective-permute-start | bytes 1572872 | tf_op jit(solution)/shard_map/ppermute | solution.py:56
  126.4 7.7 %collective-permute-start.41 = (bf16[8,128,128]{2,1,0:T(8,128)(2,1)S(1)}, bf16[8,128,128]{2,1,0:T(8,128)(2,1)S(1)}, u32[]{:S(2)}, u32[]{:S(2)}) collective-permute-start(bf16[8,128,128]{2,1,0:T(8,128)(2,1)S(1)} %slice.218), channel_id=1, source_target_pairs={{0,16},{1,49},{2,18},{3,51},{4,20},{5,53},{6,22},{7,55},{8,24},{9,... | collective-permute-start | bytes 786440 | tf_op jit(solution)/shard_map/ppermute | solution.py:56
  129.9 8.3 %collective-permute-start.39 = (bf16[16,128,128]{2,1,0:T(8,128)(2,1)S(1)}, bf16[16,128,128]{2,1,0:T(8,128)(2,1)S(1)}, u32[]{:S(2)}, u32[]{:S(2)}) collective-permute-start(bf16[16,128,128]{2,1,0:T(8,128)(2,1)S(1)} %get-tuple-element.56), channel_id=1, source_target_pairs={{0,48},{1,17},{2,50},{3,19},{4,52},{5,21},{6,54},{7,23},{8,56},{9,... | collective-permute-start | bytes 1572872 | tf_op jit(solution)/shard_map/ppermute | solution.py:56
  131.3 7.9 %collective-permute-start.37 = (bf16[8,128,128]{2,1,0:T(8,128)(2,1)S(1)}, bf16[8,128,128]{2,1,0:T(8,128)(2,1)S(1)}, u32[]{:S(2)}, u32[]{:S(2)}) collective-permute-start(bf16[8,128,128]{2,1,0:T(8,128)(2,1)S(1)} %fusion.9), channel_id=1, source_target_pairs={{0,8},{1,9},{2,10},{3,11},{4,12},{5,13},{6,14},{7,15},{8,0},{9,1},... | collective-permute-start | bytes 786440 | tf_op jit(solution)/shard_map/ppermute | solution.py:56
  134.2 6.8 %collective-permute-start.42 = (bf16[8,128,128]{2,1,0:T(8,128)(2,1)S(1)}, bf16[8,128,128]{2,1,0:T(8,128)(2,1)S(1)}, u32[]{:S(2)}, u32[]{:S(2)}) collective-permute-start(bf16[8,128,128]{2,1,0:T(8,128)(2,1)S(1)} %fusion.6), channel_id=1, source_target_pairs={{0,64},{1,65},{2,66},{3,67},{4,68},{5,69},{6,70},{7,71},{8,72},{9,... | collective-permute-start | bytes 786440 | tf_op jit(solution)/shard_map/ppermute | solution.py:56
  136.4 7.3 %collective-permute-start.35 = (bf16[8,128,128]{2,1,0:T(8,128)(2,1)S(1)}, bf16[8,128,128]{2,1,0:T(8,128)(2,1)S(1)}, u32[]{:S(2)}, u32[]{:S(2)}) collective-permute-start(bf16[8,128,128]{2,1,0:T(8,128)(2,1)S(1)} %slice.221), channel_id=1, source_target_pairs={{0,2},{1,7},{2,0},{3,5},{4,6},{5,3},{6,4},{7,1},{8,10},{9,15},{10,... | collective-permute-start | bytes 786440 | tf_op jit(solution)/shard_map/ppermute | solution.py:56
  138.3 6.8 %collective-permute-start.40 = (bf16[8,128,128]{2,1,0:T(8,128)(2,1)S(1)}, bf16[8,128,128]{2,1,0:T(8,128)(2,1)S(1)}, u32[]{:S(2)}, u32[]{:S(2)}) collective-permute-start(bf16[8,128,128]{2,1,0:T(8,128)(2,1)S(1)} %slice.219), channel_id=1, source_target_pairs={{0,16},{1,49},{2,18},{3,51},{4,20},{5,53},{6,22},{7,55},{8,24},{9,... | collective-permute-start | bytes 786440 | tf_op jit(solution)/shard_map/ppermute | solution.py:56
  145.6 16.0 %collective-permute-start.43 = (f32[512,128]{1,0:T(8,128)S(1)}, f32[512,128]{1,0:T(8,128)S(1)}, u32[]{:S(2)}, u32[]{:S(2)}) collective-permute-start(f32[512,128]{1,0:T(8,128)S(1)} %get-tuple-element.62), channel_id=1, source_target_pairs={{0,1},{1,0},{2,3},{3,2},{4,5},{5,4},{6,7},{7,6},{8,9},{9,8},{10,11... | collective-permute-start | bytes 786440 | tf_op jit(solution)/shard_map/ppermute | solution.py:56

commit v3 on v2

--- a/solution.py
+++ b/solution.py
@@ -178,26 +178,33 @@
     )(row_tiles, col_tiles, counts, own, mate, *row_parts, *col_parts)
 
 
-def gather(operand, moves):
-    across, first, second = moves
-    parts = []
-    for value in (operand, move(operand, across)):
-        near = jnp.concatenate([value, move(value, first)])
-        parts += [near, move(near, second)]
-    return parts
+def gather(operand, plans):
+    mates = [move(operand, plan[0]) for plan in plans]
+    nexts = [move(operand, plan[1]) for plan in plans]
+    sides = []
+    seconds = [move(mate, plan[1]) for plan, mate in zip(plans, mates)]
+    for plan, near, mate, second in zip(plans, nexts, mates, seconds):
+        own = jnp.concatenate([operand, near])
+        far = jnp.concatenate([mate, second])
+        sides.append([own, move(own, plan[2]), far, move(far, plan[2])])
+    return sides
+
+
+def halves(kept, got):
+    half = kept.shape[0] // 2
+    stay = kept[:half] + got[:half].astype(jnp.float32)
+    return stay, (kept[half:] + got[half:].astype(jnp.float32)).astype(jnp.bfloat16)
 
 
 def scatter_sum(sent_first, sent_next, kept_first, kept_next, moves):
     across, first, second = moves
-    half = kept_first.shape[0] // 2
     got = move(sent_first, second)
     got, sent_next = lax.optimization_barrier((got, sent_next))
-    near = kept_first + got.astype(jnp.float32)
-    sum_first = near[:half] + move(near[half:].astype(jnp.bfloat16), first).astype(jnp.float32)
-    got = move(sent_next, second)
-    near = kept_next + got.astype(jnp.float32)
-    sum_next = near[:half] + move(near[half:].astype(jnp.bfloat16), first).astype(jnp.float32)
-    return sum_next + move(sum_first.astype(jnp.bfloat16), across).astype(jnp.float32)
+    stay, send = halves(kept_first, got)
+    sum_first = (stay + move(send, first).astype(jnp.float32)).astype(jnp.bfloat16)
+    stay, send = halves(kept_next, move(sent_next, second))
+    last = move(send, first).astype(jnp.float32)
+    return (stay + move(sum_first, across).astype(jnp.float32)) + last
 
 
 def place_of(near_bit, ring, core):
@@ -252,8 +259,7 @@
         own_tiles = tiles_of(table, core, core ^ row_flip, core ^ col_flip)
         mate_tiles = tiles_of(mate_table, 1 - core, core ^ row_flip, core ^ col_flip)
         row_tiles, col_tiles = (jnp.concatenate(pair) for pair in zip(own_tiles, mate_tiles))
-        col_parts = gather(tiled, col_plan)
-        row_parts = gather(tiled, row_plan)
+        col_parts, row_parts = gather(tiled, (col_plan, row_plan))
         found = slot_products(row_tiles, col_tiles, counts, own, mate, row_parts, col_parts)
         applied = scatter_sum(*found[:4], row_plan) + scatter_sum(*found[4:], col_plan)
         shifted = applied.reshape(2 * seg, half) - center * current

time: 164 us -> 163 us (level); the launches traced: 162 us -> 163 us
  waiting for transfers between devices: 65 us -> 56.7 us
  starting transfers between devices: 72.4 us -> 79 us
  Pallas kernels: 13.9 us -> 16.8 us
    ppermute x44, waiting for transfers between devices: 65 us -> 56.7 us  [move(): return lax.ppermute(value, BOTH, table)]
    ppermute x44, starting transfers between devices: 72.4 us -> 79 us  [move(): return lax.ppermute(value, BOTH, table)]
    pallas_call x2, Pallas kernels: 13.9 us -> 16.8 us  [slot_products(): pl.pallas_call(slot_kernel, in_specs=[in_smem] * 3 + [anywhere] * 10, out...]
  transfers between devices with their start and end apart: 44 -> 44, of which waited for: 24 -> 23; matrix products, arithmetic and copies ran while one was open for 4% -> 3% of each run, Pallas kernels for 0% -> 0%
where the time goes in v3:
time: 163 us
  starting transfers between devices  79 us (48%)
  waiting for transfers between devices  56.7 us (35%)
  Pallas kernels  16.8 us (10%)
  other arithmetic  7.03 us (4%)
  between operations  2.28 us (1%)
    ppermute x44, starting transfers between devices, move(): return lax.ppermute(value, BOTH, table)  79 us
    ppermute x44, waiting for transfers between devices, move(): return lax.ppermute(value, BOTH, table)  56.7 us
    pallas_call x2, Pallas kernels, slot_products(): pl.pallas_call(slot_kernel, in_specs=[in_smem] * 3 + [anywhere] * 10, out...  16.8 us
  transfers between devices with their start and end apart: 44, of which 23 were waited for; matrix products, arithmetic and copies ran while one was open for 3% of the time, Pallas kernels for 0%

profile of v3, /device:TPU:1, one launch (start us, length us, event | category | flops | bytes accessed | tf_op | source)
XLA Modules:
  0.0 163.1 jit_solution(123180524892460054)
XLA Ops:
  0.0 1.0 broadcast_select_fusion
  1.0 1.5 collective-permute-start
  3.2 0.7 pad_add_fusion
  4.0 3.1 %collective-permute-start.10 = (bf16[8,128,128]{2,1,0:T(8,128)(2,1)S(1)}, bf16[8,128,128]{2,1,0:T(8,128)(2,1)S(1)}, u32[]{:S(2)}, u32[]{:S(2)}) collective-permute-start(bf16[8,128,128]{2,1,0:T(8,128)(2,1)S(1)} %bitcast.17), channel_id=1, source_target_pairs={{0,64},{1,65},{2,66},{3,67},{4,68},{5,69},{6,70},{7,71},{8,72},{9,... | collective-permute-start | bytes 786440 | tf_op jit(solution)/shard_map/ppermute | solution.py:56
  7.1 1.6 %collective-permute-start.8 = (bf16[8,128,128]{2,1,0:T(8,128)(2,1)S(1)}, bf16[8,128,128]{2,1,0:T(8,128)(2,1)S(1)}, u32[]{:S(2)}, u32[]{:S(2)}) collective-permute-start(bf16[8,128,128]{2,1,0:T(8,128)(2,1)S(1)} %bitcast.18), channel_id=1, source_target_pairs={{0,48},{1,17},{2,50},{3,19},{4,52},{5,21},{6,54},{7,23},{8,56},{9,... | collective-permute-start | bytes 786440 | tf_op jit(solution)/shard_map/ppermute | solution.py:56
  8.8 1.2 collective-permute-start.3
  10.4 0.5 slice.140
  10.9 2.2 %collective-permute-done.10 = bf16[8,128,128]{2,1,0:T(8,128)(2,1)S(1)} collective-permute-done((bf16[8,128,128]{2,1,0:T(8,128)(2,1)S(1)}, bf16[8,128,128]{2,1,0:T(8,128)(2,1)S(1)}, u32[]{:S(2)}, u32[]{:S(2)}) %collective-permute-start.10) | collective-permute-done | bytes 262176 | tf_op jit(solution)/shard_map/ppermute | solution.py:56
  13.1 2.8 %collective-permute-start.1 = (s32[640]{0:T(1024)S(1)}, s32[640]{0:T(1024)S(1)}, u32[]{:S(2)}, u32[]{:S(2)}) collective-permute-start(s32[640]{0:T(1024)S(1)} %pad_add_fusion), channel_id=1, source_target_pairs={{0,1},{1,0},{2,3},{3,2},{4,5},{5,4},{6,7},{7,6},{8,9},{9,8},{10,11... | collective-permute-start | bytes 7688 | tf_op jit(solution)/shard_map/ppermute | solution.py:56
  15.9 1.1 collective-permute-start.11
  17.1 2.3 %collective-permute-start.9 = (bf16[16,128,128]{2,1,0:T(8,128)(2,1)S(1)}, bf16[16,128,128]{2,1,0:T(8,128)(2,1)S(1)}, u32[]{:S(2)}, u32[]{:S(2)}) collective-permute-start(bf16[16,128,128]{2,1,0:T(8,128)(2,1)S(1)} %get-tuple-element.65.rest_4_), channel_id=1, source_target_pairs={{0,16},{1,49},{2,18},{3,51},{4,20},{5,53},{6,22},{7,55},{8,24},{9,... | collective-permute-start | bytes 1572872 | tf_op jit(solution)/shard_map/ppermute | solution.py:56
  19.4 1.2 collective-permute-start.6
  20.7 0.8 collective-permute-done.11
  21.4 2.1 %collective-permute-start.4 = (bf16[16,128,128]{2,1,0:T(8,128)(2,1)S(1)}, bf16[16,128,128]{2,1,0:T(8,128)(2,1)S(1)}, u32[]{:S(2)}, u32[]{:S(2)}) collective-permute-start(bf16[16,128,128]{2,1,0:T(8,128)(2,1)S(1)} %get-tuple-element.66.rest_0_), channel_id=1, source_target_pairs={{0,2},{1,7},{2,0},{3,5},{4,6},{5,3},{6,4},{7,1},{8,10},{9,15},{10,... | collective-permute-start | bytes 1572872 | tf_op jit(solution)/shard_map/ppermute | solution.py:56
  23.6 1.4 collective-permute-done.6
  24.9 4.4 %collective-permute-start.12 = (bf16[16,128,128]{2,1,0:T(8,128)(2,1)S(1)}, bf16[16,128,128]{2,1,0:T(8,128)(2,1)S(1)}, u32[]{:S(2)}, u32[]{:S(2)}) collective-permute-start(bf16[16,128,128]{2,1,0:T(8,128)(2,1)S(1)} %constant_dynamic-update-slice_fusion.2.rest_6_), channel_id=1, source_target_pairs={{0,16},{1,49},{2,18},{3,51},{4,20},{5,53},{6,22},{7,55},{8,24},{9,... | collective-permute-start | bytes 1572872 | tf_op jit(solution)/shard_map/ppermute | solution.py:56
  29.4 1.5 collective-permute-start.7
  30.9 0.6 add_select_fusion.5
  31.6 0.5 slice.142
  32.1 1.3 pad_add_fusion.5.count_ref
  33.4 0.7 add_select_fusion.4
  34.1 1.8 %collective-permute-done.12.rest_7_ = bf16[16,128,128]{2,1,0:T(8,128)(2,1)S(1)} collective-permute-done((bf16[16,128,128]{2,1,0:T(8,128)(2,1)S(1)}, bf16[16,128,128]{2,1,0:T(8,128)(2,1)S(1)}, u32[]{:S(2)}, u32[]{:S(2)}) %collective-permute-start.12) | collective-permute-done | bytes 524320 | tf_op jit(solution)/shard_map/ppermute | solution.py:56
  36.0 3.2 %collective-permute-done.7.rest_3_ = bf16[16,128,128]{2,1,0:T(8,128)(2,1)S(1)} collective-permute-done((bf16[16,128,128]{2,1,0:T(8,128)(2,1)S(1)}, bf16[16,128,128]{2,1,0:T(8,128)(2,1)S(1)}, u32[]{:S(2)}, u32[]{:S(2)}) %collective-permute-start.7) | collective-permute-done | bytes 524320 | tf_op jit(solution)/shard_map/ppermute | solution.py:56
  39.1 8.4 %shard_map.73 = (bf16[16,128,128]{2,1,0:T(8,128)(2,1)S(1)}, bf16[16,128,128]{2,1,0:T(8,128)(2,1)S(1)}, f32[16,128,128]{2,1,0:T(8,128)S(1)}, f32[16,128,128]{2,1,...) custom-call(s32[512]{0:T(512)S(1)} %get-tuple-element.79.row_tile_re, ...), custom_call_target="tpu_custom_call" | custom-call | flops 4294967296 | bytes 27262976 | tf_op jit(solution)/shard_map/pallas_call | solution.py:158
  47.5 2.7 %collective-permute-start.13 = (bf16[16,128,128]{2,1,0:T(8,128)(2,1)S(1)}, bf16[16,128,128]{2,1,0:T(8,128)(2,1)S(1)}, u32[]{:S(2)}, u32[]{:S(2)}) collective-permute-start(bf16[16,128,128]{2,1,0:T(8,128)(2,1)S(1)} %get-tuple-element.36), channel_id=1, source_target_pairs={{0,2},{1,7},{2,0},{3,5},{4,6},{5,3},{6,4},{7,1},{8,10},{9,15},{10,... | collective-permute-start | bytes 1572872 | tf_op jit(solution)/shard_map/ppermute | solution.py:56
  50.2 3.8 %collective-permute-start.18 = (bf16[16,128,128]{2,1,0:T(8,128)(2,1)S(1)}, bf16[16,128,128]{2,1,0:T(8,128)(2,1)S(1)}, u32[]{:S(2)}, u32[]{:S(2)}) collective-permute-start(bf16[16,128,128]{2,1,0:T(8,128)(2,1)S(1)} %get-tuple-element.42), channel_id=1, source_target_pairs={{0,16},{1,49},{2,18},{3,51},{4,20},{5,53},{6,22},{7,55},{8,24},{9,... | collective-permute-start | bytes 1572872 | tf_op jit(solution)/shard_map/ppermute | solution.py:56
  54.0 2.9 %collective-permute-done.13 = bf16[16,128,128]{2,1,0:T(8,128)(2,1)S(1)} collective-permute-done((bf16[16,128,128]{2,1,0:T(8,128)(2,1)S(1)}, bf16[16,128,128]{2,1,0:T(8,128)(2,1)S(1)}, u32[]{:S(2)}, u32[]{:S(2)}) %collective-permute-start.13) | collective-permute-done | bytes 524320 | tf_op jit(solution)/shard_map/ppermute | solution.py:56
  57.0 2.7 %collective-permute-start.14 = (bf16[16,128,128]{2,1,0:T(8,128)(2,1)S(1)}, bf16[16,128,128]{2,1,0:T(8,128)(2,1)S(1)}, u32[]{:S(2)}, u32[]{:S(2)}) collective-permute-start(bf16[16,128,128]{2,1,0:T(8,128)(2,1)S(1)} %get-tuple-element.38), channel_id=1, source_target_pairs={{0,2},{1,7},{2,0},{3,5},{4,6},{5,3},{6,4},{7,1},{8,10},{9,15},{10,... | collective-permute-start | bytes 1572872 | tf_op jit(solution)/shard_map/ppermute | solution.py:56
  59.7 0.9 collective-permute-done.18
  60.7 3.0 %collective-permute-start.19 = (bf16[16,128,128]{2,1,0:T(8,128)(2,1)S(1)}, bf16[16,128,128]{2,1,0:T(8,128)(2,1)S(1)}, u32[]{:S(2)}, u32[]{:S(2)}) collective-permute-start(bf16[16,128,128]{2,1,0:T(8,128)(2,1)S(1)} %get-tuple-element.44), channel_id=1, source_target_pairs={{0,16},{1,49},{2,18},{3,51},{4,20},{5,53},{6,22},{7,55},{8,24},{9,... | collective-permute-start | bytes 1572872 | tf_op jit(solution)/shard_map/ppermute | solution.py:56
  63.8 1.6 collective-permute-start.16
  65.4 0.8 collective-permute-done.20
  66.3 1.0 collective-permute-start.21
  67.3 1.4 collective-permute-done.14
  68.7 1.6 collective-permute-start.17
  70.3 3.0 %collective-permute-done.19 = bf16[16,128,128]{2,1,0:T(8,128)(2,1)S(1)} collective-permute-done((bf16[16,128,128]{2,1,0:T(8,128)(2,1)S(1)}, bf16[16,128,128]{2,1,0:T(8,128)(2,1)S(1)}, u32[]{:S(2)}, u32[]{:S(2)}) %collective-permute-start.19) | collective-permute-done | bytes 524320 | tf_op jit(solution)/shard_map/ppermute | solution.py:56
  73.3 1.0 collective-permute-start.22
  75.6 3.3 %collective-permute-done.22 = bf16[8,128,128]{2,1,0:T(8,128)(2,1)S(1)} collective-permute-done((bf16[8,128,128]{2,1,0:T(8,128)(2,1)S(1)}, bf16[8,128,128]{2,1,0:T(8,128)(2,1)S(1)}, u32[]{:S(2)}, u32[]{:S(2)}) %collective-permute-start.22) | collective-permute-done | bytes 262176 | tf_op jit(solution)/shard_map/ppermute | solution.py:56
  79.3 0.8 collective-permute-start.30
  80.0 2.1 %collective-permute-start.28 = (bf16[8,128,128]{2,1,0:T(8,128)(2,1)S(1)}, bf16[8,128,128]{2,1,0:T(8,128)(2,1)S(1)}, u32[]{:S(2)}, u32[]{:S(2)}) collective-permute-start(bf16[8,128,128]{2,1,0:T(8,128)(2,1)S(1)} %get-tuple-element.59), channel_id=1, source_target_pairs={{0,16},{1,49},{2,18},{3,51},{4,20},{5,53},{6,22},{7,55},{8,24},{9,... | collective-permute-start | bytes 786440 | tf_op jit(solution)/shard_map/ppermute | solution.py:56
  82.2 1.3 collective-permute-start.23
  83.5 2.9 %collective-permute-start.25 = (bf16[8,128,128]{2,1,0:T(8,128)(2,1)S(1)}, bf16[8,128,128]{2,1,0:T(8,128)(2,1)S(1)}, u32[]{:S(2)}, u32[]{:S(2)}) collective-permute-start(bf16[8,128,128]{2,1,0:T(8,128)(2,1)S(1)} %get-tuple-element.59), channel_id=1, source_target_pairs={{0,8},{1,9},{2,10},{3,11},{4,12},{5,13},{6,14},{7,15},{8,0},{9,1},... | collective-permute-start | bytes 786440 | tf_op jit(solution)/shard_map/ppermute | solution.py:56
  86.4 2.4 %collective-permute-start.31 = (bf16[8,128,128]{2,1,0:T(8,128)(2,1)S(1)}, bf16[8,128,128]{2,1,0:T(8,128)(2,1)S(1)}, u32[]{:S(2)}, u32[]{:S(2)}) collective-permute-start(bf16[8,128,128]{2,1,0:T(8,128)(2,1)S(1)} %collective-permute-done.30), channel_id=1, source_target_pairs={{0,16},{1,49},{2,18},{3,51},{4,20},{5,53},{6,22},{7,55},{8,24},{9,... | collective-permute-start | bytes 786440 | tf_op jit(solution)/shard_map/ppermute | solution.py:56
  88.9 0.7 collective-permute-start.29
  89.5 0.8 collective-permute-start.24
  90.3 1.3 collective-permute-done.25
  91.7 1.4 collective-permute-done.31
  93.3 4.8 %collective-permute-done.26 = bf16[8,128,128]{2,1,0:T(8,128)(2,1)S(1)} collective-permute-done((bf16[8,128,128]{2,1,0:T(8,128)(2,1)S(1)}, bf16[8,128,128]{2,1,0:T(8,128)(2,1)S(1)}, u32[]{:S(2)}, u32[]{:S(2)}) %collective-permute-start.26) | collective-permute-done | bytes 262176 | tf_op jit(solution)/shard_map/ppermute | solution.py:56
  98.2 1.8 %collective-permute-done.29.rest_5_ = bf16[16,128,128]{2,1,0:T(8,128)(2,1)S(1)} collective-permute-done((bf16[16,128,128]{2,1,0:T(8,128)(2,1)S(1)}, bf16[16,128,128]{2,1,0:T(8,128)(2,1)S(1)}, u32[]{:S(2)}, u32[]{:S(2)}) %collective-permute-start.29) | collective-permute-done | bytes 524320 | tf_op jit(solution)/shard_map/ppermute | solution.py:56
  100.0 7.1 %collective-permute-done.32.rest_7_ = bf16[16,128,128]{2,1,0:T(8,128)(2,1)S(1)} collective-permute-done((bf16[16,128,128]{2,1,0:T(8,128)(2,1)S(1)}, bf16[16,128,128]{2,1,0:T(8,128)(2,1)S(1)}, u32[]{:S(2)}, u32[]{:S(2)}) %collective-permute-start.32) | collective-permute-done | bytes 524320 | tf_op jit(solution)/shard_map/ppermute | solution.py:56
  107.1 8.4 %shard_map.74 = (bf16[16,128,128]{2,1,0:T(8,128)(2,1)S(1)}, bf16[16,128,128]{2,1,0:T(8,128)(2,1)S(1)}, f32[16,128,128]{2,1,0:T(8,128)S(1)}, f32[16,128,128]{2,1,...) custom-call(s32[512]{0:T(512)S(1)} %get-tuple-element.77.row_tile_re, ...), custom_call_target="tpu_custom_call" | custom-call | flops 4294967296 | bytes 27262976 | tf_op jit(solution)/shard_map/pallas_call | solution.py:158
  115.7 7.9 %collective-permute-done.33 = bf16[16,128,128]{2,1,0:T(8,128)(2,1)S(1)} collective-permute-done((bf16[16,128,128]{2,1,0:T(8,128)(2,1)S(1)}, bf16[16,128,128]{2,1,0:T(8,128)(2,1)S(1)}, u32[]{:S(2)}, u32[]{:S(2)}) %collective-permute-start.33) | collective-permute-done | bytes 524320 | tf_op jit(solution)/shard_map/ppermute | solution.py:56
  123.7 3.3 %collective-permute-start.35 = (bf16[8,128,128]{2,1,0:T(8,128)(2,1)S(1)}, bf16[8,128,128]{2,1,0:T(8,128)(2,1)S(1)}, u32[]{:S(2)}, u32[]{:S(2)}) collective-permute-start(bf16[8,128,128]{2,1,0:T(8,128)(2,1)S(1)} %add_convert_fusion.5), channel_id=1, source_target_pairs={{0,2},{1,7},{2,0},{3,5},{4,6},{5,3},{6,4},{7,1},{8,10},{9,15},{10,... | collective-permute-start | bytes 786440 | tf_op jit(solution)/shard_map/ppermute | solution.py:56
  127.1 1.4 collective-permute-start.40
  128.5 2.3 %collective-permute-done.35 = bf16[8,128,128]{2,1,0:T(8,128)(2,1)S(1)} collective-permute-done((bf16[8,128,128]{2,1,0:T(8,128)(2,1)S(1)}, bf16[8,128,128]{2,1,0:T(8,128)(2,1)S(1)}, u32[]{:S(2)}, u32[]{:S(2)}) %collective-permute-start.35) | collective-permute-done | bytes 262176 | tf_op jit(solution)/shard_map/ppermute | solution.py:56
  130.9 2.1 %collective-permute-start.36 = (bf16[8,128,128]{2,1,0:T(8,128)(2,1)S(1)}, bf16[8,128,128]{2,1,0:T(8,128)(2,1)S(1)}, u32[]{:S(2)}, u32[]{:S(2)}) collective-permute-start(bf16[8,128,128]{2,1,0:T(8,128)(2,1)S(1)} %add_convert_fusion.4), channel_id=1, source_target_pairs={{0,8},{1,9},{2,10},{3,11},{4,12},{5,13},{6,14},{7,15},{8,0},{9,1},... | collective-permute-start | bytes 786440 | tf_op jit(solution)/shard_map/ppermute | solution.py:56
  133.0 0.6 collective-permute-done.40
  133.7 4.3 %collective-permute-start.41 = (bf16[8,128,128]{2,1,0:T(8,128)(2,1)S(1)}, bf16[8,128,128]{2,1,0:T(8,128)(2,1)S(1)}, u32[]{:S(2)}, u32[]{:S(2)}) collective-permute-start(bf16[8,128,128]{2,1,0:T(8,128)(2,1)S(1)} %add_convert_fusion.1), channel_id=1, source_target_pairs={{0,64},{1,65},{2,66},{3,67},{4,68},{5,69},{6,70},{7,71},{8,72},{9,... | collective-permute-start | bytes 786440 | tf_op jit(solution)/shard_map/ppermute | solution.py:56
  138.1 2.1 %collective-permute-start.37 = (bf16[8,128,128]{2,1,0:T(8,128)(2,1)S(1)}, bf16[8,128,128]{2,1,0:T(8,128)(2,1)S(1)}, u32[]{:S(2)}, u32[]{:S(2)}) collective-permute-start(bf16[8,128,128]{2,1,0:T(8,128)(2,1)S(1)} %add_convert_fusion.3), channel_id=1, source_target_pairs={{0,2},{1,7},{2,0},{3,5},{4,6},{5,3},{6,4},{7,1},{8,10},{9,15},{10,... | collective-permute-start | bytes 786440 | tf_op jit(solution)/shard_map/ppermute | solution.py:56
  140.4 4.1 %collective-permute-done.41 = bf16[8,128,128]{2,1,0:T(8,128)(2,1)S(1)} collective-permute-done((bf16[8,128,128]{2,1,0:T(8,128)(2,1)S(1)}, bf16[8,128,128]{2,1,0:T(8,128)(2,1)S(1)}, u32[]{:S(2)}, u32[]{:S(2)}) %collective-permute-start.41) | collective-permute-done | bytes 262176 | tf_op jit(solution)/shard_map/ppermute | solution.py:56
  144.6 2.4 %collective-permute-done.42 = bf16[8,128,128]{2,1,0:T(8,128)(2,1)S(1)} collective-permute-done((bf16[8,128,128]{2,1,0:T(8,128)(2,1)S(1)}, bf16[8,128,128]{2,1,0:T(8,128)(2,1)S(1)}, u32[]{:S(2)}, u32[]{:S(2)}) %collective-permute-start.42) | collective-permute-done | bytes 262176 | tf_op jit(solution)/shard_map/ppermute | solution.py:56
  147.6 13.5 %collective-permute-start.43 = (f32[512,128]{1,0:T(8,128)S(1)}, f32[512,128]{1,0:T(8,128)S(1)}, u32[]{:S(2)}, u32[]{:S(2)}) collective-permute-start(f32[512,128]{1,0:T(8,128)S(1)} %get-tuple-element.62), channel_id=1, source_target_pairs={{0,1},{1,0},{2,3},{3,2},{4,5},{5,4},{6,7},{7,6},{8,9},{9,8},{10,11... | collective-permute-start | bytes 786440 | tf_op jit(solution)/shard_map/ppermute | solution.py:56
  161.1 1.2 collective-permute-done.43
  162.2 0.8 maximum_select_fusion
  (64 shorter events, 3.4 us)
Async XLA Ops:
  1.0 2.9 %collective-permute-start = (bf16[512,128]{1,0:T(8,128)(2,1)S(1)}, bf16[512,128]{1,0:T(8,128)(2,1)S(1)}, u32[]{:S(2)}, u32[]{:S(2)}) collective-permute-start(bf16[512,128]{1,0:T(8,128)(2,1)S(1)} %get-tuple-element.68), channel_id=1, source_target_pairs={{0,1},{1,0},{2,3},{3,2},{4,5},{5,4},{6,7},{7,6},{8,9},{9,8},{10,11... | collective-permute-start | bytes 393224 | tf_op jit(solution)/shard_map/ppermute | solution.py:56
  3.9 35.2 %collective-permute-start.2 = (bf16[256,128,128]{2,1,0:T(8,128)(2,1)}, bf16[256,128,128]{2,1,0:T(8,128)(2,1)}, u32[]{:S(2)}, u32[]{:S(2)}) collective-permute-start(bf16[256,128,128]{2,1,0:T(8,128)(2,1)} %bitcast.14), channel_id=1, source_target_pairs={{0,1},{1,0},{2,3},{3,2},{4,5},{5,4},{6,7},{7,6},{8,9},{9,8},{10,11... | collective-permute-start | bytes 25165832 | tf_op jit(solution)/shard_map/ppermute | solution.py:56
  4.0 9.0 %collective-permute-start.10 = (bf16[8,128,128]{2,1,0:T(8,128)(2,1)S(1)}, bf16[8,128,128]{2,1,0:T(8,128)(2,1)S(1)}, u32[]{:S(2)}, u32[]{:S(2)}) collective-permute-start(bf16[8,128,128]{2,1,0:T(8,128)(2,1)S(1)} %bitcast.17), channel_id=1, source_target_pairs={{0,64},{1,65},{2,66},{3,67},{4,68},{5,69},{6,70},{7,71},{8,72},{9,... | collective-permute-start | bytes 786440 | tf_op jit(solution)/shard_map/ppermute | solution.py:56
  7.1 8.8 %collective-permute-start.8 = (bf16[8,128,128]{2,1,0:T(8,128)(2,1)S(1)}, bf16[8,128,128]{2,1,0:T(8,128)(2,1)S(1)}, u32[]{:S(2)}, u32[]{:S(2)}) collective-permute-start(bf16[8,128,128]{2,1,0:T(8,128)(2,1)S(1)} %bitcast.18), channel_id=1, source_target_pairs={{0,48},{1,17},{2,50},{3,19},{4,52},{5,21},{6,54},{7,23},{8,56},{9,... | collective-permute-start | bytes 786440 | tf_op jit(solution)/shard_map/ppermute | solution.py:56
  8.8 8.3 %collective-permute-start.3 = (bf16[8,128,128]{2,1,0:T(8,128)(2,1)S(1)}, bf16[8,128,128]{2,1,0:T(8,128)(2,1)S(1)}, u32[]{:S(2)}, u32[]{:S(2)}) collective-permute-start(bf16[8,128,128]{2,1,0:T(8,128)(2,1)S(1)} %bitcast.19), channel_id=1, source_target_pairs={{0,6},{1,3},{2,4},{3,1},{4,2},{5,7},{6,0},{7,5},{8,14},{9,11},{10,... | collective-permute-start | bytes 786440 | tf_op jit(solution)/shard_map/ppermute | solution.py:56
  10.0 9.5 %collective-permute-start.5 = (bf16[8,128,128]{2,1,0:T(8,128)(2,1)S(1)}, bf16[8,128,128]{2,1,0:T(8,128)(2,1)S(1)}, u32[]{:S(2)}, u32[]{:S(2)}) collective-permute-start(bf16[8,128,128]{2,1,0:T(8,128)(2,1)S(1)} %bitcast.20), channel_id=1, source_target_pairs={{0,8},{1,9},{2,10},{3,11},{4,12},{5,13},{6,14},{7,15},{8,0},{9,1},... | collective-permute-start | bytes 786440 | tf_op jit(solution)/shard_map/ppermute | solution.py:56
  13.1 16.3 %collective-permute-start.1 = (s32[640]{0:T(1024)S(1)}, s32[640]{0:T(1024)S(1)}, u32[]{:S(2)}, u32[]{:S(2)}) collective-permute-start(s32[640]{0:T(1024)S(1)} %pad_add_fusion), channel_id=1, source_target_pairs={{0,1},{1,0},{2,3},{3,2},{4,5},{5,4},{6,7},{7,6},{8,9},{9,8},{10,11... | collective-permute-start | bytes 7688 | tf_op jit(solution)/shard_map/ppermute | solution.py:56
  15.9 5.5 %collective-permute-start.11 = (bf16[8,128,128]{2,1,0:T(8,128)(2,1)S(1)}, bf16[8,128,128]{2,1,0:T(8,128)(2,1)S(1)}, u32[]{:S(2)}, u32[]{:S(2)}) collective-permute-start(bf16[8,128,128]{2,1,0:T(8,128)(2,1)S(1)} %collective-permute-done.10), channel_id=1, source_target_pairs={{0,48},{1,17},{2,50},{3,19},{4,52},{5,21},{6,54},{7,23},{8,56},{9,... | collective-permute-start | bytes 786440 | tf_op jit(solution)/shard_map/ppermute | solution.py:56
  17.1 17.0 %collective-permute-start.9 = (bf16[16,128,128]{2,1,0:T(8,128)(2,1)S(1)}, bf16[16,128,128]{2,1,0:T(8,128)(2,1)S(1)}, u32[]{:S(2)}, u32[]{:S(2)}) collective-permute-start(bf16[16,128,128]{2,1,0:T(8,128)(2,1)S(1)} %get-tuple-element.65.rest_4_), channel_id=1, source_target_pairs={{0,16},{1,49},{2,18},{3,51},{4,20},{5,53},{6,22},{7,55},{8,24},{9,... | collective-permute-start | bytes 1572872 | tf_op jit(solution)/shard_map/ppermute | solution.py:56
  19.4 5.5 %collective-permute-start.6 = (bf16[8,128,128]{2,1,0:T(8,128)(2,1)S(1)}, bf16[8,128,128]{2,1,0:T(8,128)(2,1)S(1)}, u32[]{:S(2)}, u32[]{:S(2)}) collective-permute-start(bf16[8,128,128]{2,1,0:T(8,128)(2,1)S(1)} %collective-permute-done.5), channel_id=1, source_target_pairs={{0,6},{1,3},{2,4},{3,1},{4,2},{5,7},{6,0},{7,5},{8,14},{9,11},{10,... | collective-permute-start | bytes 786440 | tf_op jit(solution)/shard_map/ppermute | solution.py:56
  21.4 12.7 %collective-permute-start.4 = (bf16[16,128,128]{2,1,0:T(8,128)(2,1)S(1)}, bf16[16,128,128]{2,1,0:T(8,128)(2,1)S(1)}, u32[]{:S(2)}, u32[]{:S(2)}) collective-permute-start(bf16[16,128,128]{2,1,0:T(8,128)(2,1)S(1)} %get-tuple-element.66.rest_0_), channel_id=1, source_target_pairs={{0,2},{1,7},{2,0},{3,5},{4,6},{5,3},{6,4},{7,1},{8,10},{9,15},{10,... | collective-permute-start | bytes 1572872 | tf_op jit(solution)/shard_map/ppermute | solution.py:56
  24.9 11.0 %collective-permute-start.12 = (bf16[16,128,128]{2,1,0:T(8,128)(2,1)S(1)}, bf16[16,128,128]{2,1,0:T(8,128)(2,1)S(1)}, u32[]{:S(2)}, u32[]{:S(2)}) collective-permute-start(bf16[16,128,128]{2,1,0:T(8,128)(2,1)S(1)} %constant_dynamic-update-slice_fusion.2.rest_6_), channel_id=1, source_target_pairs={{0,16},{1,49},{2,18},{3,51},{4,20},{5,53},{6,22},{7,55},{8,24},{9,... | collective-permute-start | bytes 1572872 | tf_op jit(solution)/shard_map/ppermute | solution.py:56
  29.4 9.7 %collective-permute-start.7 = (bf16[16,128,128]{2,1,0:T(8,128)(2,1)S(1)}, bf16[16,128,128]{2,1,0:T(8,128)(2,1)S(1)}, u32[]{:S(2)}, u32[]{:S(2)}) collective-permute-start(bf16[16,128,128]{2,1,0:T(8,128)(2,1)S(1)} %constant_dynamic-update-slice_fusion.rest_2_), channel_id=1, source_target_pairs={{0,2},{1,7},{2,0},{3,5},{4,6},{5,3},{6,4},{7,1},{8,10},{9,15},{10,... | collective-permute-start | bytes 1572872 | tf_op jit(solution)/shard_map/ppermute | solution.py:56
  47.5 9.3 %collective-permute-start.13 = (bf16[16,128,128]{2,1,0:T(8,128)(2,1)S(1)}, bf16[16,128,128]{2,1,0:T(8,128)(2,1)S(1)}, u32[]{:S(2)}, u32[]{:S(2)}) collective-permute-start(bf16[16,128,128]{2,1,0:T(8,128)(2,1)S(1)} %get-tuple-element.36), channel_id=1, source_target_pairs={{0,2},{1,7},{2,0},{3,5},{4,6},{5,3},{6,4},{7,1},{8,10},{9,15},{10,... | collective-permute-start | bytes 1572872 | tf_op jit(solution)/shard_map/ppermute | solution.py:56
  50.2 10.3 %collective-permute-start.18 = (bf16[16,128,128]{2,1,0:T(8,128)(2,1)S(1)}, bf16[16,128,128]{2,1,0:T(8,128)(2,1)S(1)}, u32[]{:S(2)}, u32[]{:S(2)}) collective-permute-start(bf16[16,128,128]{2,1,0:T(8,128)(2,1)S(1)} %get-tuple-element.42), channel_id=1, source_target_pairs={{0,16},{1,49},{2,18},{3,51},{4,20},{5,53},{6,22},{7,55},{8,24},{9,... | collective-permute-start | bytes 1572872 | tf_op jit(solution)/shard_map/ppermute | solution.py:56
  56.9 6.8 %collective-permute-start.15 = (bf16[8,128,128]{2,1,0:T(8,128)(2,1)S(1)}, bf16[8,128,128]{2,1,0:T(8,128)(2,1)S(1)}, u32[]{:S(2)}, u32[]{:S(2)}) collective-permute-start(bf16[8,128,128]{2,1,0:T(8,128)(2,1)S(1)} %add_convert_fusion.11), channel_id=1, source_target_pairs={{0,6},{1,3},{2,4},{3,1},{4,2},{5,7},{6,0},{7,5},{8,14},{9,11},{10,... | collective-permute-start | bytes 786440 | tf_op jit(solution)/shard_map/ppermute | solution.py:56
  57.0 11.7 %collective-permute-start.14 = (bf16[16,128,128]{2,1,0:T(8,128)(2,1)S(1)}, bf16[16,128,128]{2,1,0:T(8,128)(2,1)S(1)}, u32[]{:S(2)}, u32[]{:S(2)}) collective-permute-start(bf16[16,128,128]{2,1,0:T(8,128)(2,1)S(1)} %get-tuple-element.38), channel_id=1, source_target_pairs={{0,2},{1,7},{2,0},{3,5},{4,6},{5,3},{6,4},{7,1},{8,10},{9,15},{10,... | collective-permute-start | bytes 1572872 | tf_op jit(solution)/shard_map/ppermute | solution.py:56
  60.6 5.6 %collective-permute-start.20 = (bf16[8,128,128]{2,1,0:T(8,128)(2,1)S(1)}, bf16[8,128,128]{2,1,0:T(8,128)(2,1)S(1)}, u32[]{:S(2)}, u32[]{:S(2)}) collective-permute-start(bf16[8,128,128]{2,1,0:T(8,128)(2,1)S(1)} %add_convert_fusion.8), channel_id=1, source_target_pairs={{0,48},{1,17},{2,50},{3,19},{4,52},{5,21},{6,54},{7,23},{8,56},{9,... | collective-permute-start | bytes 786440 | tf_op jit(solution)/shard_map/ppermute | solution.py:56
  60.7 12.5 %collective-permute-start.19 = (bf16[16,128,128]{2,1,0:T(8,128)(2,1)S(1)}, bf16[16,128,128]{2,1,0:T(8,128)(2,1)S(1)}, u32[]{:S(2)}, u32[]{:S(2)}) collective-permute-start(bf16[16,128,128]{2,1,0:T(8,128)(2,1)S(1)} %get-tuple-element.44), channel_id=1, source_target_pairs={{0,16},{1,49},{2,18},{3,51},{4,20},{5,53},{6,22},{7,55},{8,24},{9,... | collective-permute-start | bytes 1572872 | tf_op jit(solution)/shard_map/ppermute | solution.py:56
  63.8 11.8 %collective-permute-start.16 = (bf16[8,128,128]{2,1,0:T(8,128)(2,1)S(1)}, bf16[8,128,128]{2,1,0:T(8,128)(2,1)S(1)}, u32[]{:S(2)}, u32[]{:S(2)}) collective-permute-start(bf16[8,128,128]{2,1,0:T(8,128)(2,1)S(1)} %add_convert_fusion.10), channel_id=1, source_target_pairs={{0,8},{1,9},{2,10},{3,11},{4,12},{5,13},{6,14},{7,15},{8,0},{9,1},... | collective-permute-start | bytes 786440 | tf_op jit(solution)/shard_map/ppermute | solution.py:56
  66.3 9.3 %collective-permute-start.21 = (bf16[8,128,128]{2,1,0:T(8,128)(2,1)S(1)}, bf16[8,128,128]{2,1,0:T(8,128)(2,1)S(1)}, u32[]{:S(2)}, u32[]{:S(2)}) collective-permute-start(bf16[8,128,128]{2,1,0:T(8,128)(2,1)S(1)} %add_convert_fusion.7), channel_id=1, source_target_pairs={{0,64},{1,65},{2,66},{3,67},{4,68},{5,69},{6,70},{7,71},{8,72},{9,... | collective-permute-start | bytes 786440 | tf_op jit(solution)/shard_map/ppermute | solution.py:56
  68.7 6.9 %collective-permute-start.17 = (bf16[8,128,128]{2,1,0:T(8,128)(2,1)S(1)}, bf16[8,128,128]{2,1,0:T(8,128)(2,1)S(1)}, u32[]{:S(2)}, u32[]{:S(2)}) collective-permute-start(bf16[8,128,128]{2,1,0:T(8,128)(2,1)S(1)} %add_convert_fusion.9), channel_id=1, source_target_pairs={{0,6},{1,3},{2,4},{3,1},{4,2},{5,7},{6,0},{7,5},{8,14},{9,11},{10,... | collective-permute-start | bytes 786440 | tf_op jit(solution)/shard_map/ppermute | solution.py:56
  73.3 5.6 %collective-permute-start.22 = (bf16[8,128,128]{2,1,0:T(8,128)(2,1)S(1)}, bf16[8,128,128]{2,1,0:T(8,128)(2,1)S(1)}, u32[]{:S(2)}, u32[]{:S(2)}) collective-permute-start(bf16[8,128,128]{2,1,0:T(8,128)(2,1)S(1)} %add_convert_fusion.6), channel_id=1, source_target_pairs={{0,48},{1,17},{2,50},{3,19},{4,52},{5,21},{6,54},{7,23},{8,56},{9,... | collective-permute-start | bytes 786440 | tf_op jit(solution)/shard_map/ppermute | solution.py:56
  79.3 7.1 %collective-permute-start.30 = (bf16[8,128,128]{2,1,0:T(8,128)(2,1)S(1)}, bf16[8,128,128]{2,1,0:T(8,128)(2,1)S(1)}, u32[]{:S(2)}, u32[]{:S(2)}) collective-permute-start(bf16[8,128,128]{2,1,0:T(8,128)(2,1)S(1)} %get-tuple-element.59), channel_id=1, source_target_pairs={{0,64},{1,65},{2,66},{3,67},{4,68},{5,69},{6,70},{7,71},{8,72},{9,... | collective-permute-start | bytes 786440 | tf_op jit(solution)/shard_map/ppermute | solution.py:56
  80.0 8.7 %collective-permute-start.28 = (bf16[8,128,128]{2,1,0:T(8,128)(2,1)S(1)}, bf16[8,128,128]{2,1,0:T(8,128)(2,1)S(1)}, u32[]{:S(2)}, u32[]{:S(2)}) collective-permute-start(bf16[8,128,128]{2,1,0:T(8,128)(2,1)S(1)} %get-tuple-element.59), channel_id=1, source_target_pairs={{0,16},{1,49},{2,18},{3,51},{4,20},{5,53},{6,22},{7,55},{8,24},{9,... | collective-permute-start | bytes 786440 | tf_op jit(solution)/shard_map/ppermute | solution.py:56
  82.2 6.6 %collective-permute-start.23 = (bf16[8,128,128]{2,1,0:T(8,128)(2,1)S(1)}, bf16[8,128,128]{2,1,0:T(8,128)(2,1)S(1)}, u32[]{:S(2)}, u32[]{:S(2)}) collective-permute-start(bf16[8,128,128]{2,1,0:T(8,128)(2,1)S(1)} %get-tuple-element.59), channel_id=1, source_target_pairs={{0,2},{1,7},{2,0},{3,5},{4,6},{5,3},{6,4},{7,1},{8,10},{9,15},{10,... | collective-permute-start | bytes 786440 | tf_op jit(solution)/shard_map/ppermute | solution.py:56
  83.5 8.2 %collective-permute-start.25 = (bf16[8,128,128]{2,1,0:T(8,128)(2,1)S(1)}, bf16[8,128,128]{2,1,0:T(8,128)(2,1)S(1)}, u32[]{:S(2)}, u32[]{:S(2)}) collective-permute-start(bf16[8,128,128]{2,1,0:T(8,128)(2,1)S(1)} %get-tuple-element.59), channel_id=1, source_target_pairs={{0,8},{1,9},{2,10},{3,11},{4,12},{5,13},{6,14},{7,15},{8,0},{9,1},... | collective-permute-start | bytes 786440 | tf_op jit(solution)/shard_map/ppermute | solution.py:56
  86.4 6.7 %collective-permute-start.31 = (bf16[8,128,128]{2,1,0:T(8,128)(2,1)S(1)}, bf16[8,128,128]{2,1,0:T(8,128)(2,1)S(1)}, u32[]{:S(2)}, u32[]{:S(2)}) collective-permute-start(bf16[8,128,128]{2,1,0:T(8,128)(2,1)S(1)} %collective-permute-done.30), channel_id=1, source_target_pairs={{0,16},{1,49},{2,18},{3,51},{4,20},{5,53},{6,22},{7,55},{8,24},{9,... | collective-permute-start | bytes 786440 | tf_op jit(solution)/shard_map/ppermute | solution.py:56
  88.9 11.1 %collective-permute-start.29 = (bf16[16,128,128]{2,1,0:T(8,128)(2,1)S(1)}, bf16[16,128,128]{2,1,0:T(8,128)(2,1)S(1)}, u32[]{:S(2)}, u32[]{:S(2)}) collective-permute-start(bf16[16,128,128]{2,1,0:T(8,128)(2,1)S(1)} %get-tuple-element.63.rest_4_), channel_id=1, source_target_pairs={{0,48},{1,17},{2,50},{3,19},{4,52},{5,21},{6,54},{7,23},{8,56},{9,... | collective-permute-start | bytes 1572872 | tf_op jit(solution)/shard_map/ppermute | solution.py:56
  89.5 10.5 %collective-permute-start.24 = (bf16[16,128,128]{2,1,0:T(8,128)(2,1)S(1)}, bf16[16,128,128]{2,1,0:T(8,128)(2,1)S(1)}, u32[]{:S(2)}, u32[]{:S(2)}) collective-permute-start(bf16[16,128,128]{2,1,0:T(8,128)(2,1)S(1)} %get-tuple-element.64.rest_0_), channel_id=1, source_target_pairs={{0,6},{1,3},{2,4},{3,1},{4,2},{5,7},{6,0},{7,5},{8,14},{9,11},{10,... | collective-permute-start | bytes 1572872 | tf_op jit(solution)/shard_map/ppermute | solution.py:56
  91.6 6.4 %collective-permute-start.26 = (bf16[8,128,128]{2,1,0:T(8,128)(2,1)S(1)}, bf16[8,128,128]{2,1,0:T(8,128)(2,1)S(1)}, u32[]{:S(2)}, u32[]{:S(2)}) collective-permute-start(bf16[8,128,128]{2,1,0:T(8,128)(2,1)S(1)} %collective-permute-done.25), channel_id=1, source_target_pairs={{0,2},{1,7},{2,0},{3,5},{4,6},{5,3},{6,4},{7,1},{8,10},{9,15},{10,... | collective-permute-start | bytes 786440 | tf_op jit(solution)/shard_map/ppermute | solution.py:56
  93.2 14.0 %collective-permute-start.32 = (bf16[16,128,128]{2,1,0:T(8,128)(2,1)S(1)}, bf16[16,128,128]{2,1,0:T(8,128)(2,1)S(1)}, u32[]{:S(2)}, u32[]{:S(2)}) collective-permute-start(bf16[16,128,128]{2,1,0:T(8,128)(2,1)S(1)} %constant_dynamic-update-slice_fusion.6.rest_6_), channel_id=1, source_target_pairs={{0,48},{1,17},{2,50},{3,19},{4,52},{5,21},{6,54},{7,23},{8,56},{9,... | collective-permute-start | bytes 1572872 | tf_op jit(solution)/shard_map/ppermute | solution.py:56
  98.1 9.0 %collective-permute-start.27 = (bf16[16,128,128]{2,1,0:T(8,128)(2,1)S(1)}, bf16[16,128,128]{2,1,0:T(8,128)(2,1)S(1)}, u32[]{:S(2)}, u32[]{:S(2)}) collective-permute-start(bf16[16,128,128]{2,1,0:T(8,128)(2,1)S(1)} %constant_dynamic-update-slice_fusion.4.rest_2_), channel_id=1, source_target_pairs={{0,6},{1,3},{2,4},{3,1},{4,2},{5,7},{6,0},{7,5},{8,14},{9,11},{10,... | collective-permute-start | bytes 1572872 | tf_op jit(solution)/shard_map/ppermute | solution.py:56
  115.6 8.1 %collective-permute-start.33 = (bf16[16,128,128]{2,1,0:T(8,128)(2,1)S(1)}, bf16[16,128,128]{2,1,0:T(8,128)(2,1)S(1)}, u32[]{:S(2)}, u32[]{:S(2)}) collective-permute-start(bf16[16,128,128]{2,1,0:T(8,128)(2,1)S(1)} %get-tuple-element.48), channel_id=1, source_target_pairs={{0,6},{1,3},{2,4},{3,1},{4,2},{5,7},{6,0},{7,5},{8,14},{9,11},{10,... | collective-permute-start | bytes 1572872 | tf_op jit(solution)/shard_map/ppermute | solution.py:56
  115.6 11.4 %collective-permute-start.38 = (bf16[16,128,128]{2,1,0:T(8,128)(2,1)S(1)}, bf16[16,128,128]{2,1,0:T(8,128)(2,1)S(1)}, u32[]{:S(2)}, u32[]{:S(2)}) collective-permute-start(bf16[16,128,128]{2,1,0:T(8,128)(2,1)S(1)} %get-tuple-element.54), channel_id=1, source_target_pairs={{0,48},{1,17},{2,50},{3,19},{4,52},{5,21},{6,54},{7,23},{8,56},{9,... | collective-permute-start | bytes 1572872 | tf_op jit(solution)/shard_map/ppermute | solution.py:56
  123.7 7.1 %collective-permute-start.35 = (bf16[8,128,128]{2,1,0:T(8,128)(2,1)S(1)}, bf16[8,128,128]{2,1,0:T(8,128)(2,1)S(1)}, u32[]{:S(2)}, u32[]{:S(2)}) collective-permute-start(bf16[8,128,128]{2,1,0:T(8,128)(2,1)S(1)} %add_convert_fusion.5), channel_id=1, source_target_pairs={{0,2},{1,7},{2,0},{3,5},{4,6},{5,3},{6,4},{7,1},{8,10},{9,15},{10,... | collective-permute-start | bytes 786440 | tf_op jit(solution)/shard_map/ppermute | solution.py:56
  127.0 11.0 %collective-permute-start.34 = (bf16[16,128,128]{2,1,0:T(8,128)(2,1)S(1)}, bf16[16,128,128]{2,1,0:T(8,128)(2,1)S(1)}, u32[]{:S(2)}, u32[]{:S(2)}) collective-permute-start(bf16[16,128,128]{2,1,0:T(8,128)(2,1)S(1)} %get-tuple-element.50), channel_id=1, source_target_pairs={{0,6},{1,3},{2,4},{3,1},{4,2},{5,7},{6,0},{7,5},{8,14},{9,11},{10,... | collective-permute-start | bytes 1572872 | tf_op jit(solution)/shard_map/ppermute | solution.py:56
  127.1 6.5 %collective-permute-start.40 = (bf16[8,128,128]{2,1,0:T(8,128)(2,1)S(1)}, bf16[8,128,128]{2,1,0:T(8,128)(2,1)S(1)}, u32[]{:S(2)}, u32[]{:S(2)}) collective-permute-start(bf16[8,128,128]{2,1,0:T(8,128)(2,1)S(1)} %add_convert_fusion.2), channel_id=1, source_target_pairs={{0,16},{1,49},{2,18},{3,51},{4,20},{5,53},{6,22},{7,55},{8,24},{9,... | collective-permute-start | bytes 786440 | tf_op jit(solution)/shard_map/ppermute | solution.py:56
  128.4 11.8 %collective-permute-start.39 = (bf16[16,128,128]{2,1,0:T(8,128)(2,1)S(1)}, bf16[16,128,128]{2,1,0:T(8,128)(2,1)S(1)}, u32[]{:S(2)}, u32[]{:S(2)}) collective-permute-start(bf16[16,128,128]{2,1,0:T(8,128)(2,1)S(1)} %get-tuple-element.56), channel_id=1, source_target_pairs={{0,48},{1,17},{2,50},{3,19},{4,52},{5,21},{6,54},{7,23},{8,56},{9,... | collective-permute-start | bytes 1572872 | tf_op jit(solution)/shard_map/ppermute | solution.py:56
  130.9 9.5 %collective-permute-start.36 = (bf16[8,128,128]{2,1,0:T(8,128)(2,1)S(1)}, bf16[8,128,128]{2,1,0:T(8,128)(2,1)S(1)}, u32[]{:S(2)}, u32[]{:S(2)}) collective-permute-start(bf16[8,128,128]{2,1,0:T(8,128)(2,1)S(1)} %add_convert_fusion.4), channel_id=1, source_target_pairs={{0,8},{1,9},{2,10},{3,11},{4,12},{5,13},{6,14},{7,15},{8,0},{9,1},... | collective-permute-start | bytes 786440 | tf_op jit(solution)/shard_map/ppermute | solution.py:56
  133.7 10.7 %collective-permute-start.41 = (bf16[8,128,128]{2,1,0:T(8,128)(2,1)S(1)}, bf16[8,128,128]{2,1,0:T(8,128)(2,1)S(1)}, u32[]{:S(2)}, u32[]{:S(2)}) collective-permute-start(bf16[8,128,128]{2,1,0:T(8,128)(2,1)S(1)} %add_convert_fusion.1), channel_id=1, source_target_pairs={{0,64},{1,65},{2,66},{3,67},{4,68},{5,69},{6,70},{7,71},{8,72},{9,... | collective-permute-start | bytes 786440 | tf_op jit(solution)/shard_map/ppermute | solution.py:56
  138.1 6.5 %collective-permute-start.37 = (bf16[8,128,128]{2,1,0:T(8,128)(2,1)S(1)}, bf16[8,128,128]{2,1,0:T(8,128)(2,1)S(1)}, u32[]{:S(2)}, u32[]{:S(2)}) collective-permute-start(bf16[8,128,128]{2,1,0:T(8,128)(2,1)S(1)} %add_convert_fusion.3), channel_id=1, source_target_pairs={{0,2},{1,7},{2,0},{3,5},{4,6},{5,3},{6,4},{7,1},{8,10},{9,15},{10,... | collective-permute-start | bytes 786440 | tf_op jit(solution)/shard_map/ppermute | solution.py:56
  140.3 6.8 %collective-permute-start.42 = (bf16[8,128,128]{2,1,0:T(8,128)(2,1)S(1)}, bf16[8,128,128]{2,1,0:T(8,128)(2,1)S(1)}, u32[]{:S(2)}, u32[]{:S(2)}) collective-permute-start(bf16[8,128,128]{2,1,0:T(8,128)(2,1)S(1)} %add_convert_fusion), channel_id=1, source_target_pairs={{0,16},{1,49},{2,18},{3,51},{4,20},{5,53},{6,22},{7,55},{8,24},{9,... | collective-permute-start | bytes 786440 | tf_op jit(solution)/shard_map/ppermute | solution.py:56
  147.6 14.7 %collective-permute-start.43 = (f32[512,128]{1,0:T(8,128)S(1)}, f32[512,128]{1,0:T(8,128)S(1)}, u32[]{:S(2)}, u32[]{:S(2)}) collective-permute-start(f32[512,128]{1,0:T(8,128)S(1)} %get-tuple-element.62), channel_id=1, source_target_pairs={{0,1},{1,0},{2,3},{3,2},{4,5},{5,4},{6,7},{7,6},{8,9},{9,8},{10,11... | collective-permute-start | bytes 786440 | tf_op jit(solution)/shard_map/ppermute | solution.py:56

commit v4 on v3

--- a/solution.py
+++ b/solution.py
@@ -259,7 +259,7 @@
         own_tiles = tiles_of(table, core, core ^ row_flip, core ^ col_flip)
         mate_tiles = tiles_of(mate_table, 1 - core, core ^ row_flip, core ^ col_flip)
         row_tiles, col_tiles = (jnp.concatenate(pair) for pair in zip(own_tiles, mate_tiles))
-        col_parts, row_parts = gather(tiled, (col_plan, row_plan))
+        row_parts, col_parts = gather(tiled, (row_plan, col_plan))
         found = slot_products(row_tiles, col_tiles, counts, own, mate, row_parts, col_parts)
         applied = scatter_sum(*found[:4], row_plan) + scatter_sum(*found[4:], col_plan)
         shifted = applied.reshape(2 * seg, half) - center * current

time: 163 us -> 163 us (level)
  waiting for transfers between devices: 56.7 us -> 65 us
  Pallas kernels: 16.8 us -> 12.5 us
  starting transfers between devices: 79 us -> 74.9 us
    ppermute x44, waiting for transfers between devices: 56.7 us -> 65 us  [move(): return lax.ppermute(value, BOTH, table)]
    pallas_call x2, Pallas kernels: 16.8 us -> 12.5 us  [slot_products(): pl.pallas_call(slot_kernel, in_specs=[in_smem] * 3 + [anywhere] * 10, out...]
    ppermute x44, starting transfers between devices: 79 us -> 74.9 us  [move(): return lax.ppermute(value, BOTH, table)]
  transfers between devices with their start and end apart: 44 -> 44, of which waited for: 23 -> 26; matrix products, arithmetic and copies ran while one was open for 3% -> 3% of each run, Pallas kernels for 0% -> 0%
where the time goes in v4:
time: 163 us
  starting transfers between devices  74.9 us (46%)
  waiting for transfers between devices  65 us (40%)
  Pallas kernels  12.5 us (8%)
  other arithmetic  7.02 us (4%)
  between operations  2.29 us (1%)
    ppermute x44, starting transfers between devices, move(): return lax.ppermute(value, BOTH, table)  74.9 us
    ppermute x44, waiting for transfers between devices, move(): return lax.ppermute(value, BOTH, table)  65 us
    pallas_call x2, Pallas kernels, slot_products(): pl.pallas_call(slot_kernel, in_specs=[in_smem] * 3 + [anywhere] * 10, out...  12.5 us
  transfers between devices with their start and end apart: 44, of which 26 were waited for; matrix products, arithmetic and copies ran while one was open for 3% of the time, Pallas kernels for 0%

profile of v4, /device:TPU:1, one launch (start us, length us, event | category | flops | bytes accessed | tf_op | source)
XLA Modules:
  0.0 162.9 jit_solution(123180524892460054)
XLA Ops:
  0.0 1.0 broadcast_select_fusion
  1.0 1.5 collective-permute-start
  3.2 0.7 pad_add_fusion
  4.0 3.1 %collective-permute-start.10 = (bf16[8,128,128]{2,1,0:T(8,128)(2,1)S(1)}, bf16[8,128,128]{2,1,0:T(8,128)(2,1)S(1)}, u32[]{:S(2)}, u32[]{:S(2)}) collective-permute-start(bf16[8,128,128]{2,1,0:T(8,128)(2,1)S(1)} %bitcast.17), channel_id=1, source_target_pairs={{0,64},{1,65},{2,66},{3,67},{4,68},{5,69},{6,70},{7,71},{8,72},{9,... | collective-permute-start | bytes 786440 | tf_op jit(solution)/shard_map/ppermute | solution.py:56
  7.1 1.6 %collective-permute-start.8 = (bf16[8,128,128]{2,1,0:T(8,128)(2,1)S(1)}, bf16[8,128,128]{2,1,0:T(8,128)(2,1)S(1)}, u32[]{:S(2)}, u32[]{:S(2)}) collective-permute-start(bf16[8,128,128]{2,1,0:T(8,128)(2,1)S(1)} %bitcast.18), channel_id=1, source_target_pairs={{0,48},{1,17},{2,50},{3,19},{4,52},{5,21},{6,54},{7,23},{8,56},{9,... | collective-permute-start | bytes 786440 | tf_op jit(solution)/shard_map/ppermute | solution.py:56
  8.8 1.2 collective-permute-start.3
  10.4 0.5 slice.140
  10.9 2.2 %collective-permute-done.10 = bf16[8,128,128]{2,1,0:T(8,128)(2,1)S(1)} collective-permute-done((bf16[8,128,128]{2,1,0:T(8,128)(2,1)S(1)}, bf16[8,128,128]{2,1,0:T(8,128)(2,1)S(1)}, u32[]{:S(2)}, u32[]{:S(2)}) %collective-permute-start.10) | collective-permute-done | bytes 262176 | tf_op jit(solution)/shard_map/ppermute | solution.py:56
  13.1 2.8 %collective-permute-start.1 = (s32[640]{0:T(1024)S(1)}, s32[640]{0:T(1024)S(1)}, u32[]{:S(2)}, u32[]{:S(2)}) collective-permute-start(s32[640]{0:T(1024)S(1)} %pad_add_fusion), channel_id=1, source_target_pairs={{0,1},{1,0},{2,3},{3,2},{4,5},{5,4},{6,7},{7,6},{8,9},{9,8},{10,11... | collective-permute-start | bytes 7688 | tf_op jit(solution)/shard_map/ppermute | solution.py:56
  15.9 1.1 collective-permute-start.11
  17.1 2.3 %collective-permute-start.9 = (bf16[16,128,128]{2,1,0:T(8,128)(2,1)S(1)}, bf16[16,128,128]{2,1,0:T(8,128)(2,1)S(1)}, u32[]{:S(2)}, u32[]{:S(2)}) collective-permute-start(bf16[16,128,128]{2,1,0:T(8,128)(2,1)S(1)} %get-tuple-element.65.rest_4_), channel_id=1, source_target_pairs={{0,16},{1,49},{2,18},{3,51},{4,20},{5,53},{6,22},{7,55},{8,24},{9,... | collective-permute-start | bytes 1572872 | tf_op jit(solution)/shard_map/ppermute | solution.py:56
  19.4 1.2 collective-permute-start.6
  20.7 0.8 collective-permute-done.11
  21.4 2.1 %collective-permute-start.4 = (bf16[16,128,128]{2,1,0:T(8,128)(2,1)S(1)}, bf16[16,128,128]{2,1,0:T(8,128)(2,1)S(1)}, u32[]{:S(2)}, u32[]{:S(2)}) collective-permute-start(bf16[16,128,128]{2,1,0:T(8,128)(2,1)S(1)} %get-tuple-element.66.rest_0_), channel_id=1, source_target_pairs={{0,2},{1,7},{2,0},{3,5},{4,6},{5,3},{6,4},{7,1},{8,10},{9,15},{10,... | collective-permute-start | bytes 1572872 | tf_op jit(solution)/shard_map/ppermute | solution.py:56
  23.6 1.4 collective-permute-done.6
  24.9 4.4 %collective-permute-start.12 = (bf16[16,128,128]{2,1,0:T(8,128)(2,1)S(1)}, bf16[16,128,128]{2,1,0:T(8,128)(2,1)S(1)}, u32[]{:S(2)}, u32[]{:S(2)}) collective-permute-start(bf16[16,128,128]{2,1,0:T(8,128)(2,1)S(1)} %constant_dynamic-update-slice_fusion.2.rest_6_), channel_id=1, source_target_pairs={{0,16},{1,49},{2,18},{3,51},{4,20},{5,53},{6,22},{7,55},{8,24},{9,... | collective-permute-start | bytes 1572872 | tf_op jit(solution)/shard_map/ppermute | solution.py:56
  29.4 1.5 collective-permute-start.7
  30.9 0.6 add_select_fusion.5
  31.6 0.5 slice.142
  32.1 1.3 pad_add_fusion.5.count_ref
  33.4 0.7 add_select_fusion.4
  34.1 1.8 %collective-permute-done.12.rest_7_ = bf16[16,128,128]{2,1,0:T(8,128)(2,1)S(1)} collective-permute-done((bf16[16,128,128]{2,1,0:T(8,128)(2,1)S(1)}, bf16[16,128,128]{2,1,0:T(8,128)(2,1)S(1)}, u32[]{:S(2)}, u32[]{:S(2)}) %collective-permute-start.12) | collective-permute-done | bytes 524320 | tf_op jit(solution)/shard_map/ppermute | solution.py:56
  36.0 3.2 %collective-permute-done.7.rest_3_ = bf16[16,128,128]{2,1,0:T(8,128)(2,1)S(1)} collective-permute-done((bf16[16,128,128]{2,1,0:T(8,128)(2,1)S(1)}, bf16[16,128,128]{2,1,0:T(8,128)(2,1)S(1)}, u32[]{:S(2)}, u32[]{:S(2)}) %collective-permute-start.7) | collective-permute-done | bytes 524320 | tf_op jit(solution)/shard_map/ppermute | solution.py:56
  39.1 6.2 %shard_map.73 = (bf16[16,128,128]{2,1,0:T(8,128)(2,1)S(1)}, bf16[16,128,128]{2,1,0:T(8,128)(2,1)S(1)}, f32[16,128,128]{2,1,0:T(8,128)S(1)}, f32[16,128,128]{2,1,...) custom-call(s32[512]{0:T(512)S(1)} %get-tuple-element.79.row_tile_re, ...), custom_call_target="tpu_custom_call" | custom-call | flops 4294967296 | bytes 27262976 | tf_op jit(solution)/shard_map/pallas_call | solution.py:158
  45.4 4.9 %collective-permute-start.13 = (bf16[16,128,128]{2,1,0:T(8,128)(2,1)S(1)}, bf16[16,128,128]{2,1,0:T(8,128)(2,1)S(1)}, u32[]{:S(2)}, u32[]{:S(2)}) collective-permute-start(bf16[16,128,128]{2,1,0:T(8,128)(2,1)S(1)} %get-tuple-element.36), channel_id=1, source_target_pairs={{0,2},{1,7},{2,0},{3,5},{4,6},{5,3},{6,4},{7,1},{8,10},{9,15},{10,... | collective-permute-start | bytes 1572872 | tf_op jit(solution)/shard_map/ppermute | solution.py:56
  50.2 1.6 collective-permute-start.18
  51.8 5.0 %collective-permute-done.13 = bf16[16,128,128]{2,1,0:T(8,128)(2,1)S(1)} collective-permute-done((bf16[16,128,128]{2,1,0:T(8,128)(2,1)S(1)}, bf16[16,128,128]{2,1,0:T(8,128)(2,1)S(1)}, u32[]{:S(2)}, u32[]{:S(2)}) %collective-permute-start.13) | collective-permute-done | bytes 524320 | tf_op jit(solution)/shard_map/ppermute | solution.py:56
  57.0 2.8 %collective-permute-start.14 = (bf16[16,128,128]{2,1,0:T(8,128)(2,1)S(1)}, bf16[16,128,128]{2,1,0:T(8,128)(2,1)S(1)}, u32[]{:S(2)}, u32[]{:S(2)}) collective-permute-start(bf16[16,128,128]{2,1,0:T(8,128)(2,1)S(1)} %get-tuple-element.38), channel_id=1, source_target_pairs={{0,2},{1,7},{2,0},{3,5},{4,6},{5,3},{6,4},{7,1},{8,10},{9,15},{10,... | collective-permute-start | bytes 1572872 | tf_op jit(solution)/shard_map/ppermute | solution.py:56
  59.8 1.0 collective-permute-start.20
  60.8 0.9 collective-permute-start.19
  61.6 0.5 collective-permute-done.15
  62.3 1.3 collective-permute-start.16
  63.5 1.8 %collective-permute-done.20 = bf16[8,128,128]{2,1,0:T(8,128)(2,1)S(1)} collective-permute-done((bf16[8,128,128]{2,1,0:T(8,128)(2,1)S(1)}, bf16[8,128,128]{2,1,0:T(8,128)(2,1)S(1)}, u32[]{:S(2)}, u32[]{:S(2)}) %collective-permute-start.20) | collective-permute-done | bytes 262176 | tf_op jit(solution)/shard_map/ppermute | solution.py:56
  65.5 3.3 %collective-permute-start.21 = (bf16[8,128,128]{2,1,0:T(8,128)(2,1)S(1)}, bf16[8,128,128]{2,1,0:T(8,128)(2,1)S(1)}, u32[]{:S(2)}, u32[]{:S(2)}) collective-permute-start(bf16[8,128,128]{2,1,0:T(8,128)(2,1)S(1)} %add_convert_fusion.7), channel_id=1, source_target_pairs={{0,64},{1,65},{2,66},{3,67},{4,68},{5,69},{6,70},{7,71},{8,72},{9,... | collective-permute-start | bytes 786440 | tf_op jit(solution)/shard_map/ppermute | solution.py:56
  68.8 1.5 collective-permute-start.17
  70.3 2.4 %collective-permute-done.19 = bf16[16,128,128]{2,1,0:T(8,128)(2,1)S(1)} collective-permute-done((bf16[16,128,128]{2,1,0:T(8,128)(2,1)S(1)}, bf16[16,128,128]{2,1,0:T(8,128)(2,1)S(1)}, u32[]{:S(2)}, u32[]{:S(2)}) %collective-permute-start.19) | collective-permute-done | bytes 524320 | tf_op jit(solution)/shard_map/ppermute | solution.py:56
  74.1 0.8 collective-permute-done.17
  75.0 3.0 %collective-permute-done.22 = bf16[8,128,128]{2,1,0:T(8,128)(2,1)S(1)} collective-permute-done((bf16[8,128,128]{2,1,0:T(8,128)(2,1)S(1)}, bf16[8,128,128]{2,1,0:T(8,128)(2,1)S(1)}, u32[]{:S(2)}, u32[]{:S(2)}) %collective-permute-start.22) | collective-permute-done | bytes 262176 | tf_op jit(solution)/shard_map/ppermute | solution.py:56
  78.4 3.4 %collective-permute-start.30 = (bf16[8,128,128]{2,1,0:T(8,128)(2,1)S(1)}, bf16[8,128,128]{2,1,0:T(8,128)(2,1)S(1)}, u32[]{:S(2)}, u32[]{:S(2)}) collective-permute-start(bf16[8,128,128]{2,1,0:T(8,128)(2,1)S(1)} %get-tuple-element.59), channel_id=1, source_target_pairs={{0,64},{1,65},{2,66},{3,67},{4,68},{5,69},{6,70},{7,71},{8,72},{9,... | collective-permute-start | bytes 786440 | tf_op jit(solution)/shard_map/ppermute | solution.py:56
  81.8 2.4 %collective-permute-start.28 = (bf16[8,128,128]{2,1,0:T(8,128)(2,1)S(1)}, bf16[8,128,128]{2,1,0:T(8,128)(2,1)S(1)}, u32[]{:S(2)}, u32[]{:S(2)}) collective-permute-start(bf16[8,128,128]{2,1,0:T(8,128)(2,1)S(1)} %get-tuple-element.59), channel_id=1, source_target_pairs={{0,16},{1,49},{2,18},{3,51},{4,20},{5,53},{6,22},{7,55},{8,24},{9,... | collective-permute-start | bytes 786440 | tf_op jit(solution)/shard_map/ppermute | solution.py:56
  84.2 0.4 collective-permute-start.23
  84.7 0.8 collective-permute-done.30
  85.5 2.4 %collective-permute-start.31 = (bf16[8,128,128]{2,1,0:T(8,128)(2,1)S(1)}, bf16[8,128,128]{2,1,0:T(8,128)(2,1)S(1)}, u32[]{:S(2)}, u32[]{:S(2)}) collective-permute-start(bf16[8,128,128]{2,1,0:T(8,128)(2,1)S(1)} %collective-permute-done.30), channel_id=1, source_target_pairs={{0,16},{1,49},{2,18},{3,51},{4,20},{5,53},{6,22},{7,55},{8,24},{9,... | collective-permute-start | bytes 786440 | tf_op jit(solution)/shard_map/ppermute | solution.py:56
  88.2 2.7 %collective-permute-done.23 = bf16[8,128,128]{2,1,0:T(8,128)(2,1)S(1)} collective-permute-done((bf16[8,128,128]{2,1,0:T(8,128)(2,1)S(1)}, bf16[8,128,128]{2,1,0:T(8,128)(2,1)S(1)}, u32[]{:S(2)}, u32[]{:S(2)}) %collective-permute-start.23) | collective-permute-done | bytes 262176 | tf_op jit(solution)/shard_map/ppermute | solution.py:56
  91.1 1.8 %collective-permute-done.25 = bf16[8,128,128]{2,1,0:T(8,128)(2,1)S(1)} collective-permute-done((bf16[8,128,128]{2,1,0:T(8,128)(2,1)S(1)}, bf16[8,128,128]{2,1,0:T(8,128)(2,1)S(1)}, u32[]{:S(2)}, u32[]{:S(2)}) %collective-permute-start.25) | collective-permute-done | bytes 262176 | tf_op jit(solution)/shard_map/ppermute | solution.py:56
  93.0 1.9 %collective-permute-start.26 = (bf16[8,128,128]{2,1,0:T(8,128)(2,1)S(1)}, bf16[8,128,128]{2,1,0:T(8,128)(2,1)S(1)}, u32[]{:S(2)}, u32[]{:S(2)}) collective-permute-start(bf16[8,128,128]{2,1,0:T(8,128)(2,1)S(1)} %collective-permute-done.25), channel_id=1, source_target_pairs={{0,2},{1,7},{2,0},{3,5},{4,6},{5,3},{6,4},{7,1},{8,10},{9,15},{10,... | collective-permute-start | bytes 786440 | tf_op jit(solution)/shard_map/ppermute | solution.py:56
  95.1 4.3 %collective-permute-done.26 = bf16[8,128,128]{2,1,0:T(8,128)(2,1)S(1)} collective-permute-done((bf16[8,128,128]{2,1,0:T(8,128)(2,1)S(1)}, bf16[8,128,128]{2,1,0:T(8,128)(2,1)S(1)}, u32[]{:S(2)}, u32[]{:S(2)}) %collective-permute-start.26) | collective-permute-done | bytes 262176 | tf_op jit(solution)/shard_map/ppermute | solution.py:56
  99.5 0.8 collective-permute-start.27
  100.3 1.4 collective-permute-done.29.rest_5_
  101.7 6.1 %collective-permute-done.32.rest_7_ = bf16[16,128,128]{2,1,0:T(8,128)(2,1)S(1)} collective-permute-done((bf16[16,128,128]{2,1,0:T(8,128)(2,1)S(1)}, bf16[16,128,128]{2,1,0:T(8,128)(2,1)S(1)}, u32[]{:S(2)}, u32[]{:S(2)}) %collective-permute-start.32) | collective-permute-done | bytes 524320 | tf_op jit(solution)/shard_map/ppermute | solution.py:56
  107.8 2.9 %collective-permute-done.27.rest_3_ = bf16[16,128,128]{2,1,0:T(8,128)(2,1)S(1)} collective-permute-done((bf16[16,128,128]{2,1,0:T(8,128)(2,1)S(1)}, bf16[16,128,128]{2,1,0:T(8,128)(2,1)S(1)}, u32[]{:S(2)}, u32[]{:S(2)}) %collective-permute-start.27) | collective-permute-done | bytes 524320 | tf_op jit(solution)/shard_map/ppermute | solution.py:56
  110.7 6.2 %shard_map.74 = (bf16[16,128,128]{2,1,0:T(8,128)(2,1)S(1)}, bf16[16,128,128]{2,1,0:T(8,128)(2,1)S(1)}, f32[16,128,128]{2,1,0:T(8,128)S(1)}, f32[16,128,128]{2,1,...) custom-call(s32[512]{0:T(512)S(1)} %get-tuple-element.77.row_tile_re, ...), custom_call_target="tpu_custom_call" | custom-call | flops 4294967296 | bytes 27262976 | tf_op jit(solution)/shard_map/pallas_call | solution.py:158
  116.9 3.0 %collective-permute-start.33 = (bf16[16,128,128]{2,1,0:T(8,128)(2,1)S(1)}, bf16[16,128,128]{2,1,0:T(8,128)(2,1)S(1)}, u32[]{:S(2)}, u32[]{:S(2)}) collective-permute-start(bf16[16,128,128]{2,1,0:T(8,128)(2,1)S(1)} %get-tuple-element.48), channel_id=1, source_target_pairs={{0,6},{1,3},{2,4},{3,1},{4,2},{5,7},{6,0},{7,5},{8,14},{9,11},{10,... | collective-permute-start | bytes 1572872 | tf_op jit(solution)/shard_map/ppermute | solution.py:56
  119.9 6.6 %collective-permute-done.33 = bf16[16,128,128]{2,1,0:T(8,128)(2,1)S(1)} collective-permute-done((bf16[16,128,128]{2,1,0:T(8,128)(2,1)S(1)}, bf16[16,128,128]{2,1,0:T(8,128)(2,1)S(1)}, u32[]{:S(2)}, u32[]{:S(2)}) %collective-permute-start.33) | collective-permute-done | bytes 524320 | tf_op jit(solution)/shard_map/ppermute | solution.py:56
  126.5 3.4 %collective-permute-start.35 = (bf16[8,128,128]{2,1,0:T(8,128)(2,1)S(1)}, bf16[8,128,128]{2,1,0:T(8,128)(2,1)S(1)}, u32[]{:S(2)}, u32[]{:S(2)}) collective-permute-start(bf16[8,128,128]{2,1,0:T(8,128)(2,1)S(1)} %add_convert_fusion.5), channel_id=1, source_target_pairs={{0,2},{1,7},{2,0},{3,5},{4,6},{5,3},{6,4},{7,1},{8,10},{9,15},{10,... | collective-permute-start | bytes 786440 | tf_op jit(solution)/shard_map/ppermute | solution.py:56
  130.2 5.8 %collective-permute-done.35 = bf16[8,128,128]{2,1,0:T(8,128)(2,1)S(1)} collective-permute-done((bf16[8,128,128]{2,1,0:T(8,128)(2,1)S(1)}, bf16[8,128,128]{2,1,0:T(8,128)(2,1)S(1)}, u32[]{:S(2)}, u32[]{:S(2)}) %collective-permute-start.35) | collective-permute-done | bytes 262176 | tf_op jit(solution)/shard_map/ppermute | solution.py:56
  136.2 2.5 %collective-permute-done.40 = bf16[8,128,128]{2,1,0:T(8,128)(2,1)S(1)} collective-permute-done((bf16[8,128,128]{2,1,0:T(8,128)(2,1)S(1)}, bf16[8,128,128]{2,1,0:T(8,128)(2,1)S(1)}, u32[]{:S(2)}, u32[]{:S(2)}) %collective-permute-start.40) | collective-permute-done | bytes 262176 | tf_op jit(solution)/shard_map/ppermute | solution.py:56
  139.5 1.8 %collective-permute-start.42 = (bf16[8,128,128]{2,1,0:T(8,128)(2,1)S(1)}, bf16[8,128,128]{2,1,0:T(8,128)(2,1)S(1)}, u32[]{:S(2)}, u32[]{:S(2)}) collective-permute-start(bf16[8,128,128]{2,1,0:T(8,128)(2,1)S(1)} %add_convert_fusion), channel_id=1, source_target_pairs={{0,16},{1,49},{2,18},{3,51},{4,20},{5,53},{6,22},{7,55},{8,24},{9,... | collective-permute-start | bytes 786440 | tf_op jit(solution)/shard_map/ppermute | solution.py:56
  141.3 0.5 collective-permute-done.36
  141.7 3.9 %collective-permute-done.41 = bf16[8,128,128]{2,1,0:T(8,128)(2,1)S(1)} collective-permute-done((bf16[8,128,128]{2,1,0:T(8,128)(2,1)S(1)}, bf16[8,128,128]{2,1,0:T(8,128)(2,1)S(1)}, u32[]{:S(2)}, u32[]{:S(2)}) %collective-permute-start.41) | collective-permute-done | bytes 262176 | tf_op jit(solution)/shard_map/ppermute | solution.py:56
  145.7 1.3 collective-permute-done.37
  147.4 13.5 %collective-permute-start.43 = (f32[512,128]{1,0:T(8,128)S(1)}, f32[512,128]{1,0:T(8,128)S(1)}, u32[]{:S(2)}, u32[]{:S(2)}) collective-permute-start(f32[512,128]{1,0:T(8,128)S(1)} %get-tuple-element.62), channel_id=1, source_target_pairs={{0,1},{1,0},{2,3},{3,2},{4,5},{5,4},{6,7},{7,6},{8,9},{9,8},{10,11... | collective-permute-start | bytes 786440 | tf_op jit(solution)/shard_map/ppermute | solution.py:56
  160.9 1.2 collective-permute-done.43
  162.1 0.8 maximum_select_fusion
  (64 shorter events, 4.2 us)
Async XLA Ops:
  1.0 2.9 %collective-permute-start = (bf16[512,128]{1,0:T(8,128)(2,1)S(1)}, bf16[512,128]{1,0:T(8,128)(2,1)S(1)}, u32[]{:S(2)}, u32[]{:S(2)}) collective-permute-start(bf16[512,128]{1,0:T(8,128)(2,1)S(1)} %get-tuple-element.68), channel_id=1, source_target_pairs={{0,1},{1,0},{2,3},{3,2},{4,5},{5,4},{6,7},{7,6},{8,9},{9,8},{10,11... | collective-permute-start | bytes 393224 | tf_op jit(solution)/shard_map/ppermute | solution.py:56
  3.9 35.2 %collective-permute-start.2 = (bf16[256,128,128]{2,1,0:T(8,128)(2,1)}, bf16[256,128,128]{2,1,0:T(8,128)(2,1)}, u32[]{:S(2)}, u32[]{:S(2)}) collective-permute-start(bf16[256,128,128]{2,1,0:T(8,128)(2,1)} %bitcast.14), channel_id=1, source_target_pairs={{0,1},{1,0},{2,3},{3,2},{4,5},{5,4},{6,7},{7,6},{8,9},{9,8},{10,11... | collective-permute-start | bytes 25165832 | tf_op jit(solution)/shard_map/ppermute | solution.py:56
  4.0 9.0 %collective-permute-start.10 = (bf16[8,128,128]{2,1,0:T(8,128)(2,1)S(1)}, bf16[8,128,128]{2,1,0:T(8,128)(2,1)S(1)}, u32[]{:S(2)}, u32[]{:S(2)}) collective-permute-start(bf16[8,128,128]{2,1,0:T(8,128)(2,1)S(1)} %bitcast.17), channel_id=1, source_target_pairs={{0,64},{1,65},{2,66},{3,67},{4,68},{5,69},{6,70},{7,71},{8,72},{9,... | collective-permute-start | bytes 786440 | tf_op jit(solution)/shard_map/ppermute | solution.py:56
  7.1 8.8 %collective-permute-start.8 = (bf16[8,128,128]{2,1,0:T(8,128)(2,1)S(1)}, bf16[8,128,128]{2,1,0:T(8,128)(2,1)S(1)}, u32[]{:S(2)}, u32[]{:S(2)}) collective-permute-start(bf16[8,128,128]{2,1,0:T(8,128)(2,1)S(1)} %bitcast.18), channel_id=1, source_target_pairs={{0,48},{1,17},{2,50},{3,19},{4,52},{5,21},{6,54},{7,23},{8,56},{9,... | collective-permute-start | bytes 786440 | tf_op jit(solution)/shard_map/ppermute | solution.py:56
  8.8 8.3 %collective-permute-start.3 = (bf16[8,128,128]{2,1,0:T(8,128)(2,1)S(1)}, bf16[8,128,128]{2,1,0:T(8,128)(2,1)S(1)}, u32[]{:S(2)}, u32[]{:S(2)}) collective-permute-start(bf16[8,128,128]{2,1,0:T(8,128)(2,1)S(1)} %bitcast.19), channel_id=1, source_target_pairs={{0,6},{1,3},{2,4},{3,1},{4,2},{5,7},{6,0},{7,5},{8,14},{9,11},{10,... | collective-permute-start | bytes 786440 | tf_op jit(solution)/shard_map/ppermute | solution.py:56
  10.0 9.5 %collective-permute-start.5 = (bf16[8,128,128]{2,1,0:T(8,128)(2,1)S(1)}, bf16[8,128,128]{2,1,0:T(8,128)(2,1)S(1)}, u32[]{:S(2)}, u32[]{:S(2)}) collective-permute-start(bf16[8,128,128]{2,1,0:T(8,128)(2,1)S(1)} %bitcast.20), channel_id=1, source_target_pairs={{0,8},{1,9},{2,10},{3,11},{4,12},{5,13},{6,14},{7,15},{8,0},{9,1},... | collective-permute-start | bytes 786440 | tf_op jit(solution)/shard_map/ppermute | solution.py:56
  13.1 16.3 %collective-permute-start.1 = (s32[640]{0:T(1024)S(1)}, s32[640]{0:T(1024)S(1)}, u32[]{:S(2)}, u32[]{:S(2)}) collective-permute-start(s32[640]{0:T(1024)S(1)} %pad_add_fusion), channel_id=1, source_target_pairs={{0,1},{1,0},{2,3},{3,2},{4,5},{5,4},{6,7},{7,6},{8,9},{9,8},{10,11... | collective-permute-start | bytes 7688 | tf_op jit(solution)/shard_map/ppermute | solution.py:56
  15.9 5.5 %collective-permute-start.11 = (bf16[8,128,128]{2,1,0:T(8,128)(2,1)S(1)}, bf16[8,128,128]{2,1,0:T(8,128)(2,1)S(1)}, u32[]{:S(2)}, u32[]{:S(2)}) collective-permute-start(bf16[8,128,128]{2,1,0:T(8,128)(2,1)S(1)} %collective-permute-done.10), channel_id=1, source_target_pairs={{0,48},{1,17},{2,50},{3,19},{4,52},{5,21},{6,54},{7,23},{8,56},{9,... | collective-permute-start | bytes 786440 | tf_op jit(solution)/shard_map/ppermute | solution.py:56
  17.1 17.0 %collective-permute-start.9 = (bf16[16,128,128]{2,1,0:T(8,128)(2,1)S(1)}, bf16[16,128,128]{2,1,0:T(8,128)(2,1)S(1)}, u32[]{:S(2)}, u32[]{:S(2)}) collective-permute-start(bf16[16,128,128]{2,1,0:T(8,128)(2,1)S(1)} %get-tuple-element.65.rest_4_), channel_id=1, source_target_pairs={{0,16},{1,49},{2,18},{3,51},{4,20},{5,53},{6,22},{7,55},{8,24},{9,... | collective-permute-start | bytes 1572872 | tf_op jit(solution)/shard_map/ppermute | solution.py:56
  19.4 5.5 %collective-permute-start.6 = (bf16[8,128,128]{2,1,0:T(8,128)(2,1)S(1)}, bf16[8,128,128]{2,1,0:T(8,128)(2,1)S(1)}, u32[]{:S(2)}, u32[]{:S(2)}) collective-permute-start(bf16[8,128,128]{2,1,0:T(8,128)(2,1)S(1)} %collective-permute-done.5), channel_id=1, source_target_pairs={{0,6},{1,3},{2,4},{3,1},{4,2},{5,7},{6,0},{7,5},{8,14},{9,11},{10,... | collective-permute-start | bytes 786440 | tf_op jit(solution)/shard_map/ppermute | solution.py:56
  21.4 12.7 %collective-permute-start.4 = (bf16[16,128,128]{2,1,0:T(8,128)(2,1)S(1)}, bf16[16,128,128]{2,1,0:T(8,128)(2,1)S(1)}, u32[]{:S(2)}, u32[]{:S(2)}) collective-permute-start(bf16[16,128,128]{2,1,0:T(8,128)(2,1)S(1)} %get-tuple-element.66.rest_0_), channel_id=1, source_target_pairs={{0,2},{1,7},{2,0},{3,5},{4,6},{5,3},{6,4},{7,1},{8,10},{9,15},{10,... | collective-permute-start | bytes 1572872 | tf_op jit(solution)/shard_map/ppermute | solution.py:56
  24.9 11.0 %collective-permute-start.12 = (bf16[16,128,128]{2,1,0:T(8,128)(2,1)S(1)}, bf16[16,128,128]{2,1,0:T(8,128)(2,1)S(1)}, u32[]{:S(2)}, u32[]{:S(2)}) collective-permute-start(bf16[16,128,128]{2,1,0:T(8,128)(2,1)S(1)} %constant_dynamic-update-slice_fusion.2.rest_6_), channel_id=1, source_target_pairs={{0,16},{1,49},{2,18},{3,51},{4,20},{5,53},{6,22},{7,55},{8,24},{9,... | collective-permute-start | bytes 1572872 | tf_op jit(solution)/shard_map/ppermute | solution.py:56
  29.4 9.7 %collective-permute-start.7 = (bf16[16,128,128]{2,1,0:T(8,128)(2,1)S(1)}, bf16[16,128,128]{2,1,0:T(8,128)(2,1)S(1)}, u32[]{:S(2)}, u32[]{:S(2)}) collective-permute-start(bf16[16,128,128]{2,1,0:T(8,128)(2,1)S(1)} %constant_dynamic-update-slice_fusion.rest_2_), channel_id=1, source_target_pairs={{0,2},{1,7},{2,0},{3,5},{4,6},{5,3},{6,4},{7,1},{8,10},{9,15},{10,... | collective-permute-start | bytes 1572872 | tf_op jit(solution)/shard_map/ppermute | solution.py:56
  45.4 11.5 %collective-permute-start.13 = (bf16[16,128,128]{2,1,0:T(8,128)(2,1)S(1)}, bf16[16,128,128]{2,1,0:T(8,128)(2,1)S(1)}, u32[]{:S(2)}, u32[]{:S(2)}) collective-permute-start(bf16[16,128,128]{2,1,0:T(8,128)(2,1)S(1)} %get-tuple-element.36), channel_id=1, source_target_pairs={{0,2},{1,7},{2,0},{3,5},{4,6},{5,3},{6,4},{7,1},{8,10},{9,15},{10,... | collective-permute-start | bytes 1572872 | tf_op jit(solution)/shard_map/ppermute | solution.py:56
  50.2 9.5 %collective-permute-start.18 = (bf16[16,128,128]{2,1,0:T(8,128)(2,1)S(1)}, bf16[16,128,128]{2,1,0:T(8,128)(2,1)S(1)}, u32[]{:S(2)}, u32[]{:S(2)}) collective-permute-start(bf16[16,128,128]{2,1,0:T(8,128)(2,1)S(1)} %get-tuple-element.42), channel_id=1, source_target_pairs={{0,16},{1,49},{2,18},{3,51},{4,20},{5,53},{6,22},{7,55},{8,24},{9,... | collective-permute-start | bytes 1572872 | tf_op jit(solution)/shard_map/ppermute | solution.py:56
  56.9 5.3 %collective-permute-start.15 = (bf16[8,128,128]{2,1,0:T(8,128)(2,1)S(1)}, bf16[8,128,128]{2,1,0:T(8,128)(2,1)S(1)}, u32[]{:S(2)}, u32[]{:S(2)}) collective-permute-start(bf16[8,128,128]{2,1,0:T(8,128)(2,1)S(1)} %add_convert_fusion.11), channel_id=1, source_target_pairs={{0,6},{1,3},{2,4},{3,1},{4,2},{5,7},{6,0},{7,5},{8,14},{9,11},{10,... | collective-permute-start | bytes 786440 | tf_op jit(solution)/shard_map/ppermute | solution.py:56
  57.0 11.8 %collective-permute-start.14 = (bf16[16,128,128]{2,1,0:T(8,128)(2,1)S(1)}, bf16[16,128,128]{2,1,0:T(8,128)(2,1)S(1)}, u32[]{:S(2)}, u32[]{:S(2)}) collective-permute-start(bf16[16,128,128]{2,1,0:T(8,128)(2,1)S(1)} %get-tuple-element.38), channel_id=1, source_target_pairs={{0,2},{1,7},{2,0},{3,5},{4,6},{5,3},{6,4},{7,1},{8,10},{9,15},{10,... | collective-permute-start | bytes 1572872 | tf_op jit(solution)/shard_map/ppermute | solution.py:56
  59.8 5.6 %collective-permute-start.20 = (bf16[8,128,128]{2,1,0:T(8,128)(2,1)S(1)}, bf16[8,128,128]{2,1,0:T(8,128)(2,1)S(1)}, u32[]{:S(2)}, u32[]{:S(2)}) collective-permute-start(bf16[8,128,128]{2,1,0:T(8,128)(2,1)S(1)} %add_convert_fusion.8), channel_id=1, source_target_pairs={{0,48},{1,17},{2,50},{3,19},{4,52},{5,21},{6,54},{7,23},{8,56},{9,... | collective-permute-start | bytes 786440 | tf_op jit(solution)/shard_map/ppermute | solution.py:56
  60.8 11.9 %collective-permute-start.19 = (bf16[16,128,128]{2,1,0:T(8,128)(2,1)S(1)}, bf16[16,128,128]{2,1,0:T(8,128)(2,1)S(1)}, u32[]{:S(2)}, u32[]{:S(2)}) collective-permute-start(bf16[16,128,128]{2,1,0:T(8,128)(2,1)S(1)} %get-tuple-element.44), channel_id=1, source_target_pairs={{0,16},{1,49},{2,18},{3,51},{4,20},{5,53},{6,22},{7,55},{8,24},{9,... | collective-permute-start | bytes 1572872 | tf_op jit(solution)/shard_map/ppermute | solution.py:56
  62.3 11.8 %collective-permute-start.16 = (bf16[8,128,128]{2,1,0:T(8,128)(2,1)S(1)}, bf16[8,128,128]{2,1,0:T(8,128)(2,1)S(1)}, u32[]{:S(2)}, u32[]{:S(2)}) collective-permute-start(bf16[8,128,128]{2,1,0:T(8,128)(2,1)S(1)} %add_convert_fusion.10), channel_id=1, source_target_pairs={{0,8},{1,9},{2,10},{3,11},{4,12},{5,13},{6,14},{7,15},{8,0},{9,1},... | collective-permute-start | bytes 786440 | tf_op jit(solution)/shard_map/ppermute | solution.py:56
  65.5 8.6 %collective-permute-start.21 = (bf16[8,128,128]{2,1,0:T(8,128)(2,1)S(1)}, bf16[8,128,128]{2,1,0:T(8,128)(2,1)S(1)}, u32[]{:S(2)}, u32[]{:S(2)}) collective-permute-start(bf16[8,128,128]{2,1,0:T(8,128)(2,1)S(1)} %add_convert_fusion.7), channel_id=1, source_target_pairs={{0,64},{1,65},{2,66},{3,67},{4,68},{5,69},{6,70},{7,71},{8,72},{9,... | collective-permute-start | bytes 786440 | tf_op jit(solution)/shard_map/ppermute | solution.py:56
  68.8 6.1 %collective-permute-start.17 = (bf16[8,128,128]{2,1,0:T(8,128)(2,1)S(1)}, bf16[8,128,128]{2,1,0:T(8,128)(2,1)S(1)}, u32[]{:S(2)}, u32[]{:S(2)}) collective-permute-start(bf16[8,128,128]{2,1,0:T(8,128)(2,1)S(1)} %add_convert_fusion.9), channel_id=1, source_target_pairs={{0,6},{1,3},{2,4},{3,1},{4,2},{5,7},{6,0},{7,5},{8,14},{9,11},{10,... | collective-permute-start | bytes 786440 | tf_op jit(solution)/shard_map/ppermute | solution.py:56
  72.7 5.3 %collective-permute-start.22 = (bf16[8,128,128]{2,1,0:T(8,128)(2,1)S(1)}, bf16[8,128,128]{2,1,0:T(8,128)(2,1)S(1)}, u32[]{:S(2)}, u32[]{:S(2)}) collective-permute-start(bf16[8,128,128]{2,1,0:T(8,128)(2,1)S(1)} %add_convert_fusion.6), channel_id=1, source_target_pairs={{0,48},{1,17},{2,50},{3,19},{4,52},{5,21},{6,54},{7,23},{8,56},{9,... | collective-permute-start | bytes 786440 | tf_op jit(solution)/shard_map/ppermute | solution.py:56
  78.4 7.2 %collective-permute-start.30 = (bf16[8,128,128]{2,1,0:T(8,128)(2,1)S(1)}, bf16[8,128,128]{2,1,0:T(8,128)(2,1)S(1)}, u32[]{:S(2)}, u32[]{:S(2)}) collective-permute-start(bf16[8,128,128]{2,1,0:T(8,128)(2,1)S(1)} %get-tuple-element.59), channel_id=1, source_target_pairs={{0,64},{1,65},{2,66},{3,67},{4,68},{5,69},{6,70},{7,71},{8,72},{9,... | collective-permute-start | bytes 786440 | tf_op jit(solution)/shard_map/ppermute | solution.py:56
  81.8 6.4 %collective-permute-start.28 = (bf16[8,128,128]{2,1,0:T(8,128)(2,1)S(1)}, bf16[8,128,128]{2,1,0:T(8,128)(2,1)S(1)}, u32[]{:S(2)}, u32[]{:S(2)}) collective-permute-start(bf16[8,128,128]{2,1,0:T(8,128)(2,1)S(1)} %get-tuple-element.59), channel_id=1, source_target_pairs={{0,16},{1,49},{2,18},{3,51},{4,20},{5,53},{6,22},{7,55},{8,24},{9,... | collective-permute-start | bytes 786440 | tf_op jit(solution)/shard_map/ppermute | solution.py:56
  84.2 6.7 %collective-permute-start.23 = (bf16[8,128,128]{2,1,0:T(8,128)(2,1)S(1)}, bf16[8,128,128]{2,1,0:T(8,128)(2,1)S(1)}, u32[]{:S(2)}, u32[]{:S(2)}) collective-permute-start(bf16[8,128,128]{2,1,0:T(8,128)(2,1)S(1)} %get-tuple-element.59), channel_id=1, source_target_pairs={{0,2},{1,7},{2,0},{3,5},{4,6},{5,3},{6,4},{7,1},{8,10},{9,15},{10,... | collective-permute-start | bytes 786440 | tf_op jit(solution)/shard_map/ppermute | solution.py:56
  84.6 8.4 %collective-permute-start.25 = (bf16[8,128,128]{2,1,0:T(8,128)(2,1)S(1)}, bf16[8,128,128]{2,1,0:T(8,128)(2,1)S(1)}, u32[]{:S(2)}, u32[]{:S(2)}) collective-permute-start(bf16[8,128,128]{2,1,0:T(8,128)(2,1)S(1)} %get-tuple-element.59), channel_id=1, source_target_pairs={{0,8},{1,9},{2,10},{3,11},{4,12},{5,13},{6,14},{7,15},{8,0},{9,1},... | collective-permute-start | bytes 786440 | tf_op jit(solution)/shard_map/ppermute | solution.py:56
  85.5 9.4 %collective-permute-start.31 = (bf16[8,128,128]{2,1,0:T(8,128)(2,1)S(1)}, bf16[8,128,128]{2,1,0:T(8,128)(2,1)S(1)}, u32[]{:S(2)}, u32[]{:S(2)}) collective-permute-start(bf16[8,128,128]{2,1,0:T(8,128)(2,1)S(1)} %collective-permute-done.30), channel_id=1, source_target_pairs={{0,16},{1,49},{2,18},{3,51},{4,20},{5,53},{6,22},{7,55},{8,24},{9,... | collective-permute-start | bytes 786440 | tf_op jit(solution)/shard_map/ppermute | solution.py:56
  91.0 10.7 %collective-permute-start.29 = (bf16[16,128,128]{2,1,0:T(8,128)(2,1)S(1)}, bf16[16,128,128]{2,1,0:T(8,128)(2,1)S(1)}, u32[]{:S(2)}, u32[]{:S(2)}) collective-permute-start(bf16[16,128,128]{2,1,0:T(8,128)(2,1)S(1)} %get-tuple-element.63.rest_4_), channel_id=1, source_target_pairs={{0,48},{1,17},{2,50},{3,19},{4,52},{5,21},{6,54},{7,23},{8,56},{9,... | collective-permute-start | bytes 1572872 | tf_op jit(solution)/shard_map/ppermute | solution.py:56
  91.1 10.6 %collective-permute-start.24 = (bf16[16,128,128]{2,1,0:T(8,128)(2,1)S(1)}, bf16[16,128,128]{2,1,0:T(8,128)(2,1)S(1)}, u32[]{:S(2)}, u32[]{:S(2)}) collective-permute-start(bf16[16,128,128]{2,1,0:T(8,128)(2,1)S(1)} %get-tuple-element.64.rest_0_), channel_id=1, source_target_pairs={{0,6},{1,3},{2,4},{3,1},{4,2},{5,7},{6,0},{7,5},{8,14},{9,11},{10,... | collective-permute-start | bytes 1572872 | tf_op jit(solution)/shard_map/ppermute | solution.py:56
  93.0 6.4 %collective-permute-start.26 = (bf16[8,128,128]{2,1,0:T(8,128)(2,1)S(1)}, bf16[8,128,128]{2,1,0:T(8,128)(2,1)S(1)}, u32[]{:S(2)}, u32[]{:S(2)}) collective-permute-start(bf16[8,128,128]{2,1,0:T(8,128)(2,1)S(1)} %collective-permute-done.25), channel_id=1, source_target_pairs={{0,2},{1,7},{2,0},{3,5},{4,6},{5,3},{6,4},{7,1},{8,10},{9,15},{10,... | collective-permute-start | bytes 786440 | tf_op jit(solution)/shard_map/ppermute | solution.py:56
  95.0 12.8 %collective-permute-start.32 = (bf16[16,128,128]{2,1,0:T(8,128)(2,1)S(1)}, bf16[16,128,128]{2,1,0:T(8,128)(2,1)S(1)}, u32[]{:S(2)}, u32[]{:S(2)}) collective-permute-start(bf16[16,128,128]{2,1,0:T(8,128)(2,1)S(1)} %constant_dynamic-update-slice_fusion.6.rest_6_), channel_id=1, source_target_pairs={{0,48},{1,17},{2,50},{3,19},{4,52},{5,21},{6,54},{7,23},{8,56},{9,... | collective-permute-start | bytes 1572872 | tf_op jit(solution)/shard_map/ppermute | solution.py:56
  99.5 11.2 %collective-permute-start.27 = (bf16[16,128,128]{2,1,0:T(8,128)(2,1)S(1)}, bf16[16,128,128]{2,1,0:T(8,128)(2,1)S(1)}, u32[]{:S(2)}, u32[]{:S(2)}) collective-permute-start(bf16[16,128,128]{2,1,0:T(8,128)(2,1)S(1)} %constant_dynamic-update-slice_fusion.4.rest_2_), channel_id=1, source_target_pairs={{0,6},{1,3},{2,4},{3,1},{4,2},{5,7},{6,0},{7,5},{8,14},{9,11},{10,... | collective-permute-start | bytes 1572872 | tf_op jit(solution)/shard_map/ppermute | solution.py:56
  116.9 9.6 %collective-permute-start.33 = (bf16[16,128,128]{2,1,0:T(8,128)(2,1)S(1)}, bf16[16,128,128]{2,1,0:T(8,128)(2,1)S(1)}, u32[]{:S(2)}, u32[]{:S(2)}) collective-permute-start(bf16[16,128,128]{2,1,0:T(8,128)(2,1)S(1)} %get-tuple-element.48), channel_id=1, source_target_pairs={{0,6},{1,3},{2,4},{3,1},{4,2},{5,7},{6,0},{7,5},{8,14},{9,11},{10,... | collective-permute-start | bytes 1572872 | tf_op jit(solution)/shard_map/ppermute | solution.py:56
  119.9 10.1 %collective-permute-start.38 = (bf16[16,128,128]{2,1,0:T(8,128)(2,1)S(1)}, bf16[16,128,128]{2,1,0:T(8,128)(2,1)S(1)}, u32[]{:S(2)}, u32[]{:S(2)}) collective-permute-start(bf16[16,128,128]{2,1,0:T(8,128)(2,1)S(1)} %get-tuple-element.54), channel_id=1, source_target_pairs={{0,48},{1,17},{2,50},{3,19},{4,52},{5,21},{6,54},{7,23},{8,56},{9,... | collective-permute-start | bytes 1572872 | tf_op jit(solution)/shard_map/ppermute | solution.py:56
  126.5 9.5 %collective-permute-start.35 = (bf16[8,128,128]{2,1,0:T(8,128)(2,1)S(1)}, bf16[8,128,128]{2,1,0:T(8,128)(2,1)S(1)}, u32[]{:S(2)}, u32[]{:S(2)}) collective-permute-start(bf16[8,128,128]{2,1,0:T(8,128)(2,1)S(1)} %add_convert_fusion.5), channel_id=1, source_target_pairs={{0,2},{1,7},{2,0},{3,5},{4,6},{5,3},{6,4},{7,1},{8,10},{9,15},{10,... | collective-permute-start | bytes 786440 | tf_op jit(solution)/shard_map/ppermute | solution.py:56
  130.0 9.0 %collective-permute-start.34 = (bf16[16,128,128]{2,1,0:T(8,128)(2,1)S(1)}, bf16[16,128,128]{2,1,0:T(8,128)(2,1)S(1)}, u32[]{:S(2)}, u32[]{:S(2)}) collective-permute-start(bf16[16,128,128]{2,1,0:T(8,128)(2,1)S(1)} %get-tuple-element.50), channel_id=1, source_target_pairs={{0,6},{1,3},{2,4},{3,1},{4,2},{5,7},{6,0},{7,5},{8,14},{9,11},{10,... | collective-permute-start | bytes 1572872 | tf_op jit(solution)/shard_map/ppermute | solution.py:56
  130.0 8.7 %collective-permute-start.40 = (bf16[8,128,128]{2,1,0:T(8,128)(2,1)S(1)}, bf16[8,128,128]{2,1,0:T(8,128)(2,1)S(1)}, u32[]{:S(2)}, u32[]{:S(2)}) collective-permute-start(bf16[8,128,128]{2,1,0:T(8,128)(2,1)S(1)} %add_convert_fusion.2), channel_id=1, source_target_pairs={{0,16},{1,49},{2,18},{3,51},{4,20},{5,53},{6,22},{7,55},{8,24},{9,... | collective-permute-start | bytes 786440 | tf_op jit(solution)/shard_map/ppermute | solution.py:56
  130.1 9.3 %collective-permute-start.39 = (bf16[16,128,128]{2,1,0:T(8,128)(2,1)S(1)}, bf16[16,128,128]{2,1,0:T(8,128)(2,1)S(1)}, u32[]{:S(2)}, u32[]{:S(2)}) collective-permute-start(bf16[16,128,128]{2,1,0:T(8,128)(2,1)S(1)} %get-tuple-element.56), channel_id=1, source_target_pairs={{0,48},{1,17},{2,50},{3,19},{4,52},{5,21},{6,54},{7,23},{8,56},{9,... | collective-permute-start | bytes 1572872 | tf_op jit(solution)/shard_map/ppermute | solution.py:56
  136.1 5.6 %collective-permute-start.36 = (bf16[8,128,128]{2,1,0:T(8,128)(2,1)S(1)}, bf16[8,128,128]{2,1,0:T(8,128)(2,1)S(1)}, u32[]{:S(2)}, u32[]{:S(2)}) collective-permute-start(bf16[8,128,128]{2,1,0:T(8,128)(2,1)S(1)} %add_convert_fusion.4), channel_id=1, source_target_pairs={{0,8},{1,9},{2,10},{3,11},{4,12},{5,13},{6,14},{7,15},{8,0},{9,1},... | collective-permute-start | bytes 786440 | tf_op jit(solution)/shard_map/ppermute | solution.py:56
  138.8 6.8 %collective-permute-start.41 = (bf16[8,128,128]{2,1,0:T(8,128)(2,1)S(1)}, bf16[8,128,128]{2,1,0:T(8,128)(2,1)S(1)}, u32[]{:S(2)}, u32[]{:S(2)}) collective-permute-start(bf16[8,128,128]{2,1,0:T(8,128)(2,1)S(1)} %add_convert_fusion.1), channel_id=1, source_target_pairs={{0,64},{1,65},{2,66},{3,67},{4,68},{5,69},{6,70},{7,71},{8,72},{9,... | collective-permute-start | bytes 786440 | tf_op jit(solution)/shard_map/ppermute | solution.py:56
  139.0 7.9 %collective-permute-start.37 = (bf16[8,128,128]{2,1,0:T(8,128)(2,1)S(1)}, bf16[8,128,128]{2,1,0:T(8,128)(2,1)S(1)}, u32[]{:S(2)}, u32[]{:S(2)}) collective-permute-start(bf16[8,128,128]{2,1,0:T(8,128)(2,1)S(1)} %add_convert_fusion.3), channel_id=1, source_target_pairs={{0,2},{1,7},{2,0},{3,5},{4,6},{5,3},{6,4},{7,1},{8,10},{9,15},{10,... | collective-permute-start | bytes 786440 | tf_op jit(solution)/shard_map/ppermute | solution.py:56
  139.5 7.5 %collective-permute-start.42 = (bf16[8,128,128]{2,1,0:T(8,128)(2,1)S(1)}, bf16[8,128,128]{2,1,0:T(8,128)(2,1)S(1)}, u32[]{:S(2)}, u32[]{:S(2)}) collective-permute-start(bf16[8,128,128]{2,1,0:T(8,128)(2,1)S(1)} %add_convert_fusion), channel_id=1, source_target_pairs={{0,16},{1,49},{2,18},{3,51},{4,20},{5,53},{6,22},{7,55},{8,24},{9,... | collective-permute-start | bytes 786440 | tf_op jit(solution)/shard_map/ppermute | solution.py:56
  147.4 14.7 %collective-permute-start.43 = (f32[512,128]{1,0:T(8,128)S(1)}, f32[512,128]{1,0:T(8,128)S(1)}, u32[]{:S(2)}, u32[]{:S(2)}) collective-permute-start(f32[512,128]{1,0:T(8,128)S(1)} %get-tuple-element.62), channel_id=1, source_target_pairs={{0,1},{1,0},{2,3},{3,2},{4,5},{5,4},{6,7},{7,6},{8,9},{9,8},{10,11... | collective-permute-start | bytes 786440 | tf_op jit(solution)/shard_map/ppermute | solution.py:56
